TPU v7x, 256 devices: a whole 4x4x8 slice. The times are simulated.
256 devices in a mesh: row: 16 (over z, core), col: 16 (over x, y).
Axes of the slice: x: 4, y: 4, z: 8, core: 2. Of those that a mesh axis runs over, the one named last changes fastest.
Arguments:
- weights: float32 [4096, 28672], P('row', 'col'), may hold values from -6 to 6
- momentum: float32 [4096, 28672], P('row', 'col'), may hold values from -6 to 6
- gradient: bfloat16 [4096, 28672], P('row', 'col'), may hold values from -200 to 200
- right_factor: float32 [512, 28672], P('row', 'col'), may hold values from -6 to 6
Outputs:
- new_weights: float32 [4096, 28672], P('row', 'col')
- new_momentum: float32 [4096, 28672], P('row', 'col')
- new_right: float32 [512, 28672], P('row', 'col')
All inputs are finite; a program needn't handle non-finite values.
Results may differ from a plain program's by a relative error of at most 0.0003.
Values sent between devices are 32-bit elements; how exact they have to be, the bound alone decides.
No kernel may reach another device: no remote copies, remote signals or barrier semaphores. Data moves between devices by JAX's collectives and lax.ppermute only.
A program may use at most 64 MiB of HBM per device.

v0:
```python
import jax
import jax.numpy as jnp
from jax import lax
from jax.sharding import PartitionSpec as P

N = 28672


decay_keep = 0.05
step_size = 0.5
eps_norm = 1e-06


def inner_rows(first, second):
    return lax.dot_general(
        first,
        second,
        (((0,), (0,)), ((), ())),
        precision=lax.Precision.HIGHEST,
        preferred_element_type=jnp.float32,
    )


def matmul(first, second):
    return jnp.dot(
        first, second, precision=lax.Precision.HIGHEST, preferred_element_type=jnp.float32
    )


def solve_lower(gram_matrix, left):
    factor = jnp.linalg.cholesky(gram_matrix)
    return jax.scipy.linalg.solve_triangular(factor, left.T, lower=True).T


def local(weights, momentum, gradient, right_factor):
    buffer = momentum + gradient.astype(jnp.float32)
    left_part = lax.dot_general(
        buffer,
        lax.all_gather(right_factor, "row", axis=0, tiled=True),
        (((1,), (1,)), ((), ())),
        precision=lax.Precision.HIGHEST,
        preferred_element_type=jnp.float32,
    )
    left = lax.psum(left_part, "col")
    gram_matrix = lax.psum(inner_rows(left, left), "row")
    ortho = solve_lower(gram_matrix, left)
    share = right_factor.shape[0]
    right_t = lax.psum(inner_rows(ortho, buffer), "row")
    squares = lax.psum(jnp.sum(right_t * right_t, axis=1), "col")
    scale = jnp.sqrt(squares / N + eps_norm)
    normed = right_t / scale[:, None]
    new_right = lax.dynamic_slice_in_dim(normed, lax.axis_index("row") * share, share, 0)
    new_momentum = buffer - decay_keep * matmul(ortho, right_t)
    new_weights = weights - step_size * matmul(ortho, normed)
    return (new_weights, new_momentum, new_right)


def solution(mesh):
    return jax.shard_map(
        local,
        mesh=mesh,
        in_specs=(P("row", "col"), P("row", "col"), P("row", "col"), P("row", "col")),
        out_specs=(P("row", "col"), P("row", "col"), P("row", "col")),
        check_vma=False,
    )
```

profile of v0, /device:TPU:1, one launch (start us, length us, event | category | flops | bytes accessed | tf_op | source)
XLA Modules:
  0.0 598.4 jit_solution(4358862408177276749)
XLA Ops:
  7.9 47.7 %all-gather.2.cloned.1.call-done = f32[512,1792]{1,0:T(8,128)} async-done(((f32[32,1792]{1,0:T(8,128)}), f32[512,1792]{1,0:T(8,128)}) %all-gather.2.cloned.1.call-update) | async-done | bytes 3670032 | tf_op jit(solution)/shard_map/all_gather | solution.py:39
  55.7 7.0 %fusion.4 = f32[256,512]{1,0:T(8,128)} fusion(f32[512,1792]{1,0:T(8,128)} %all-gather.2.cloned.1.call-done, f32[256,1792]{1,0:T(8,128)} %param.5, bf16[256,1792]{1,0:T(8,128)(2,1)} %param.6), kind=kOutput, calls=%fused_computation.22 | convolution fusion | flops 2819489792 | bytes 6946816 | tf_op jit(solution)/shard_map/dot_general | solution.py:37
  62.7 92.3 %all-reduce.5.cloned.1.call-done = f32[256,512]{1,0:T(8,128)} async-done(((f32[256,512]{1,0:T(8,128)}), f32[256,512]{1,0:T(8,128)}) %all-reduce.5.cloned.1.call-update) | async-done | bytes 524304 | tf_op jit(solution)/shard_map/psum | solution.py:44
  155.0 3.2 fusion.38
  158.5 112.0 %all-reduce.7.cloned.1.call-done = f32[512,512]{0,1:T(8,128)} async-done(((f32[512,512]{0,1:T(8,128)}), f32[512,512]{0,1:T(8,128)}) %all-reduce.7.cloned.1.call-update) | async-done | bytes 1048592 | tf_op jit(solution)/shard_map/psum | solution.py:45
  272.4 11.7 %cholesky.104 = f32[128,128]{1,0:T(8,128)S(1)} custom-call(f32[128,128]{1,0:T(8,128)S(1)} %cholesky.266), custom_call_target="Cholesky" | custom-call | tf_op jit(solution)/shard_map/jit(cholesky)/cholesky | solution.py:31
  284.2 9.8 %custom-call.31 = f32[1,128,128]{1,2,0:T(8,128)S(1)} custom-call(f32[1,128,128]{2,1,0:T(8,128)S(1)} %get-tuple-element.30), custom_call_target="InvertDiagBlocksLowerTriangular" | custom-call | tf_op jit(solution)/shard_map/jit(cholesky)/cholesky | solution.py:31
  294.8 11.7 %cholesky.217 = f32[128,128]{1,0:T(8,128)S(1)} custom-call(f32[128,128]{1,0:T(8,128)S(1)} %cholesky.270), custom_call_target="Cholesky" | custom-call | tf_op jit(solution)/shard_map/jit(cholesky)/cholesky | solution.py:31
  306.5 10.0 %custom-call.32 = f32[1,128,128]{1,2,0:T(8,128)S(1)} custom-call(f32[1,128,128]{2,1,0:T(8,128)S(1)} %get-tuple-element.27), custom_call_target="InvertDiagBlocksLowerTriangular" | custom-call | tf_op jit(solution)/shard_map/jit(cholesky)/cholesky | solution.py:31
  317.2 11.7 %cholesky.238 = f32[128,128]{1,0:T(8,128)S(1)} custom-call(f32[128,128]{1,0:T(8,128)S(1)} %cholesky.275), custom_call_target="Cholesky" | custom-call | tf_op jit(solution)/shard_map/jit(cholesky)/cholesky | solution.py:31
  329.7 9.8 %custom-call.33 = f32[1,128,128]{1,2,0:T(8,128)S(1)} custom-call(f32[1,128,128]{2,1,0:T(8,128)S(1)} %get-tuple-element.24), custom_call_target="InvertDiagBlocksLowerTriangular" | custom-call | tf_op jit(solution)/shard_map/jit(cholesky)/cholesky | solution.py:31
  340.1 11.7 %cholesky.255 = f32[128,128]{1,0:T(8,128)S(1)} custom-call(f32[128,128]{1,0:T(8,128)S(1)} %convolution_subtract_fusion.5), custom_call_target="Cholesky" | custom-call | tf_op jit(solution)/shard_map/jit(cholesky)/cholesky | solution.py:31
  357.1 12.0 %while.1 = (s32[]{:T(128)}, f32[512,512]{1,0:T(8,128)}, s32[4,2]{0,1:T(2,128)S(1)}, f32[4,128,128]{2,1,0:T(8,128)S(1)}, s32[]{:T(128)}) while((s32[]{:T(128)}, f32[512,512]{1,0:T(8,128)}, s32[4,2]{0,1:T(2,128)S(1)}, f32[4,128,128]{2,1,0:T(8,128)S(1)}, s32[]{:T(128)}) %tuple.31), condition=%wide.while_cond, body=%wide.while_body.sunk | while | flops 2 | bytes 131181 | solution.py:32
  357.8 2.3 bitcast_dynamic-update-slice_fusion.2
  360.8 2.3 bitcast_dynamic-update-slice_fusion.2
  363.9 2.3 bitcast_dynamic-update-slice_fusion.2
  369.2 39.9 %custom-call.34 = f32[4,128,128]{1,2,0:T(8,128)} custom-call(f32[4,128,128]{2,1,0:T(8,128)S(1)} %get-tuple-element.10), custom_call_target="InvertDiagBlocksLowerTriangular" | custom-call | tf_op jit(solution)/shard_map/jit(_solve_triangular)/triangular_solve | solution.py:32
  418.4 5.0 fusion.3
  423.4 119.7 %all-reduce.9.cloned.1.call-done = f32[512,1792]{1,0:T(8,128)} async-done(((f32[512,1792]{1,0:T(8,128)}), f32[512,1792]{1,0:T(8,128)}) %all-reduce.9.cloned.1.call-update) | async-done | bytes 3670032 | tf_op jit(solution)/shard_map/psum | solution.py:48
  543.1 2.4 multiply_reduce_fusion
  545.5 33.6 %psum.31 = f32[512]{0:T(512)S(1)} all-reduce(f32[512]{0:T(512)S(1)} %multiply_reduce_fusion), channel_id=1, replica_groups=mesh['row'=16,'col'=16] {'col'}, use_global_device_ids=true, to_apply=%region_12.13 | all-reduce | flops 512 | bytes 4096 | tf_op jit(solution)/shard_map/psum | solution.py:49
  579.1 2.5 broadcast_divide_fusion
  581.8 4.6 fusion.1
  587.1 4.6 fusion
  (65 shorter events, 23.6 us)
Async XLA Ops:
  7.2 48.5 %all-gather.2.cloned.1.call-start = ((), (), s32[]{:S(2)}) async-start(), calls=%async_computation | async-start | bytes 3899392 | tf_op jit(solution)/shard_map/all_gather | solution.py:39
  7.9 147.1 %all-reduce.5.cloned.1.call-start = ((), (), s32[]{:S(2)}) async-start(), calls=%async_computation.1 | async-start | bytes 1048576 | tf_op jit(solution)/shard_map/psum | solution.py:44
  62.7 207.8 %all-reduce.7.cloned.1.call-start = ((), (), s32[]{:S(2)}) async-start(), calls=%async_computation.2 | async-start | bytes 2097152 | tf_op jit(solution)/shard_map/psum | solution.py:45
  158.2 384.9 %all-reduce.9.cloned.1.call-start = ((), (), s32[]{:S(2)}) async-start(), calls=%async_computation.3 | async-start | bytes 7340032 | tf_op jit(solution)/shard_map/psum | solution.py:48
  270.5 1.7 copy-start.4
  328.9 80.2 %copy-start.3 = (f32[256,512]{1,0:T(8,128)S(1)}, f32[256,512]{1,0:T(8,128)}, u32[]{:S(2)}) copy-start(f32[256,512]{1,0:T(8,128)} %all-reduce.5.cloned.1.call-done) | copy-start | bytes 1572868
  369.2 49.2 %copy-start.1 = (f32[256,1792]{1,0:T(8,128)S(1)}, f32[256,1792]{1,0:T(8,128)}, u32[]{:S(2)}) copy-start(f32[256,1792]{1,0:T(8,128)} %param.5) | copy-start | bytes 5505028
  369.2 49.2 %copy-start.2 = (bf16[256,1792]{1,0:T(8,128)(2,1)S(1)}, bf16[256,1792]{1,0:T(8,128)(2,1)}, u32[]{:S(2)}) copy-start(bf16[256,1792]{1,0:T(8,128)(2,1)} %param.6) | copy-start | bytes 2752516
  415.4 3.0 copy-start.5
  579.1 2.5 copy-start.6
  579.1 2.7 copy-start.7
  581.8 5.3 copy-start
Sparse Core Ops, SparseCore 0:
  9.8 45.7 all-gather.1
  62.8 92.1 all-reduce.4
  158.4 112.0 all-reduce.6
  423.5 119.5 all-reduce.8
where the time goes:
time: 608 us; the launch traced here: 598 us
  waiting for transfers between devices  372 us (61%)
  other arithmetic  125 us (21%)
  matrix products  35.4 us (6%)
  blocking collectives  33.6 us (6%)
  between operations  16.8 us (3%)
  local copies, waits for them, and re-layouts  14.6 us (2%)
    psum x1, waiting for transfers between devices, local(): right_t = lax.psum(inner_rows(ortho, buffer), 'row')  120 us
    psum x1, waiting for transfers between devices, local(): gram_matrix = lax.psum(inner_rows(left, left), 'row')  112 us
    psum x1, waiting for transfers between devices, local(): left = lax.psum(left_part, 'col')  92.3 us
    another operation x14, other arithmetic, solve_lower(): factor = jnp.linalg.cholesky(gram_matrix)  78.6 us
    all_gather x1, waiting for transfers between devices, local(): lax.all_gather(right_factor, 'row', axis=0, tiled=True)  47.7 us
    another operation x3, other arithmetic, solve_lower(): return jax.scipy.linalg.solve_triangular(factor, left.T, lower=True).T  41.4 us
    psum x1, blocking collectives, local(): squares = lax.psum(jnp.sum(right_t * right_t, axis=1), 'col')  33.6 us
  transfers between devices with their start and end apart: 4, of which 4 were waited for; matrix products, arithmetic and copies ran while one was open for 0% of the time, Pallas kernels for 0%

commit v1 on v0

v1 whole, which is shorter than its diff:
```python
import jax
import jax.numpy as jnp
from jax import lax
from jax.experimental import pallas as pl
from jax.experimental.pallas import tpu as pltpu
from jax.sharding import Mesh, PartitionSpec as P

N = 28672
R = 512
Z = 8
XY = 16
TILE = 128

decay_keep = 0.05
step_size = 0.5
eps_norm = 1e-06

F32 = jnp.float32
HIGHEST = lax.Precision.HIGHEST


def split_three(values):
    high = values.astype(jnp.bfloat16).astype(F32)
    rest = values - high
    middle = rest.astype(jnp.bfloat16).astype(F32)
    low = (rest - middle).astype(jnp.bfloat16).astype(F32)
    return high, middle, low


def inverse_root(value):
    guess = lax.rsqrt(value)
    return guess * (1.5 - 0.5 * value * (guess * guess))


def invert_factor_8(entries):
    size = len(entries)
    left = [row[:] for row in entries]
    inverse = [[None] * size for _ in range(size)]
    for j in range(size):
        root = inverse_root(left[j][j])
        column = [None] * size
        for i in range(j + 1, size):
            column[i] = left[i][j] * root
        for i in range(j + 1, size):
            for k in range(j + 1, i + 1):
                left[i][k] = left[i][k] - column[i] * column[k]
        for c in range(j):
            inverse[j][c] = inverse[j][c] * root
        inverse[j][j] = root
        for i in range(j + 1, size):
            for c in range(j + 1):
                term = column[i] * inverse[j][c]
                inverse[i][c] = -term if inverse[i][c] is None else inverse[i][c] - term
    return inverse


def invert_factor_tile(state, result):
    sublane = lax.broadcasted_iota(jnp.int32, (8, TILE), 0)
    for step in range(TILE // 8):
        at = 8 * step
        rows = state[at : at + 8, :]
        lanes = [jnp.broadcast_to(rows[:, at + j : at + j + 1], (8, TILE)) for j in range(8)]
        entries = [
            [jnp.broadcast_to(lanes[j][i : i + 1, :], (8, TILE)) for j in range(i + 1)] for i in range(8)
        ]
        inverse = invert_factor_8(entries)
        first, second = None, None
        for j in range(8):
            column = jnp.zeros((8, TILE), F32)
            for i in range(j, 8):
                column = jnp.where(sublane == i, inverse[i][j], column)
            one = column * jnp.broadcast_to(rows[j : j + 1, :TILE], (8, TILE))
            two = column * jnp.broadcast_to(rows[j : j + 1, TILE:], (8, TILE))
            first = one if first is None else first + one
            second = two if second is None else second + two
        result[at : at + 8, :] = second
        if at + 8 < TILE:
            high, middle, low = split_three(jnp.concatenate([first, second], 1))
            right = jnp.concatenate([high, middle, high, low, high, middle], 0).astype(jnp.bfloat16)
            high, middle, low = high[:, :TILE], middle[:, :TILE], low[:, :TILE]
            left = jnp.concatenate([high, high, middle, high, low, middle], 0).astype(jnp.bfloat16)
            update = lax.dot_general(left, right, (((0,), (0,)), ((), ())), preferred_element_type=F32)
            state[at + 8 :, :] = state[at + 8 :, :] - update[at + 8 :, :]


def inverse_factor_kernel(first, last, rest_in, inverse_in, result_in, rest, inverse, result, state, tile, panel):
    identity = jnp.where(
        lax.broadcasted_iota(jnp.int32, (TILE, TILE), 0) == lax.broadcasted_iota(jnp.int32, (TILE, TILE), 1), 1.0, 0.0
    )
    rest[...] = rest_in[...]
    if first == 0:
        rows = lax.broadcasted_iota(jnp.int32, (R, R), 0)
        columns = lax.broadcasted_iota(jnp.int32, (R, R), 1)
        inverse[...] = jnp.where(rows == columns, 1.0, 0.0)
    else:
        inverse[...] = inverse_in[...]
        result[...] = result_in[...]

    @pl.loop(first, last)
    def _(k):
        at = pl.multiple_of(k * TILE, TILE)
        state[:, :TILE] = rest[pl.ds(at, TILE), pl.ds(at, TILE)]
        state[:, TILE:] = identity
        invert_factor_tile(state, tile)
        upper = jnp.dot(tile[...], rest[pl.ds(at, TILE), :], precision=HIGHEST, preferred_element_type=F32)
        lower = jnp.dot(tile[...], inverse[pl.ds(at, TILE), :], precision=HIGHEST, preferred_element_type=F32)
        result[pl.ds(at, TILE), :] = lower
        panel[...] = upper
        for i in range(1, R // TILE):

            @pl.when(i > k)
            def _():
                below = pl.ds(i * TILE, TILE)
                factor = panel[:, i * TILE : (i + 1) * TILE]
                dims = (((0,), (0,)), ((), ()))
                rest[below, :] -= lax.dot_general(factor, upper, dims, precision=HIGHEST, preferred_element_type=F32)
                inverse[below, :] -= lax.dot_general(factor, lower, dims, precision=HIGHEST, preferred_element_type=F32)


def factor_steps(first, last, rest, inverse=None, result=None):
    whole = pl.BlockSpec(memory_space=pltpu.VMEM)
    square = jax.ShapeDtypeStruct((R, R), F32)
    given = (rest,) if first == 0 else (rest, inverse, result)

    def kernel(*refs):
        if first == 0:
            inverse_factor_kernel(first, last, refs[0], None, None, *refs[1:])
        else:
            inverse_factor_kernel(first, last, *refs)

    return pl.pallas_call(
        kernel,
        out_shape=(square, square, square),
        in_specs=[whole] * len(given),
        out_specs=(whole, whole, whole),
        scratch_shapes=[pltpu.VMEM((TILE, 2 * TILE), F32), pltpu.VMEM((TILE, TILE), F32), pltpu.VMEM((TILE, R), F32)],
        compiler_params=pltpu.CompilerParams(vmem_limit_bytes=24 * 2**20),
        cost_estimate=pl.CostEstimate(flops=10**10, bytes_accessed=2 * 4 * R * R, transcendentals=R),
        name="inverse_factor",
    )(*given)


def split_two(values):
    high = values.astype(jnp.bfloat16)
    return high, (values - high.astype(F32)).astype(jnp.bfloat16)


def product3(first, second, dims):
    def one(a, b):
        return lax.dot_general(a, b, (dims, ((), ())), preferred_element_type=F32)

    return one(first[0], second[0]) + (one(first[0], second[1]) + one(first[1], second[0]))


WIDTH = 256
NN = ((1,), (0,))
NT = ((1,), (1,))
LIMIT = 32 * 2**20


def call(kernel, steps, operands, specs, outs, out_specs, scratch=(), name=None, flops=10**9):
    return pl.pallas_call(
        kernel,
        grid=(steps,),
        out_shape=outs,
        in_specs=specs,
        out_specs=out_specs,
        scratch_shapes=list(scratch),
        compiler_params=pltpu.CompilerParams(vmem_limit_bytes=LIMIT, dimension_semantics=("arbitrary",)),
        cost_estimate=pl.CostEstimate(flops=flops, bytes_accessed=4 * 2**20, transcendentals=0),
        name=name,
    )(*operands)


def wide(rows):
    return pl.BlockSpec((rows, WIDTH), lambda j: (0, j))


def whole(*shape):
    return pl.BlockSpec(shape, lambda j: (0,) * len(shape))


def left_product(blocks, chip):
    rows, columns = chip.shape
    ranks = sum(b.shape[0] for b in blocks)

    def kernel(*refs):
        parts, chip_ref, out = refs[:-2], refs[-2], refs[-1]
        right = jnp.concatenate([p[...] for p in parts], 0)
        term = product3(split_two(right), split_two(chip_ref[...]), NT)

        @pl.when(pl.program_id(0) == 0)
        def _():
            out[...] = term

        @pl.when(pl.program_id(0) > 0)
        def _():
            out[...] += term

    return call(
        kernel,
        columns // WIDTH,
        (*blocks, chip),
        [wide(b.shape[0]) for b in blocks] + [wide(rows)],
        jax.ShapeDtypeStruct((ranks, rows), F32),
        whole(ranks, rows),
        name="left_product",
    )


def right_product(left, chip):
    ranks, rows = left.shape
    columns = chip.shape[1]

    def kernel(left_ref, chip_ref, out, high, low):
        @pl.when(pl.program_id(0) == 0)
        def _():
            high[...], low[...] = split_two(left_ref[...])

        out[...] = product3((high[...], low[...]), split_two(chip_ref[...]), NN)

    half = pltpu.VMEM((ranks, rows), jnp.bfloat16)
    return call(
        kernel,
        columns // WIDTH,
        (left, chip),
        [whole(ranks, rows), wide(rows)],
        jax.ShapeDtypeStruct((ranks, columns), F32),
        wide(ranks),
        (half, half),
        name="right_product",
    )


def right_and_squares(inverse, product):
    columns = product.shape[1]
    steps = columns // WIDTH

    def kernel(inverse_ref, product_ref, out, sums, high, low, total):
        j = pl.program_id(0)

        @pl.when(j == 0)
        def _():
            high[...], low[...] = split_two(inverse_ref[...])
            total[...] = jnp.zeros_like(total)

        right = product3((high[...], low[...]), split_two(product_ref[...]), NN)
        out[...] = right
        squares = right * right
        total[...] += squares[:, :128] + squares[:, 128:]

        @pl.when(j == steps - 1)
        def _():
            sums[...] = lax.dot_general(
                jnp.ones((8, 128), F32), total[...], (NT, ((), ())), precision=HIGHEST, preferred_element_type=F32
            )

    half = pltpu.VMEM((R, R), jnp.bfloat16)
    return call(
        kernel,
        steps,
        (inverse, product),
        [whole(R, R), wide(R)],
        (jax.ShapeDtypeStruct((R, columns), F32), jax.ShapeDtypeStruct((8, R), F32)),
        (wide(R), whole(8, R)),
        (half, half, pltpu.VMEM((R, 128), F32)),
        name="right_and_squares",
    )


def momentum_update(buffer, ortho, right):
    rows, columns = buffer.shape

    def kernel(buffer_ref, ortho_ref, right_ref, out, high, low):
        @pl.when(pl.program_id(0) == 0)
        def _():
            high[...], low[...] = split_two(ortho_ref[...])

        out[...] = buffer_ref[...] - decay_keep * product3((high[...], low[...]), split_two(right_ref[...]), NN)

    half = pltpu.VMEM((rows, R), jnp.bfloat16)
    return call(
        kernel,
        columns // WIDTH,
        (buffer, ortho, right),
        [wide(rows), whole(rows, R), wide(R)],
        jax.ShapeDtypeStruct((rows, columns), F32),
        wide(rows),
        (half, half),
        name="momentum_update",
    )


def weights_update(weights, ortho, right, sums, start, share):
    rows, columns = weights.shape
    count = sums.shape[0]

    def kernel(start_ref, weights_ref, ortho_ref, right_ref, sums_ref, out, own, high, low, own_scale):
        at = pl.multiple_of(start_ref[0], share)

        @pl.when(pl.program_id(0) == 0)
        def _():
            scale = jnp.sqrt(jnp.sum(sums_ref[...], axis=0, keepdims=True) / N + eps_norm)
            high[...], low[...] = split_two(ortho_ref[...] / scale)
            lanes = lax.broadcasted_iota(jnp.int32, (share, R), 1)
            chosen = lanes == at + lax.broadcasted_iota(jnp.int32, (share, R), 0)
            picked = jnp.sum(jnp.where(chosen, jnp.broadcast_to(scale, (share, R)), 0.0), axis=1, keepdims=True)
            own_scale[...] = jnp.broadcast_to(picked, own_scale.shape)

        out[...] = weights_ref[...] - step_size * product3((high[...], low[...]), split_two(right_ref[...]), NN)
        own[...] = right_ref[pl.ds(at, share), :] / own_scale[...]

    half = pltpu.VMEM((rows, R), jnp.bfloat16)
    return call(
        kernel,
        columns // WIDTH,
        (start, weights, ortho, right, sums),
        [pl.BlockSpec(memory_space=pltpu.SMEM), wide(rows), whole(rows, R), wide(R), whole(count, R)],
        (jax.ShapeDtypeStruct((rows, columns), F32), jax.ShapeDtypeStruct((share, columns), F32)),
        (wide(rows), wide(share)),
        (half, half, pltpu.VMEM((share, WIDTH), F32)),
        name="weights_update",
    )


SIZES = {"z": Z, "core": 2, "x": 4, "y": 4}


def shift(values, axis, by):
    size = SIZES[axis]
    return lax.ppermute(values, axis, [(i, (i + by) % size) for i in range(size)])


def spread(values, axes, count):
    whole = jnp.broadcast_to(values[None], (count,) + values.shape)
    return lax.all_to_all(whole, axes, 0, 0, tiled=True)


def gather_z(own):
    half = own.shape[0] // 2
    below1, above1 = shift(own, "z", 1), shift(own, "z", -1)
    below2, above2 = shift(own, "z", 2), shift(own, "z", -2)
    below3, above3 = shift(below2, "z", 1), shift(above2, "z", -1)
    across = (shift(below3[:half], "z", 1), shift(above3[half:], "z", -1))
    return [own, above1, above2, above3, across, below3, below2, below1]


def dot(first, second, dims, precision):
    return lax.dot_general(
        first, second, ((dims[0], dims[1]), ((), ())), precision=precision, preferred_element_type=F32
    )


def local(weights, momentum, gradient, right_factor):
    core = lax.axis_index("core")
    plane = lax.axis_index("x") * 4 + lax.axis_index("y")
    z = lax.axis_index("z")
    share = right_factor.shape[0]

    buffer = momentum + gradient.astype(F32)
    right = gather_z(right_factor)
    beside = shift(buffer, "core", 1)
    chip = jnp.where(
        core == 0, jnp.concatenate([buffer, beside], 0), jnp.concatenate([beside, buffer], 0)
    )

    blocks = [*right[:4], *right[4], *right[5:]]
    part = left_product(blocks, chip)
    rows = part.shape[1]
    pieces = lax.all_to_all(part.reshape(XY, -1, rows), ("x", "y"), 0, 0, tiled=True)
    left = spread(jnp.sum(pieces, 0), ("x", "y"), XY).reshape(Z, share, rows)
    own = lax.dynamic_slice_in_dim(jnp.concatenate([left, left], 0), (Z - z) % Z, Z, 0)

    product = right_product(own.reshape(Z * share, rows), chip)
    product = lax.psum_scatter(product, "z", scatter_dimension=0, tiled=True)

    other = shift(own, "core", 1)
    left_all = jnp.stack([jnp.where(core == 0, own, other), jnp.where(core == 0, other, own)], 1)
    left_all = left_all.reshape(R, rows)
    height = R // (2 * XY)
    mine = lax.dynamic_slice_in_dim(left_all, (core * XY + plane) * height, height, 0)
    gram = jnp.sum(spread(dot(mine, left_all, ((1,), (1,)), HIGHEST), "z", Z), 0)
    gram = spread(gram, ("x", "y"), XY).reshape(R // 2, R)
    gram_other = shift(gram, "core", 1)
    gram = jnp.where(
        core == 0, jnp.concatenate([gram, gram_other], 0), jnp.concatenate([gram_other, gram], 0)
    )
    state = factor_steps(0, 2, gram)
    state, product = lax.optimization_barrier((state, product))
    product = lax.all_gather(product, ("z", "core"), axis=0, tiled=True)
    _, _, inverse = factor_steps(2, 4, *state)

    height = rows // 2
    left_own = jnp.where(core == 0, left_all[:, :height], left_all[:, height:])
    ortho = dot(left_own, inverse, ((0,), (1,)), HIGHEST)
    right_t, sums = right_and_squares(inverse, product)
    sums = spread(sums[:1], ("x", "y"), XY).reshape(XY, R)
    start = jnp.full((1,), (2 * z + core) * share, jnp.int32)
    new_momentum = momentum_update(buffer, ortho, right_t)
    new_weights, new_right = weights_update(weights, ortho, right_t, sums, start, share)
    return (new_weights, new_momentum, new_right)


def solution(mesh):
    fine = Mesh(mesh.devices.reshape(Z, 2, 4, 4), ("z", "core", "x", "y"))
    spec = P(("z", "core"), ("x", "y"))
    return jax.shard_map(
        local, mesh=fine, in_specs=(spec, spec, spec, spec), out_specs=(spec, spec, spec), check_vma=False
    )
```

time: 608 us -> 220 us (0.36); the launches traced: 598 us -> 219 us
  waiting for transfers between devices: 372 us -> 37.2 us
  other arithmetic: 125 us -> 4.9 us
  Pallas kernels: 0 us -> 54.8 us
  starting transfers between devices: 0.33 us -> 33.9 us
  matrix products: 35.4 us -> 2.83 us
  blocking collectives: 33.6 us -> 49.3 us
  local copies, waits for them, and re-layouts: 14.6 us -> 21.8 us
    psum x3 -> x0, waiting for transfers between devices: 324 us -> none  [the longest x1 120 us: local(): right_t = lax.psum(inner_rows(ortho, buffer), 'row')]
    another operation x17 -> x2, other arithmetic: 120 us -> 0.29 us  [local(): jnp.stack([jnp.where(core == 0, own, other), jnp.where(core == 0, other,...]
    pallas_call x0 -> x7, Pallas kernels: none -> 54.8 us  [the longest x2 33.2 us: factor_steps(): pl.pallas_call(kernel, out_shape=(square, square, square), in_specs=[whol...]
    all_to_all x0 -> x3, blocking collectives: none -> 49.3 us  [the longest x2 33.6 us: spread(): return lax.all_to_all(whole, axes, 0, 0, tiled=True)]
    all_gather x1, waiting for transfers between devices: 47.7 us -> 13.3 us  [local(): product = lax.all_gather(product, ('z', 'core'), axis=0, tiled=True)]
    psum x1 -> x0, blocking collectives: 33.6 us -> none  [local(): squares = lax.psum(jnp.sum(right_t * right_t, axis=1), 'col')]
    ppermute x0 -> x11, starting transfers between devices: none -> 23.7 us  [shift(): lax.ppermute(values, axis, [(i, (i + by) % size) for i in range(size)])]
    dot_general x5 -> x2, matrix products: 24.4 us -> 2.83 us  [dot(): lax.dot_general(first, second, ((dims[0], dims[1]), ((), ())), precision=...]
  transfers between devices with their start and end apart: 4 -> 15, of which waited for: 4 -> 9; matrix products, arithmetic and copies ran while one was open for 0% -> 3% of each run, Pallas kernels for 0% -> 19%
where the time goes in v1:
time: 220 us; the launch traced here: 219 us
  Pallas kernels  54.8 us (25%)
  blocking collectives  49.3 us (22%)
  waiting for transfers between devices  37.2 us (17%)
  starting transfers between devices  33.9 us (15%)
  local copies, waits for them, and re-layouts  21.8 us (10%)
  between operations  14.3 us (6%)
  other arithmetic  4.9 us (2%)
  matrix products  2.83 us (1%)
    all_to_all x2, blocking collectives, spread(): return lax.all_to_all(whole, axes, 0, 0, tiled=True)  33.6 us
    pallas_call x2, Pallas kernels, factor_steps(): pl.pallas_call(kernel, out_shape=(square, square, square), in_specs=[whol...  33.2 us
    ppermute x11, starting transfers between devices, shift(): lax.ppermute(values, axis, [(i, (i + by) % size) for i in range(size)])  23.7 us
    pallas_call x5, Pallas kernels, call(): pl.pallas_call(kernel, grid=(steps,), out_shape=outs, in_specs=specs, out...  21.5 us
    unnamed x35, local copies, waits for them, and re-layouts  20.3 us
    all_to_all x1, blocking collectives, local(): lax.all_to_all(part.reshape(XY, -1, rows), ('x', 'y'), 0, 0, tiled=True)  15.8 us
    ppermute x11, waiting for transfers between devices, shift(): lax.ppermute(values, axis, [(i, (i + by) % size) for i in range(size)])  15 us
    all_gather x1, waiting for transfers between devices, local(): product = lax.all_gather(product, ('z', 'core'), axis=0, tiled=True)  13.3 us
  transfers between devices with their start and end apart: 15, of which 9 were waited for; matrix products, arithmetic and copies ran while one was open for 3% of the time, Pallas kernels for 19%

profile of v1, /device:TPU:1, one launch (start us, length us, event | category | flops | bytes accessed | tf_op | source)
XLA Modules:
  0.0 219.1 jit_solution(5815995890880378636)
XLA Ops:
  9.1 3.3 %collective-permute-start.8 = (f32[256,1792]{1,0:T(8,128)S(1)}, f32[256,1792]{1,0:T(8,128)}, u32[]{:S(2)}, u32[]{:S(2)}) collective-permute-start(f32[256,1792]{1,0:T(8,128)S(1)} %convert_add_fusion.buffer_ref), channel_id=1, source_target_pairs={{0,16},{16,0},{1,17},{17,1},{2,18},{18,2},{3,19},{19,3},{4,20},{20... | collective-permute-start | bytes 5505032 | tf_op jit(solution)/shard_map/ppermute | solution.py:331
  13.7 3.0 %collective-permute-start.1 = (f32[32,1792]{1,0:T(8,128)S(1)}, f32[32,1792]{1,0:T(8,128)S(1)}, u32[]{:S(2)}, u32[]{:S(2)}) collective-permute-start(f32[32,1792]{1,0:T(8,128)S(1)} %copy-done.8), channel_id=1, source_target_pairs={{0,192},{32,224},{64,0},{96,32},{128,64},{160,96},{192,128},{224,1... | collective-permute-start | bytes 688136 | tf_op jit(solution)/shard_map/ppermute | solution.py:331
  16.7 7.4 %collective-permute-done.3.refs_7_ = f32[32,1792]{1,0:T(8,128)S(1)} collective-permute-done((f32[32,1792]{1,0:T(8,128)S(1)}, f32[32,1792]{1,0:T(8,128)S(1)}, u32[]{:S(2)}, u32[]{:S(2)}) %collective-permute-start.3) | collective-permute-done | bytes 229408 | tf_op jit(solution)/shard_map/ppermute | solution.py:331
  24.2 4.1 %collective-permute-start.4 = (f32[32,1792]{1,0:T(8,128)S(1)}, f32[32,1792]{1,0:T(8,128)S(1)}, u32[]{:S(2)}, u32[]{:S(2)}) collective-permute-start(f32[32,1792]{1,0:T(8,128)S(1)} %collective-permute-done.3.refs_7_), channel_id=1, source_target_pairs={{0,32},{32,64},{64,96},{96,128},{128,160},{160,192},{192,224},{224... | collective-permute-start | bytes 688136 | tf_op jit(solution)/shard_map/ppermute | solution.py:331
  29.0 2.2 %collective-permute-start = (f32[32,1792]{1,0:T(8,128)S(1)}, f32[32,1792]{1,0:T(8,128)S(1)}, u32[]{:S(2)}, u32[]{:S(2)}) collective-permute-start(f32[32,1792]{1,0:T(8,128)S(1)} %copy-done.8), channel_id=1, source_target_pairs={{0,224},{32,0},{64,32},{96,64},{128,96},{160,128},{192,160},{224,1... | collective-permute-start | bytes 688136 | tf_op jit(solution)/shard_map/ppermute | solution.py:331
  31.2 2.9 %collective-permute-done.4.refs_6_ = f32[32,1792]{1,0:T(8,128)S(1)} collective-permute-done((f32[32,1792]{1,0:T(8,128)S(1)}, f32[32,1792]{1,0:T(8,128)S(1)}, u32[]{:S(2)}, u32[]{:S(2)}) %collective-permute-start.4) | collective-permute-done | bytes 229408 | tf_op jit(solution)/shard_map/ppermute | solution.py:331
  34.8 2.1 collective-permute-start.6
  36.9 2.4 %maximum_select_fusion.refs_9_.chip_ref = f32[512,1792]{1,0:T(8,128)S(1)} fusion(f32[256,1792]{1,0:T(8,128)} %collective-permute-done.8, f32[256,1792]{1,0:T(8,128)S(1)} %convert_add_fusion.buffer_ref, pred[]{:T(512)S(6)} %eq.4), kind=kLoop, calls=%fused_computation | loop fusion | flops 2752512 | bytes 7340033 | tf_op jit(solution)/shard_map/jit(_where)/select_n | solution.py:363
  42.2 3.7 %left_product.1 = f32[256,512]{1,0:T(8,128)S(1)} custom-call(f32[32,1792]{1,0:T(8,128)S(1)} %copy-done.8, f32[32,1792]{1,0:T(8,128)S(1)} %collective-permute-done.refs_1_, f32[32,1792]{1,0:T(8,128)S(1)} %collective-permute-done.1.refs_2_, f32[32,1792]{1,0:T(8,128)S(1)} %collective-permute-done.2.refs_3_, f32[16,1792]{1,0:T(8,128)S(1)} %collective-permute-done.5.refs_4_, ...), custom_call_target="tpu_custom_call" | custom-call | flops 1000000000 | bytes 4194304 | tf_op jit(solution)/shard_map/left_product/pallas_call | solution.py:162
  45.9 15.8 %all_to_all.25 = f32[16,16,512]{2,1,0:T(8,128)S(1)} all-to-all(f32[16,16,512]{2,1,0:T(8,128)S(1)} %bitcast.18), channel_id=1, replica_groups=mesh['z'=8,'core'=2,'x'=4,'y'=4] {'x','y'}, dimensions={0} | all-to-all | bytes 1048576 | tf_op jit(solution)/shard_map/all_to_all | solution.py:370
  62.6 3.6 %all-to-all-start.1 = ((f32[16,16,512]{2,1,0:T(8,128)}), f32[16,16,512]{2,1,0:T(8,128)S(1)}, u32[]{:S(2)}, u32[]{:S(2)}) async-start(f32[16,16,512]{2,1,0:T(8,128)} %broadcast_in_dim.13), calls=%async_computation.1 | async-start | bytes 1048576 | tf_op jit(solution)/shard_map/all_to_all | solution.py:336
  66.2 8.8 %all-to-all-done.1 = f32[16,16,512]{2,1,0:T(8,128)S(1)} async-done(((f32[16,16,512]{2,1,0:T(8,128)}), f32[16,16,512]{2,1,0:T(8,128)S(1)}, u32[]{:S(2)}, u32[]{:S(2)}) %all-to-all-start.1) | async-done | bytes 524320 | tf_op jit(solution)/shard_map/all_to_all | solution.py:336
  75.2 4.5 %collective-permute-start.9 = (f32[8,32,512]{2,1,0:T(8,128)S(1)}, f32[8,32,512]{2,1,0:T(8,128)S(1)}, u32[]{:S(2)}, u32[]{:S(2)}) collective-permute-start(f32[8,32,512]{2,1,0:T(8,128)S(1)} %fusion), channel_id=1, source_target_pairs={{0,16},{16,0},{1,17},{17,1},{2,18},{18,2},{3,19},{19,3},{4,20},{20... | collective-permute-start | bytes 1572872 | tf_op jit(solution)/shard_map/ppermute | solution.py:331
  81.7 3.2 %right_product.1 = f32[256,1792]{1,0:T(8,128)S(1)} custom-call(f32[256,512]{1,0:T(8,128)S(1)} %bitcast.19, f32[512,1792]{1,0:T(8,128)S(1)} %copy-done.1), custom_call_target="tpu_custom_call" | custom-call | flops 1000000000 | bytes 4194304 | tf_op jit(solution)/shard_map/right_product/pallas_call | solution.py:162
  88.5 20.6 %all_to_all.26 = f32[8,16,512]{2,1,0:T(8,128)S(1)} all-to-all(f32[8,16,512]{2,1,0:T(8,128)S(1)} %broadcast_in_dim.14), channel_id=1, replica_groups=mesh['z'=8,'core'=2,'x'=4,'y'=4] {'z'}, dimensions={0} | all-to-all | bytes 524288 | tf_op jit(solution)/shard_map/all_to_all | solution.py:336
  109.2 13.0 %all_to_all.27 = f32[16,16,512]{2,1,0:T(8,128)S(1)} all-to-all(f32[16,16,512]{2,1,0:T(8,128)S(1)} %broadcast_in_dim.15), channel_id=1, replica_groups=mesh['z'=8,'core'=2,'x'=4,'y'=4] {'x','y'}, dimensions={0} | all-to-all | bytes 1048576 | tf_op jit(solution)/shard_map/all_to_all | solution.py:336
  122.2 2.1 collective-permute-start.10
  125.9 17.3 %inverse_factor.2 = (f32[512,512]{1,0:T(8,128)S(1)}, f32[512,512]{1,0:T(8,128)S(1)}, f32[512,512]{1,0:T(8,128)S(1)}) custom-call(f32[512,512]{1,0:T(8,128)S(1)} %maximum_select_fusion.1.refs_0_), custom_call_target="tpu_custom_call" | custom-call | flops 10000000000 | bytes 2097152 | tf_op jit(solution)/shard_map/inverse_factor/pallas_call | solution.py:131
  149.8 16.0 %inverse_factor.3 = (f32[512,512]{1,0:T(8,128)}, f32[512,512]{1,0:T(8,128)}, f32[512,512]{1,0:T(8,128)S(1)}) custom-call(f32[512,512]{1,0:T(8,128)S(1)} %copy-done.10, f32[512,512]{1,0:T(8,128)S(1)} %copy-done.12, f32[512,512]{1,0:T(8,128)S(1)} %copy-done.14), custom_call_target="tpu_custom_call" | custom-call | flops 10000000000 | bytes 2097152 | tf_op jit(solution)/shard_map/inverse_factor/pallas_call | solution.py:131
  167.7 13.3 %all-gather.2.cloned.1.call-done.product_ref = f32[512,1792]{1,0:T(8,128)} async-done(((f32[32,1792]{1,0:T(8,128)}), f32[512,1792]{1,0:T(8,128)}) %all-gather.2.cloned.1.call-update) | async-done | bytes 3670032 | tf_op jit(solution)/shard_map/all_gather | solution.py:390
  183.1 5.2 %right_and_squares.1 = (f32[512,1792]{1,0:T(8,128)S(1)}, f32[8,512]{1,0:T(8,128)S(1)}) custom-call(f32[512,512]{1,0:T(8,128)S(1)} %get-tuple-element.21.inverse_ref, f32[512,1792]{1,0:T(8,128)S(1)} %copy-done.6), custom_call_target="tpu_custom_call" | custom-call | flops 1000000000 | bytes 4194304 | tf_op jit(solution)/shard_map/right_and_squares/pallas_call | solution.py:162
  190.7 6.5 %all-to-all-start.4 = ((f32[16,1,512]{2,1,0:T(1,128)}), f32[16,1,512]{2,1,0:T(1,128)S(1)}, u32[]{:S(2)}, u32[]{:S(2)}) async-start(f32[16,1,512]{2,1,0:T(1,128)} %broadcast_in_dim.34), calls=%async_computation.5 | async-start | bytes 65536 | tf_op jit(solution)/shard_map/all_to_all | solution.py:336
  199.2 4.7 %momentum_update.1 = f32[256,1792]{1,0:T(8,128)} custom-call(f32[256,1792]{1,0:T(8,128)S(1)} %convert_add_fusion.buffer_ref, f32[256,512]{1,0:T(8,128)S(1)} %fusion.1.ortho_ref, f32[512,1792]{1,0:T(8,128)S(1)} %copy-done.3), custom_call_target="tpu_custom_call" | custom-call | flops 1000000000 | bytes 4194304 | tf_op jit(solution)/shard_map/momentum_update/pallas_call | solution.py:162
  207.4 4.8 %weights_update.1 = (f32[256,1792]{1,0:T(8,128)}, f32[32,1792]{1,0:T(8,128)}) custom-call(s32[1]{0:T(128)} %bitcast.start_ref, f32[256,1792]{1,0:T(8,128)S(1)} %copy-done.7, f32[256,512]{1,0:T(8,128)S(1)} %fusion.1.ortho_ref, f32[512,1792]{1,0:T(8,128)S(1)} %copy-done.4, f32[16,512]{1,0:T(8,128)S(1)} %bitcast.20), custom_call_target="tpu_custom_call" | custom-call | flops 1000000000 | bytes 4194304 | tf_op jit(solution)/shard_map/weights_update/pallas_call | solution.py:162
  (70 shorter events, 34.3 us)
Async XLA Ops:
  7.2 5.3 %copy-start.8 = (f32[32,1792]{1,0:T(8,128)S(1)}, f32[32,1792]{1,0:T(8,128)}, u32[]{:S(2)}) copy-start(f32[32,1792]{1,0:T(8,128)} %refs_0_.1) | copy-start | bytes 688132
  9.1 27.8 %collective-permute-start.8 = (f32[256,1792]{1,0:T(8,128)S(1)}, f32[256,1792]{1,0:T(8,128)}, u32[]{:S(2)}, u32[]{:S(2)}) collective-permute-start(f32[256,1792]{1,0:T(8,128)S(1)} %convert_add_fusion.buffer_ref), channel_id=1, source_target_pairs={{0,16},{16,0},{1,17},{17,1},{2,18},{18,2},{3,19},{19,3},{4,20},{20... | collective-permute-start | bytes 5505032 | tf_op jit(solution)/shard_map/ppermute | solution.py:331
  12.4 11.7 %collective-permute-start.3 = (f32[32,1792]{1,0:T(8,128)S(1)}, f32[32,1792]{1,0:T(8,128)S(1)}, u32[]{:S(2)}, u32[]{:S(2)}) collective-permute-start(f32[32,1792]{1,0:T(8,128)S(1)} %copy-done.8), channel_id=1, source_target_pairs={{0,64},{32,96},{64,128},{96,160},{128,192},{160,224},{192,0},{224,... | collective-permute-start | bytes 688136 | tf_op jit(solution)/shard_map/ppermute | solution.py:331
  13.7 14.8 %collective-permute-start.1 = (f32[32,1792]{1,0:T(8,128)S(1)}, f32[32,1792]{1,0:T(8,128)S(1)}, u32[]{:S(2)}, u32[]{:S(2)}) collective-permute-start(f32[32,1792]{1,0:T(8,128)S(1)} %copy-done.8), channel_id=1, source_target_pairs={{0,192},{32,224},{64,0},{96,32},{128,64},{160,96},{192,128},{224,1... | collective-permute-start | bytes 688136 | tf_op jit(solution)/shard_map/ppermute | solution.py:331
  24.2 9.9 %collective-permute-start.4 = (f32[32,1792]{1,0:T(8,128)S(1)}, f32[32,1792]{1,0:T(8,128)S(1)}, u32[]{:S(2)}, u32[]{:S(2)}) collective-permute-start(f32[32,1792]{1,0:T(8,128)S(1)} %collective-permute-done.3.refs_7_), channel_id=1, source_target_pairs={{0,32},{32,64},{64,96},{96,128},{128,160},{160,192},{192,224},{224... | collective-permute-start | bytes 688136 | tf_op jit(solution)/shard_map/ppermute | solution.py:331
  28.5 6.3 %collective-permute-start.2 = (f32[32,1792]{1,0:T(8,128)S(1)}, f32[32,1792]{1,0:T(8,128)S(1)}, u32[]{:S(2)}, u32[]{:S(2)}) collective-permute-start(f32[32,1792]{1,0:T(8,128)S(1)} %collective-permute-done.1.refs_2_), channel_id=1, source_target_pairs={{0,224},{32,0},{64,32},{96,64},{128,96},{160,128},{192,160},{224,1... | collective-permute-start | bytes 688136 | tf_op jit(solution)/shard_map/ppermute | solution.py:331
  29.0 10.7 %collective-permute-start = (f32[32,1792]{1,0:T(8,128)S(1)}, f32[32,1792]{1,0:T(8,128)S(1)}, u32[]{:S(2)}, u32[]{:S(2)}) collective-permute-start(f32[32,1792]{1,0:T(8,128)S(1)} %copy-done.8), channel_id=1, source_target_pairs={{0,224},{32,0},{64,32},{96,64},{128,96},{160,128},{192,160},{224,1... | collective-permute-start | bytes 688136 | tf_op jit(solution)/shard_map/ppermute | solution.py:331
  31.1 8.5 %collective-permute-start.7 = (f32[32,1792]{1,0:T(8,128)S(1)}, f32[32,1792]{1,0:T(8,128)S(1)}, u32[]{:S(2)}, u32[]{:S(2)}) collective-permute-start(f32[32,1792]{1,0:T(8,128)S(1)} %copy-done.8), channel_id=1, source_target_pairs={{0,32},{32,64},{64,96},{96,128},{128,160},{160,192},{192,224},{224... | collective-permute-start | bytes 688136 | tf_op jit(solution)/shard_map/ppermute | solution.py:331
  34.1 6.5 %collective-permute-start.5 = (f32[16,1792]{1,0:T(8,128)S(1)}, f32[16,1792]{1,0:T(8,128)S(1)}, u32[]{:S(2)}, u32[]{:S(2)}) collective-permute-start(f32[16,1792]{1,0:T(8,128)S(1)} %slice.20), channel_id=1, source_target_pairs={{0,32},{32,64},{64,96},{96,128},{128,160},{160,192},{192,224},{224... | collective-permute-start | bytes 344072 | tf_op jit(solution)/shard_map/ppermute | solution.py:331
  34.8 7.3 %collective-permute-start.6 = (f32[16,1792]{1,0:T(8,128)S(1)}, f32[16,1792]{1,0:T(8,128)S(1)}, u32[]{:S(2)}, u32[]{:S(2)}) collective-permute-start(f32[16,1792]{1,0:T(8,128)S(1)} %slice.21), channel_id=1, source_target_pairs={{0,224},{32,0},{64,32},{96,64},{128,96},{160,128},{192,160},{224,1... | collective-permute-start | bytes 344072 | tf_op jit(solution)/shard_map/ppermute | solution.py:331
  39.3 6.6 %copy-start = (f32[512,1792]{1,0:T(8,128)}, f32[512,1792]{1,0:T(8,128)S(1)}, u32[]{:S(2)}) copy-start(f32[512,1792]{1,0:T(8,128)S(1)} %maximum_select_fusion.refs_9_.chip_ref) | copy-start | bytes 11010052
  62.6 12.5 %all-to-all-start.1 = ((f32[16,16,512]{2,1,0:T(8,128)}), f32[16,16,512]{2,1,0:T(8,128)S(1)}, u32[]{:S(2)}, u32[]{:S(2)}) async-start(f32[16,16,512]{2,1,0:T(8,128)} %broadcast_in_dim.13), calls=%async_computation.1 | async-start | bytes 1048576 | tf_op jit(solution)/shard_map/all_to_all | solution.py:336
  66.2 80.0 %reduce-scatter.2.cloned.1.call-start = ((), (), s32[]{:S(2)}) async-start(), calls=%async_computation.6 | async-start | bytes 2064384 | tf_op jit(solution)/shard_map/reduce_scatter | solution.py:375
  75.2 11.0 %collective-permute-start.9 = (f32[8,32,512]{2,1,0:T(8,128)S(1)}, f32[8,32,512]{2,1,0:T(8,128)S(1)}, u32[]{:S(2)}, u32[]{:S(2)}) collective-permute-start(f32[8,32,512]{2,1,0:T(8,128)S(1)} %fusion), channel_id=1, source_target_pairs={{0,16},{16,0},{1,17},{17,1},{2,18},{18,2},{3,19},{19,3},{4,20},{20... | collective-permute-start | bytes 1572872 | tf_op jit(solution)/shard_map/ppermute | solution.py:331
  79.7 2.0 copy-start.1
  86.1 94.9 %all-gather.2.cloned.1.call-start = ((), (), s32[]{:S(2)}) async-start(), calls=%async_computation.7 | async-start | bytes 3899392 | tf_op jit(solution)/shard_map/all_gather | solution.py:390
  122.2 3.6 %collective-permute-start.10 = (f32[256,512]{1,0:T(8,128)S(1)}, f32[256,512]{1,0:T(8,128)S(1)}, u32[]{:S(2)}, u32[]{:S(2)}) collective-permute-start(f32[256,512]{1,0:T(8,128)S(1)} %bitcast.25), channel_id=1, source_target_pairs={{0,16},{16,0},{1,17},{17,1},{2,18},{18,2},{3,19},{19,3},{4,20},{20... | collective-permute-start | bytes 1572872 | tf_op jit(solution)/shard_map/ppermute | solution.py:331
  149.8 16.0 %copy-start.16 = (f32[8,2,32,512]{3,2,1,0:T(8,128)S(1)}, f32[8,2,32,512]{3,2,1,0:T(8,128)}, u32[]{:S(2)}) copy-start(f32[8,2,32,512]{3,2,1,0:T(8,128)} %copy-done.15) | copy-start | bytes 3145732
  181.0 2.0 copy-start.6
  188.2 1.8 copy-start.2
  190.7 13.2 %all-to-all-start.4 = ((f32[16,1,512]{2,1,0:T(1,128)}), f32[16,1,512]{2,1,0:T(1,128)S(1)}, u32[]{:S(2)}, u32[]{:S(2)}) async-start(f32[16,1,512]{2,1,0:T(1,128)} %broadcast_in_dim.34), calls=%async_computation.5 | async-start | bytes 65536 | tf_op jit(solution)/shard_map/all_to_all | solution.py:336
  197.2 2.0 copy-start.3
  203.9 2.0 copy-start.4
  205.9 1.5 copy-start.7
  (8 other events, 8.9 us)
Sparse Core Ops, SparseCore 0:
  86.3 38.0 reduce-scatter.1
  146.3 34.7 all-gather.1

commit v2 on v1

--- a/solution.py
+++ b/solution.py
@@ -27,23 +27,20 @@
     return high, middle, low
 
 
-def inverse_root(value):
-    guess = lax.rsqrt(value)
-    return guess * (1.5 - 0.5 * value * (guess * guess))
-
-
 def invert_factor_8(entries):
     size = len(entries)
     left = [row[:] for row in entries]
     inverse = [[None] * size for _ in range(size)]
     for j in range(size):
-        root = inverse_root(left[j][j])
+        root = lax.rsqrt(left[j][j])
+        square = root * root
+        for i in range(j + 1, size):
+            share = left[i][j] * square
+            for k in range(j + 1, i + 1):
+                left[i][k] = left[i][k] - share * left[k][j]
         column = [None] * size
         for i in range(j + 1, size):
             column[i] = left[i][j] * root
-        for i in range(j + 1, size):
-            for k in range(j + 1, i + 1):
-                left[i][k] = left[i][k] - column[i] * column[k]
         for c in range(j):
             inverse[j][c] = inverse[j][c] * root
         inverse[j][j] = root
@@ -56,9 +53,10 @@
 
 def invert_factor_tile(state, result):
     sublane = lax.broadcasted_iota(jnp.int32, (8, TILE), 0)
+    lane = lax.broadcasted_iota(jnp.int32, (8, TILE), 1)
+    rows = state[0:8, :]
     for step in range(TILE // 8):
         at = 8 * step
-        rows = state[at : at + 8, :]
         lanes = [jnp.broadcast_to(rows[:, at + j : at + j + 1], (8, TILE)) for j in range(8)]
         entries = [
             [jnp.broadcast_to(lanes[j][i : i + 1, :], (8, TILE)) for j in range(i + 1)] for i in range(8)
@@ -74,29 +72,35 @@
             first = one if first is None else first + one
             second = two if second is None else second + two
         result[at : at + 8, :] = second
-        if at + 8 < TILE:
+        after = at + 8
+        if after == TILE:
+            break
+        next_first, next_second = state[after : after + 8, :TILE], state[after : after + 8, TILE:]
+        for k in range(8):
+            one = jnp.broadcast_to(first[k : k + 1, :], (8, TILE))
+            two = jnp.broadcast_to(second[k : k + 1, :], (8, TILE))
+            factor = jnp.sum(jnp.where(lane == after + sublane, one, 0.0), axis=1, keepdims=True)
+            next_first, next_second = next_first - factor * one, next_second - factor * two
+        rows = jnp.concatenate([next_first, next_second], 1)
+        if after + 8 < TILE:
             high, middle, low = split_three(jnp.concatenate([first, second], 1))
             right = jnp.concatenate([high, middle, high, low, high, middle], 0).astype(jnp.bfloat16)
             high, middle, low = high[:, :TILE], middle[:, :TILE], low[:, :TILE]
             left = jnp.concatenate([high, high, middle, high, low, middle], 0).astype(jnp.bfloat16)
             update = lax.dot_general(left, right, (((0,), (0,)), ((), ())), preferred_element_type=F32)
-            state[at + 8 :, :] = state[at + 8 :, :] - update[at + 8 :, :]
-
-
-def inverse_factor_kernel(first, last, rest_in, inverse_in, result_in, rest, inverse, result, state, tile, panel):
+            state[after + 8 :, :] = state[after + 8 :, :] - update[after + 8 :, :]
+
+
+def inverse_factor_kernel(gram, earlier, inverse, rest, state, tile, panel):
+    rows = lax.broadcasted_iota(jnp.int32, (R, R), 0)
+    columns = lax.broadcasted_iota(jnp.int32, (R, R), 1)
+    rest[...] = gram[...]
+    inverse[...] = jnp.where(rows == columns, 1.0, 0.0)
     identity = jnp.where(
         lax.broadcasted_iota(jnp.int32, (TILE, TILE), 0) == lax.broadcasted_iota(jnp.int32, (TILE, TILE), 1), 1.0, 0.0
     )
-    rest[...] = rest_in[...]
-    if first == 0:
-        rows = lax.broadcasted_iota(jnp.int32, (R, R), 0)
-        columns = lax.broadcasted_iota(jnp.int32, (R, R), 1)
-        inverse[...] = jnp.where(rows == columns, 1.0, 0.0)
-    else:
-        inverse[...] = inverse_in[...]
-        result[...] = result_in[...]
-
-    @pl.loop(first, last)
+
+    @pl.loop(0, R // TILE)
     def _(k):
         at = pl.multiple_of(k * TILE, TILE)
         state[:, :TILE] = rest[pl.ds(at, TILE), pl.ds(at, TILE)]
@@ -104,7 +108,7 @@
         invert_factor_tile(state, tile)
         upper = jnp.dot(tile[...], rest[pl.ds(at, TILE), :], precision=HIGHEST, preferred_element_type=F32)
         lower = jnp.dot(tile[...], inverse[pl.ds(at, TILE), :], precision=HIGHEST, preferred_element_type=F32)
-        result[pl.ds(at, TILE), :] = lower
+        inverse[pl.ds(at, TILE), :] = lower
         panel[...] = upper
         for i in range(1, R // TILE):
 
@@ -117,27 +121,23 @@
                 inverse[below, :] -= lax.dot_general(factor, lower, dims, precision=HIGHEST, preferred_element_type=F32)
 
 
-def factor_steps(first, last, rest, inverse=None, result=None):
+def inverse_factor(gram, earlier):
     whole = pl.BlockSpec(memory_space=pltpu.VMEM)
-    square = jax.ShapeDtypeStruct((R, R), F32)
-    given = (rest,) if first == 0 else (rest, inverse, result)
-
-    def kernel(*refs):
-        if first == 0:
-            inverse_factor_kernel(first, last, refs[0], None, None, *refs[1:])
-        else:
-            inverse_factor_kernel(first, last, *refs)
-
     return pl.pallas_call(
-        kernel,
-        out_shape=(square, square, square),
-        in_specs=[whole] * len(given),
-        out_specs=(whole, whole, whole),
-        scratch_shapes=[pltpu.VMEM((TILE, 2 * TILE), F32), pltpu.VMEM((TILE, TILE), F32), pltpu.VMEM((TILE, R), F32)],
-        compiler_params=pltpu.CompilerParams(vmem_limit_bytes=24 * 2**20),
-        cost_estimate=pl.CostEstimate(flops=10**10, bytes_accessed=2 * 4 * R * R, transcendentals=R),
+        inverse_factor_kernel,
+        out_shape=jax.ShapeDtypeStruct((R, R), F32),
+        in_specs=[whole, pl.BlockSpec(memory_space=pl.ANY)],
+        out_specs=whole,
+        scratch_shapes=[
+            pltpu.VMEM((R, R), F32),
+            pltpu.VMEM((TILE, 2 * TILE), F32),
+            pltpu.VMEM((TILE, TILE), F32),
+            pltpu.VMEM((TILE, R), F32),
+        ],
+        compiler_params=pltpu.CompilerParams(vmem_limit_bytes=12 * 2**20),
+        cost_estimate=pl.CostEstimate(flops=3 * 10**10, bytes_accessed=2 * 4 * R * R, transcendentals=R),
         name="inverse_factor",
-    )(*given)
+    )(gram, earlier)
 
 
 def split_two(values):
@@ -152,13 +152,13 @@
     return one(first[0], second[0]) + (one(first[0], second[1]) + one(first[1], second[0]))
 
 
-WIDTH = 256
+WIDTH = 896
 NN = ((1,), (0,))
 NT = ((1,), (1,))
-LIMIT = 32 * 2**20
-
-
-def call(kernel, steps, operands, specs, outs, out_specs, scratch=(), name=None, flops=10**9):
+LIMIT = 52 * 2**20
+
+
+def call(kernel, steps, operands, specs, outs, out_specs, scratch=(), name=None, flops=3 * 10**9):
     return pl.pallas_call(
         kernel,
         grid=(steps,),
@@ -236,7 +236,7 @@
     columns = product.shape[1]
     steps = columns // WIDTH
 
-    def kernel(inverse_ref, product_ref, out, sums, high, low, total):
+    def kernel(inverse_ref, product_ref, out_high, out_low, sums, high, low, total):
         j = pl.program_id(0)
 
         @pl.when(j == 0)
@@ -245,9 +245,9 @@
             total[...] = jnp.zeros_like(total)
 
         right = product3((high[...], low[...]), split_two(product_ref[...]), NN)
-        out[...] = right
+        out_high[...], out_low[...] = split_two(right)
         squares = right * right
-        total[...] += squares[:, :128] + squares[:, 128:]
+        total[...] += sum(squares[:, i : i + 128] for i in range(0, WIDTH, 128))
 
         @pl.when(j == steps - 1)
         def _():
@@ -256,13 +256,14 @@
             )
 
     half = pltpu.VMEM((R, R), jnp.bfloat16)
+    pair = jax.ShapeDtypeStruct((R, columns), jnp.bfloat16)
     return call(
         kernel,
         steps,
         (inverse, product),
         [whole(R, R), wide(R)],
-        (jax.ShapeDtypeStruct((R, columns), F32), jax.ShapeDtypeStruct((8, R), F32)),
-        (wide(R), whole(8, R)),
+        (pair, pair, jax.ShapeDtypeStruct((8, R), F32)),
+        (wide(R), wide(R), whole(8, R)),
         (half, half, pltpu.VMEM((R, 128), F32)),
         name="right_and_squares",
     )
@@ -271,19 +272,21 @@
 def momentum_update(buffer, ortho, right):
     rows, columns = buffer.shape
 
-    def kernel(buffer_ref, ortho_ref, right_ref, out, high, low):
+    def kernel(buffer_ref, ortho_ref, right_high, right_low, out, high, low):
         @pl.when(pl.program_id(0) == 0)
         def _():
             high[...], low[...] = split_two(ortho_ref[...])
 
-        out[...] = buffer_ref[...] - decay_keep * product3((high[...], low[...]), split_two(right_ref[...]), NN)
+        out[...] = buffer_ref[...] - decay_keep * product3(
+            (high[...], low[...]), (right_high[...], right_low[...]), NN
+        )
 
     half = pltpu.VMEM((rows, R), jnp.bfloat16)
     return call(
         kernel,
         columns // WIDTH,
-        (buffer, ortho, right),
-        [wide(rows), whole(rows, R), wide(R)],
+        (buffer, ortho, *right),
+        [wide(rows), whole(rows, R), wide(R), wide(R)],
         jax.ShapeDtypeStruct((rows, columns), F32),
         wide(rows),
         (half, half),
@@ -295,7 +298,7 @@
     rows, columns = weights.shape
     count = sums.shape[0]
 
-    def kernel(start_ref, weights_ref, ortho_ref, right_ref, sums_ref, out, own, high, low, own_scale):
+    def kernel(start_ref, weights_ref, ortho_ref, right_high, right_low, sums_ref, out, own, high, low, own_scale):
         at = pl.multiple_of(start_ref[0], share)
 
         @pl.when(pl.program_id(0) == 0)
@@ -307,15 +310,18 @@
             picked = jnp.sum(jnp.where(chosen, jnp.broadcast_to(scale, (share, R)), 0.0), axis=1, keepdims=True)
             own_scale[...] = jnp.broadcast_to(picked, own_scale.shape)
 
-        out[...] = weights_ref[...] - step_size * product3((high[...], low[...]), split_two(right_ref[...]), NN)
-        own[...] = right_ref[pl.ds(at, share), :] / own_scale[...]
+        out[...] = weights_ref[...] - step_size * product3(
+            (high[...], low[...]), (right_high[...], right_low[...]), NN
+        )
+        here = pl.ds(at, share)
+        own[...] = (right_high[here, :].astype(F32) + right_low[here, :].astype(F32)) / own_scale[...]
 
     half = pltpu.VMEM((rows, R), jnp.bfloat16)
     return call(
         kernel,
         columns // WIDTH,
-        (start, weights, ortho, right, sums),
-        [pl.BlockSpec(memory_space=pltpu.SMEM), wide(rows), whole(rows, R), wide(R), whole(count, R)],
+        (start, weights, ortho, *right, sums),
+        [pl.BlockSpec(memory_space=pltpu.SMEM), wide(rows), whole(rows, R), wide(R), wide(R), whole(count, R)],
         (jax.ShapeDtypeStruct((rows, columns), F32), jax.ShapeDtypeStruct((share, columns), F32)),
         (wide(rows), wide(share)),
         (half, half, pltpu.VMEM((share, WIDTH), F32)),
@@ -385,15 +391,13 @@
     gram = jnp.where(
         core == 0, jnp.concatenate([gram, gram_other], 0), jnp.concatenate([gram_other, gram], 0)
     )
-    state = factor_steps(0, 2, gram)
-    state, product = lax.optimization_barrier((state, product))
+    inverse = inverse_factor(gram, product)
     product = lax.all_gather(product, ("z", "core"), axis=0, tiled=True)
-    _, _, inverse = factor_steps(2, 4, *state)
 
     height = rows // 2
     left_own = jnp.where(core == 0, left_all[:, :height], left_all[:, height:])
     ortho = dot(left_own, inverse, ((0,), (1,)), HIGHEST)
-    right_t, sums = right_and_squares(inverse, product)
+    *right_t, sums = right_and_squares(inverse, product)
     sums = spread(sums[:1], ("x", "y"), XY).reshape(XY, R)
     start = jnp.full((1,), (2 * z + core) * share, jnp.int32)
     new_momentum = momentum_update(buffer, ortho, right_t)

time: 220 us -> 220 us (level)
  waiting for transfers between devices: 37.2 us -> 64.6 us
  local copies, waits for them, and re-layouts: 21.8 us -> 1.61 us
  Pallas kernels: 54.8 us -> 50.2 us
  blocking collectives: 49.3 us -> 46.9 us
    reduce_scatter x1, waiting for transfers between devices: 0.01 us -> 39.3 us  [local(): product = lax.psum_scatter(product, 'z', scatter_dimension=0, tiled=True)]
    unnamed x35 -> x7, local copies, waits for them, and re-layouts: 20.3 us -> 0.02 us
    all_gather x1, waiting for transfers between devices: 13.3 us -> 0.02 us  [local(): product = lax.all_gather(product, ('z', 'core'), axis=0, tiled=True)]
    pallas_call x2 -> x1, Pallas kernels: 33.2 us -> 24.6 us  [inverse_factor(): pl.pallas_call(inverse_factor_kernel, out_shape=jax.ShapeDtypeStruct((R,...]
    pallas_call x5, Pallas kernels: 21.5 us -> 25.6 us  [call(): pl.pallas_call(kernel, grid=(steps,), out_shape=outs, in_specs=specs, out...]
    all_to_all x2, starting transfers between devices: 10.1 us -> 7.07 us  [spread(): return lax.all_to_all(whole, axes, 0, 0, tiled=True)]
    all_to_all x2, blocking collectives: 33.6 us -> 30.9 us  [spread(): return lax.all_to_all(whole, axes, 0, 0, tiled=True)]
  transfers between devices with their start and end apart: 15 -> 15, of which waited for: 9 -> 9; matrix products, arithmetic and copies ran while one was open for 3% -> 3% of each run, Pallas kernels for 19% -> 13%
where the time goes in v2:
time: 220 us
  waiting for transfers between devices  64.6 us (29%)
  Pallas kernels  50.2 us (23%)
  blocking collectives  46.9 us (21%)
  starting transfers between devices  32.9 us (15%)
  between operations  14.2 us (6%)
  other arithmetic  6.67 us (3%)
  matrix products  2.84 us (1%)
    reduce_scatter x1, waiting for transfers between devices, local(): product = lax.psum_scatter(product, 'z', scatter_dimension=0, tiled=True)  39.3 us
    all_to_all x2, blocking collectives, spread(): return lax.all_to_all(whole, axes, 0, 0, tiled=True)  30.9 us
    ppermute x11, starting transfers between devices, shift(): lax.ppermute(values, axis, [(i, (i + by) % size) for i in range(size)])  25.8 us
    pallas_call x5, Pallas kernels, call(): pl.pallas_call(kernel, grid=(steps,), out_shape=outs, in_specs=specs, out...  25.6 us
    pallas_call x1, Pallas kernels, inverse_factor(): pl.pallas_call(inverse_factor_kernel, out_shape=jax.ShapeDtypeStruct((R,...  24.6 us
    all_to_all x1, blocking collectives, local(): lax.all_to_all(part.reshape(XY, -1, rows), ('x', 'y'), 0, 0, tiled=True)  15.9 us
    ppermute x11, waiting for transfers between devices, shift(): lax.ppermute(values, axis, [(i, (i + by) % size) for i in range(size)])  14.7 us
    all_to_all x2, waiting for transfers between devices, spread(): return lax.all_to_all(whole, axes, 0, 0, tiled=True)  10.5 us
  transfers between devices with their start and end apart: 15, of which 9 were waited for; matrix products, arithmetic and copies ran while one was open for 3% of the time, Pallas kernels for 13%

profile of v2, /device:TPU:1, one launch (start us, length us, event | category | flops | bytes accessed | tf_op | source)
XLA Modules:
  0.0 219.9 jit_solution(9466514071989398038)
XLA Ops:
  7.2 1.9 convert_add_fusion.buffer_ref
  9.1 3.3 %collective-permute-start.8 = (f32[256,1792]{1,0:T(8,128)S(1)}, f32[256,1792]{1,0:T(8,128)}, u32[]{:S(2)}, u32[]{:S(2)}) collective-permute-start(f32[256,1792]{1,0:T(8,128)S(1)} %convert_add_fusion.buffer_ref), channel_id=1, source_target_pairs={{0,16},{16,0},{1,17},{17,1},{2,18},{18,2},{3,19},{19,3},{4,20},{20... | collective-permute-start | bytes 5505032 | tf_op jit(solution)/shard_map/ppermute | solution.py:337
  13.7 3.0 %collective-permute-start.1 = (f32[32,1792]{1,0:T(8,128)S(1)}, f32[32,1792]{1,0:T(8,128)S(1)}, u32[]{:S(2)}, u32[]{:S(2)}) collective-permute-start(f32[32,1792]{1,0:T(8,128)S(1)} %copy-done.1), channel_id=1, source_target_pairs={{0,192},{32,224},{64,0},{96,32},{128,64},{160,96},{192,128},{224,1... | collective-permute-start | bytes 688136 | tf_op jit(solution)/shard_map/ppermute | solution.py:337
  16.7 7.4 %collective-permute-done.3.refs_7_ = f32[32,1792]{1,0:T(8,128)S(1)} collective-permute-done((f32[32,1792]{1,0:T(8,128)S(1)}, f32[32,1792]{1,0:T(8,128)S(1)}, u32[]{:S(2)}, u32[]{:S(2)}) %collective-permute-start.3) | collective-permute-done | bytes 229408 | tf_op jit(solution)/shard_map/ppermute | solution.py:337
  24.2 4.1 %collective-permute-start.4 = (f32[32,1792]{1,0:T(8,128)S(1)}, f32[32,1792]{1,0:T(8,128)S(1)}, u32[]{:S(2)}, u32[]{:S(2)}) collective-permute-start(f32[32,1792]{1,0:T(8,128)S(1)} %collective-permute-done.3.refs_7_), channel_id=1, source_target_pairs={{0,32},{32,64},{64,96},{96,128},{128,160},{160,192},{192,224},{224... | collective-permute-start | bytes 688136 | tf_op jit(solution)/shard_map/ppermute | solution.py:337
  29.0 2.2 collective-permute-start
  31.2 2.9 %collective-permute-done.4.refs_6_ = f32[32,1792]{1,0:T(8,128)S(1)} collective-permute-done((f32[32,1792]{1,0:T(8,128)S(1)}, f32[32,1792]{1,0:T(8,128)S(1)}, u32[]{:S(2)}, u32[]{:S(2)}) %collective-permute-start.4) | collective-permute-done | bytes 229408 | tf_op jit(solution)/shard_map/ppermute | solution.py:337
  34.8 2.1 collective-permute-start.6
  36.9 4.2 %maximum_select_fusion.refs_9_.chip_ref = f32[512,1792]{1,0:T(8,128)} fusion(f32[256,1792]{1,0:T(8,128)} %collective-permute-done.8, f32[256,1792]{1,0:T(8,128)S(1)} %convert_add_fusion.buffer_ref, pred[]{:T(512)S(6)} %eq.4), kind=kLoop, calls=%fused_computation | loop fusion | flops 2752512 | bytes 7340033 | tf_op jit(solution)/shard_map/jit(_where)/select_n | solution.py:369
  42.2 4.5 %left_product.1 = f32[256,512]{1,0:T(8,128)} custom-call(f32[32,1792]{1,0:T(8,128)S(1)} %copy-done.1, f32[32,1792]{1,0:T(8,128)S(1)} %collective-permute-done.refs_1_, f32[32,1792]{1,0:T(8,128)S(1)} %collective-permute-done.1.refs_2_, f32[32,1792]{1,0:T(8,128)S(1)} %collective-permute-done.2.refs_3_, f32[16,1792]{1,0:T(8,128)S(1)} %collective-permute-done.5.refs_4_, ...), custom_call_target="tpu_custom_call" | custom-call | flops 3000000000 | bytes 4194304 | tf_op jit(solution)/shard_map/left_product/pallas_call | solution.py:162
  46.7 15.9 %all_to_all.25 = f32[16,16,512]{2,1,0:T(8,128)S(1)} all-to-all(f32[16,16,512]{2,1,0:T(8,128)} %bitcast.26), channel_id=1, replica_groups=mesh['z'=8,'core'=2,'x'=4,'y'=4] {'x','y'}, dimensions={0} | all-to-all | bytes 1048576 | tf_op jit(solution)/shard_map/all_to_all | solution.py:376
  63.5 3.6 %all-to-all-start.1 = ((f32[16,16,512]{2,1,0:T(8,128)}), f32[16,16,512]{2,1,0:T(8,128)S(1)}, u32[]{:S(2)}, u32[]{:S(2)}) async-start(f32[16,16,512]{2,1,0:T(8,128)} %broadcast_in_dim.13), calls=%async_computation.1 | async-start | bytes 1048576 | tf_op jit(solution)/shard_map/all_to_all | solution.py:342
  67.1 8.8 %all-to-all-done.1 = f32[16,16,512]{2,1,0:T(8,128)S(1)} async-done(((f32[16,16,512]{2,1,0:T(8,128)}), f32[16,16,512]{2,1,0:T(8,128)S(1)}, u32[]{:S(2)}, u32[]{:S(2)}) %all-to-all-start.1) | async-done | bytes 524320 | tf_op jit(solution)/shard_map/all_to_all | solution.py:342
  76.1 4.5 %right_product.1 = f32[256,1792]{1,0:T(8,128)} custom-call(f32[256,512]{1,0:T(8,128)S(1)} %bitcast.18, f32[512,1792]{1,0:T(8,128)} %maximum_select_fusion.refs_9_.chip_ref), custom_call_target="tpu_custom_call" | custom-call | flops 3000000000 | bytes 4194304 | tf_op jit(solution)/shard_map/right_product/pallas_call | solution.py:162
  80.7 39.3 %reduce-scatter.2.cloned.1.call-done.earlier = f32[32,1792]{1,0:T(8,128)} async-done(((f32[256,1792]{1,0:T(8,128)}), f32[32,1792]{1,0:T(8,128)}) %reduce-scatter.2.cloned.1.call-update) | async-done | bytes 229392 | tf_op jit(solution)/shard_map/reduce_scatter | solution.py:381
  120.0 4.7 %collective-permute-start.9 = (f32[8,32,512]{2,1,0:T(8,128)S(1)}, f32[8,32,512]{2,1,0:T(8,128)S(1)}, u32[]{:S(2)}, u32[]{:S(2)}) collective-permute-start(f32[8,32,512]{2,1,0:T(8,128)S(1)} %fusion), channel_id=1, source_target_pairs={{0,16},{16,0},{1,17},{17,1},{2,18},{18,2},{3,19},{19,3},{4,20},{20... | collective-permute-start | bytes 1572872 | tf_op jit(solution)/shard_map/ppermute | solution.py:337
  127.6 15.5 %all_to_all.26 = f32[8,16,512]{2,1,0:T(8,128)S(1)} all-to-all(f32[8,16,512]{2,1,0:T(8,128)S(1)} %broadcast_in_dim.14), channel_id=1, replica_groups=mesh['z'=8,'core'=2,'x'=4,'y'=4] {'z'}, dimensions={0} | all-to-all | bytes 524288 | tf_op jit(solution)/shard_map/all_to_all | solution.py:342
  143.1 15.5 %all_to_all.27 = f32[16,16,512]{2,1,0:T(8,128)S(1)} all-to-all(f32[16,16,512]{2,1,0:T(8,128)S(1)} %broadcast_in_dim.15), channel_id=1, replica_groups=mesh['z'=8,'core'=2,'x'=4,'y'=4] {'x','y'}, dimensions={0} | all-to-all | bytes 1048576 | tf_op jit(solution)/shard_map/all_to_all | solution.py:342
  158.6 3.9 %collective-permute-start.10 = (f32[256,512]{1,0:T(8,128)S(1)}, f32[256,512]{1,0:T(8,128)S(1)}, u32[]{:S(2)}, u32[]{:S(2)}) collective-permute-start(f32[256,512]{1,0:T(8,128)S(1)} %bitcast.24), channel_id=1, source_target_pairs={{0,16},{16,0},{1,17},{17,1},{2,18},{18,2},{3,19},{19,3},{4,20},{20... | collective-permute-start | bytes 1572872 | tf_op jit(solution)/shard_map/ppermute | solution.py:337
  164.1 24.6 %inverse_factor.1.inverse_ref = f32[512,512]{1,0:T(8,128)S(1)} custom-call(f32[512,512]{1,0:T(8,128)S(1)} %maximum_select_fusion.1.gram, f32[32,1792]{1,0:T(8,128)S(1)} %copy-done), custom_call_target="tpu_custom_call" | custom-call | flops 30000001024 | bytes 2097152 | tf_op jit(solution)/shard_map/inverse_factor/pallas_call | solution.py:126
  190.7 7.0 %right_and_squares.1 = (bf16[512,1792]{1,0:T(8,128)(2,1)}, bf16[512,1792]{1,0:T(8,128)(2,1)}, f32[8,512]{1,0:T(8,128)S(1)}) custom-call(f32[512,512]{1,0:T(8,128)S(1)} %inverse_factor.1.inverse_ref, f32[512,1792]{1,0:T(8,128)} %all-gather.2.cloned.1.call-done.product_ref), custom_call_target="tpu_custom_call" | custom-call | flops 3000000000 | bytes 4194304 | tf_op jit(solution)/shard_map/right_and_squares/pallas_call | solution.py:162
  198.3 3.5 %all-to-all-start.4 = ((f32[16,1,512]{2,1,0:T(1,128)}), f32[16,1,512]{2,1,0:T(1,128)S(1)}, u32[]{:S(2)}, u32[]{:S(2)}) async-start(f32[16,1,512]{2,1,0:T(1,128)} %broadcast_in_dim.34), calls=%async_computation.5 | async-start | bytes 65536 | tf_op jit(solution)/shard_map/all_to_all | solution.py:342
  201.8 4.8 %momentum_update.1 = f32[256,1792]{1,0:T(8,128)} custom-call(f32[256,1792]{1,0:T(8,128)} %copy-done.2, f32[256,512]{1,0:T(8,128)S(1)} %fusion.1.ortho_ref, bf16[512,1792]{1,0:T(8,128)(2,1)} %get-tuple-element.8.right_high, bf16[512,1792]{1,0:T(8,128)(2,1)} %get-tuple-element.9.right_low), custom_call_target="tpu_custom_call" | custom-call | flops 3000000000 | bytes 4194304 | tf_op jit(solution)/shard_map/momentum_update/pallas_call | solution.py:162
  208.2 4.9 %weights_update.1 = (f32[256,1792]{1,0:T(8,128)}, f32[32,1792]{1,0:T(8,128)}) custom-call(s32[1]{0:T(128)} %bitcast.start_ref, f32[256,1792]{1,0:T(8,128)} %weights_ref.1, f32[256,512]{1,0:T(8,128)S(1)} %fusion.1.ortho_ref, bf16[512,1792]{1,0:T(8,128)(2,1)} %get-tuple-element.8.right_high, bf16[512,1792]{1,0:T(8,128)(2,1)} %get-tuple-element.9.right_low, ...), custom_call_target="tpu_custom_call" | custom-call | flops 3000000000 | bytes 4194304 | tf_op jit(solution)/shard_map/weights_update/pallas_call | solution.py:162
  (41 shorter events, 13.6 us)
Async XLA Ops:
  7.2 5.3 %copy-start.1 = (f32[32,1792]{1,0:T(8,128)S(1)}, f32[32,1792]{1,0:T(8,128)}, u32[]{:S(2)}) copy-start(f32[32,1792]{1,0:T(8,128)} %refs_0_.1) | copy-start | bytes 688132
  9.1 32.0 %copy-start.2 = (f32[256,1792]{1,0:T(8,128)}, f32[256,1792]{1,0:T(8,128)S(1)}, u32[]{:S(2)}) copy-start(f32[256,1792]{1,0:T(8,128)S(1)} %convert_add_fusion.buffer_ref) | copy-start | bytes 5505028
  9.1 27.8 %collective-permute-start.8 = (f32[256,1792]{1,0:T(8,128)S(1)}, f32[256,1792]{1,0:T(8,128)}, u32[]{:S(2)}, u32[]{:S(2)}) collective-permute-start(f32[256,1792]{1,0:T(8,128)S(1)} %convert_add_fusion.buffer_ref), channel_id=1, source_target_pairs={{0,16},{16,0},{1,17},{17,1},{2,18},{18,2},{3,19},{19,3},{4,20},{20... | collective-permute-start | bytes 5505032 | tf_op jit(solution)/shard_map/ppermute | solution.py:337
  12.4 11.7 %collective-permute-start.3 = (f32[32,1792]{1,0:T(8,128)S(1)}, f32[32,1792]{1,0:T(8,128)S(1)}, u32[]{:S(2)}, u32[]{:S(2)}) collective-permute-start(f32[32,1792]{1,0:T(8,128)S(1)} %copy-done.1), channel_id=1, source_target_pairs={{0,64},{32,96},{64,128},{96,160},{128,192},{160,224},{192,0},{224,... | collective-permute-start | bytes 688136 | tf_op jit(solution)/shard_map/ppermute | solution.py:337
  13.7 14.8 %collective-permute-start.1 = (f32[32,1792]{1,0:T(8,128)S(1)}, f32[32,1792]{1,0:T(8,128)S(1)}, u32[]{:S(2)}, u32[]{:S(2)}) collective-permute-start(f32[32,1792]{1,0:T(8,128)S(1)} %copy-done.1), channel_id=1, source_target_pairs={{0,192},{32,224},{64,0},{96,32},{128,64},{160,96},{192,128},{224,1... | collective-permute-start | bytes 688136 | tf_op jit(solution)/shard_map/ppermute | solution.py:337
  24.2 9.9 %collective-permute-start.4 = (f32[32,1792]{1,0:T(8,128)S(1)}, f32[32,1792]{1,0:T(8,128)S(1)}, u32[]{:S(2)}, u32[]{:S(2)}) collective-permute-start(f32[32,1792]{1,0:T(8,128)S(1)} %collective-permute-done.3.refs_7_), channel_id=1, source_target_pairs={{0,32},{32,64},{64,96},{96,128},{128,160},{160,192},{192,224},{224... | collective-permute-start | bytes 688136 | tf_op jit(solution)/shard_map/ppermute | solution.py:337
  28.5 6.3 %collective-permute-start.2 = (f32[32,1792]{1,0:T(8,128)S(1)}, f32[32,1792]{1,0:T(8,128)S(1)}, u32[]{:S(2)}, u32[]{:S(2)}) collective-permute-start(f32[32,1792]{1,0:T(8,128)S(1)} %collective-permute-done.1.refs_2_), channel_id=1, source_target_pairs={{0,224},{32,0},{64,32},{96,64},{128,96},{160,128},{192,160},{224,1... | collective-permute-start | bytes 688136 | tf_op jit(solution)/shard_map/ppermute | solution.py:337
  29.0 12.2 %collective-permute-start = (f32[32,1792]{1,0:T(8,128)S(1)}, f32[32,1792]{1,0:T(8,128)S(1)}, u32[]{:S(2)}, u32[]{:S(2)}) collective-permute-start(f32[32,1792]{1,0:T(8,128)S(1)} %copy-done.1), channel_id=1, source_target_pairs={{0,224},{32,0},{64,32},{96,64},{128,96},{160,128},{192,160},{224,1... | collective-permute-start | bytes 688136 | tf_op jit(solution)/shard_map/ppermute | solution.py:337
  31.2 10.0 %collective-permute-start.7 = (f32[32,1792]{1,0:T(8,128)S(1)}, f32[32,1792]{1,0:T(8,128)S(1)}, u32[]{:S(2)}, u32[]{:S(2)}) collective-permute-start(f32[32,1792]{1,0:T(8,128)S(1)} %copy-done.1), channel_id=1, source_target_pairs={{0,32},{32,64},{64,96},{96,128},{128,160},{160,192},{192,224},{224... | collective-permute-start | bytes 688136 | tf_op jit(solution)/shard_map/ppermute | solution.py:337
  34.1 7.1 %collective-permute-start.5 = (f32[16,1792]{1,0:T(8,128)S(1)}, f32[16,1792]{1,0:T(8,128)S(1)}, u32[]{:S(2)}, u32[]{:S(2)}) collective-permute-start(f32[16,1792]{1,0:T(8,128)S(1)} %slice.20), channel_id=1, source_target_pairs={{0,32},{32,64},{64,96},{96,128},{128,160},{160,192},{192,224},{224... | collective-permute-start | bytes 344072 | tf_op jit(solution)/shard_map/ppermute | solution.py:337
  34.8 7.3 %collective-permute-start.6 = (f32[16,1792]{1,0:T(8,128)S(1)}, f32[16,1792]{1,0:T(8,128)S(1)}, u32[]{:S(2)}, u32[]{:S(2)}) collective-permute-start(f32[16,1792]{1,0:T(8,128)S(1)} %slice.21), channel_id=1, source_target_pairs={{0,224},{32,0},{64,32},{96,64},{128,96},{160,128},{192,160},{224,1... | collective-permute-start | bytes 344072 | tf_op jit(solution)/shard_map/ppermute | solution.py:337
  63.5 12.5 %all-to-all-start.1 = ((f32[16,16,512]{2,1,0:T(8,128)}), f32[16,16,512]{2,1,0:T(8,128)S(1)}, u32[]{:S(2)}, u32[]{:S(2)}) async-start(f32[16,16,512]{2,1,0:T(8,128)} %broadcast_in_dim.13), calls=%async_computation.1 | async-start | bytes 1048576 | tf_op jit(solution)/shard_map/all_to_all | solution.py:342
  67.1 52.9 %reduce-scatter.2.cloned.1.call-start = ((), (), s32[]{:S(2)}) async-start(), calls=%async_computation.6 | async-start | bytes 2064384 | tf_op jit(solution)/shard_map/reduce_scatter | solution.py:381
  80.7 110.0 %all-gather.2.cloned.1.call-start = ((), (), s32[]{:S(2)}) async-start(), calls=%async_computation.7 | async-start | bytes 3899392 | tf_op jit(solution)/shard_map/all_gather | solution.py:395
  120.0 6.2 %collective-permute-start.9 = (f32[8,32,512]{2,1,0:T(8,128)S(1)}, f32[8,32,512]{2,1,0:T(8,128)S(1)}, u32[]{:S(2)}, u32[]{:S(2)}) collective-permute-start(f32[8,32,512]{2,1,0:T(8,128)S(1)} %fusion), channel_id=1, source_target_pairs={{0,16},{16,0},{1,17},{17,1},{2,18},{18,2},{3,19},{19,3},{4,20},{20... | collective-permute-start | bytes 1572872 | tf_op jit(solution)/shard_map/ppermute | solution.py:337
  143.0 21.1 %copy-start = (f32[32,1792]{1,0:T(8,128)S(1)}, f32[32,1792]{1,0:T(8,128)}, u32[]{:S(2)}) copy-start(f32[32,1792]{1,0:T(8,128)} %reduce-scatter.2.cloned.1.call-done.earlier) | copy-start | bytes 688132
  158.6 5.5 %collective-permute-start.10 = (f32[256,512]{1,0:T(8,128)S(1)}, f32[256,512]{1,0:T(8,128)S(1)}, u32[]{:S(2)}, u32[]{:S(2)}) collective-permute-start(f32[256,512]{1,0:T(8,128)S(1)} %bitcast.24), channel_id=1, source_target_pairs={{0,16},{16,0},{1,17},{17,1},{2,18},{18,2},{3,19},{19,3},{4,20},{20... | collective-permute-start | bytes 1572872 | tf_op jit(solution)/shard_map/ppermute | solution.py:337
  198.3 9.9 %all-to-all-start.4 = ((f32[16,1,512]{2,1,0:T(1,128)}), f32[16,1,512]{2,1,0:T(1,128)S(1)}, u32[]{:S(2)}, u32[]{:S(2)}) async-start(f32[16,1,512]{2,1,0:T(1,128)} %broadcast_in_dim.34), calls=%async_computation.5 | async-start | bytes 65536 | tf_op jit(solution)/shard_map/all_to_all | solution.py:342
Sparse Core Ops, SparseCore 0:
  80.8 39.1 reduce-scatter.1
  121.8 45.8 all-gather.1

commit v3 on v2

--- a/solution.py
+++ b/solution.py
@@ -15,6 +15,7 @@
 step_size = 0.5
 eps_norm = 1e-06
 
+LIMIT = 52 * 2**20
 F32 = jnp.float32
 HIGHEST = lax.Precision.HIGHEST
 
@@ -91,7 +92,7 @@
             state[after + 8 :, :] = state[after + 8 :, :] - update[after + 8 :, :]
 
 
-def inverse_factor_kernel(gram, earlier, inverse, rest, state, tile, panel):
+def inverse_factor_kernel(gram, earlier, inverse, rest, state, tile):
     rows = lax.broadcasted_iota(jnp.int32, (R, R), 0)
     columns = lax.broadcasted_iota(jnp.int32, (R, R), 1)
     rest[...] = gram[...]
@@ -100,25 +101,34 @@
         lax.broadcasted_iota(jnp.int32, (TILE, TILE), 0) == lax.broadcasted_iota(jnp.int32, (TILE, TILE), 1), 1.0, 0.0
     )
 
+    def eliminate(k):
+        here, left, right = slice(k * TILE, (k + 1) * TILE), slice(0, (k + 1) * TILE), slice((k + 1) * TILE, R)
+        lower = jnp.dot(tile[...], inverse[here, left], precision=HIGHEST, preferred_element_type=F32)
+        inverse[here, left] = lower
+        if k == R // TILE - 1:
+            return
+        upper = jnp.dot(tile[...], rest[here, right], precision=HIGHEST, preferred_element_type=F32)
+        dims = (((0,), (0,)), ((), ()))
+        for i in range(k + 1, R // TILE):
+            below = slice(i * TILE, (i + 1) * TILE)
+            skip = (i - k - 1) * TILE
+            factor = upper[:, skip : skip + TILE]
+            rest[below, below.start :] -= lax.dot_general(
+                factor, upper[:, skip:], dims, precision=HIGHEST, preferred_element_type=F32
+            )
+            inverse[below, left] -= lax.dot_general(factor, lower, dims, precision=HIGHEST, preferred_element_type=F32)
+
     @pl.loop(0, R // TILE)
     def _(k):
         at = pl.multiple_of(k * TILE, TILE)
         state[:, :TILE] = rest[pl.ds(at, TILE), pl.ds(at, TILE)]
         state[:, TILE:] = identity
         invert_factor_tile(state, tile)
-        upper = jnp.dot(tile[...], rest[pl.ds(at, TILE), :], precision=HIGHEST, preferred_element_type=F32)
-        lower = jnp.dot(tile[...], inverse[pl.ds(at, TILE), :], precision=HIGHEST, preferred_element_type=F32)
-        inverse[pl.ds(at, TILE), :] = lower
-        panel[...] = upper
-        for i in range(1, R // TILE):
-
-            @pl.when(i > k)
+        for done in range(R // TILE):
+
+            @pl.when(k == done)
             def _():
-                below = pl.ds(i * TILE, TILE)
-                factor = panel[:, i * TILE : (i + 1) * TILE]
-                dims = (((0,), (0,)), ((), ()))
-                rest[below, :] -= lax.dot_general(factor, upper, dims, precision=HIGHEST, preferred_element_type=F32)
-                inverse[below, :] -= lax.dot_general(factor, lower, dims, precision=HIGHEST, preferred_element_type=F32)
+                eliminate(done)
 
 
 def inverse_factor(gram, earlier):
@@ -132,7 +142,6 @@
             pltpu.VMEM((R, R), F32),
             pltpu.VMEM((TILE, 2 * TILE), F32),
             pltpu.VMEM((TILE, TILE), F32),
-            pltpu.VMEM((TILE, R), F32),
         ],
         compiler_params=pltpu.CompilerParams(vmem_limit_bytes=12 * 2**20),
         cost_estimate=pl.CostEstimate(flops=3 * 10**10, bytes_accessed=2 * 4 * R * R, transcendentals=R),
@@ -140,6 +149,25 @@
     )(gram, earlier)
 
 
+def copy_after(values, earlier):
+    def kernel(values_ref, _, out, done):
+        copy = pltpu.make_async_copy(values_ref, out, done)
+        copy.start()
+        copy.wait()
+
+    there = pl.BlockSpec(memory_space=pl.ANY)
+    return pl.pallas_call(
+        kernel,
+        out_shape=jax.ShapeDtypeStruct(values.shape, values.dtype),
+        in_specs=[there, there],
+        out_specs=there,
+        scratch_shapes=[pltpu.SemaphoreType.DMA],
+        compiler_params=pltpu.CompilerParams(vmem_limit_bytes=LIMIT),
+        cost_estimate=pl.CostEstimate(flops=1, bytes_accessed=2 * 4 * values.size, transcendentals=0),
+        name="copy_after",
+    )(values, earlier)
+
+
 def split_two(values):
     high = values.astype(jnp.bfloat16)
     return high, (values - high.astype(F32)).astype(jnp.bfloat16)
@@ -155,10 +183,9 @@
 WIDTH = 896
 NN = ((1,), (0,))
 NT = ((1,), (1,))
-LIMIT = 52 * 2**20
-
-
-def call(kernel, steps, operands, specs, outs, out_specs, scratch=(), name=None, flops=3 * 10**9):
+
+
+def call(kernel, steps, operands, specs, outs, out_specs, scratch=(), name=None, flops=3 * 10**9, limit=LIMIT):
     return pl.pallas_call(
         kernel,
         grid=(steps,),
@@ -166,7 +193,7 @@
         in_specs=specs,
         out_specs=out_specs,
         scratch_shapes=list(scratch),
-        compiler_params=pltpu.CompilerParams(vmem_limit_bytes=LIMIT, dimension_semantics=("arbitrary",)),
+        compiler_params=pltpu.CompilerParams(vmem_limit_bytes=limit, dimension_semantics=("arbitrary",)),
         cost_estimate=pl.CostEstimate(flops=flops, bytes_accessed=4 * 2**20, transcendentals=0),
         name=name,
     )(*operands)
@@ -205,6 +232,7 @@
         jax.ShapeDtypeStruct((ranks, rows), F32),
         whole(ranks, rows),
         name="left_product",
+        limit=16 * 2**20,
     )
 
 
@@ -391,6 +419,7 @@
     gram = jnp.where(
         core == 0, jnp.concatenate([gram, gram_other], 0), jnp.concatenate([gram_other, gram], 0)
     )
+    product = copy_after(product, gram)
     inverse = inverse_factor(gram, product)
     product = lax.all_gather(product, ("z", "core"), axis=0, tiled=True)
 

time: 220 us -> 200 us (0.909)
  waiting for transfers between devices: 64.6 us -> 46.1 us
  Pallas kernels: 50.2 us -> 46.3 us
  starting transfers between devices: 32.9 us -> 35.1 us
    reduce_scatter x1, waiting for transfers between devices: 39.3 us -> 0.02 us  [local(): product = lax.psum_scatter(product, 'z', scatter_dimension=0, tiled=True)]
    all_gather x1, waiting for transfers between devices: 0.02 us -> 19 us  [local(): product = lax.all_gather(product, ('z', 'core'), axis=0, tiled=True)]
    all_to_all x2, starting transfers between devices: 7.07 us -> 9.91 us  [spread(): return lax.all_to_all(whole, axes, 0, 0, tiled=True)]
    pallas_call x1, Pallas kernels: 24.6 us -> 21.9 us  [inverse_factor(): pl.pallas_call(inverse_factor_kernel, out_shape=jax.ShapeDtypeStruct((R,...]
  transfers between devices with their start and end apart: 15 -> 15, of which waited for: 9 -> 11; matrix products, arithmetic and copies ran while one was open for 3% -> 3% of each run, Pallas kernels for 13% -> 13%
where the time goes in v3:
time: 200 us
  blocking collectives  47.8 us (24%)
  Pallas kernels  46.3 us (23%)
  waiting for transfers between devices  46.1 us (23%)
  starting transfers between devices  35.1 us (18%)
  between operations  14.2 us (7%)
  other arithmetic  4.94 us (2%)
  matrix products  2.84 us (1%)
  local copies, waits for them, and re-layouts  2.54 us (1%)
    all_to_all x2, blocking collectives, spread(): return lax.all_to_all(whole, axes, 0, 0, tiled=True)  32 us
    ppermute x11, starting transfers between devices, shift(): lax.ppermute(values, axis, [(i, (i + by) % size) for i in range(size)])  25.1 us
    pallas_call x5, Pallas kernels, call(): pl.pallas_call(kernel, grid=(steps,), out_shape=outs, in_specs=specs, out...  23.7 us
    pallas_call x1, Pallas kernels, inverse_factor(): pl.pallas_call(inverse_factor_kernel, out_shape=jax.ShapeDtypeStruct((R,...  21.9 us
    all_gather x1, waiting for transfers between devices, local(): product = lax.all_gather(product, ('z', 'core'), axis=0, tiled=True)  19 us
    ppermute x11, waiting for transfers between devices, shift(): lax.ppermute(values, axis, [(i, (i + by) % size) for i in range(size)])  16.5 us
    all_to_all x1, blocking collectives, local(): lax.all_to_all(part.reshape(XY, -1, rows), ('x', 'y'), 0, 0, tiled=True)  15.8 us
    all_to_all x2, waiting for transfers between devices, spread(): return lax.all_to_all(whole, axes, 0, 0, tiled=True)  10.5 us
  transfers between devices with their start and end apart: 15, of which 11 were waited for; matrix products, arithmetic and copies ran while one was open for 3% of the time, Pallas kernels for 13%

profile of v3, /device:TPU:1, one launch (start us, length us, event | category | flops | bytes accessed | tf_op | source)
XLA Modules:
  0.0 199.9 jit_solution(5602120798063951466)
XLA Ops:
  7.2 1.9 convert_add_fusion.buffer_ref
  9.1 3.3 %collective-permute-start.8 = (f32[256,1792]{1,0:T(8,128)S(1)}, f32[256,1792]{1,0:T(8,128)}, u32[]{:S(2)}, u32[]{:S(2)}) collective-permute-start(f32[256,1792]{1,0:T(8,128)S(1)} %convert_add_fusion.buffer_ref), channel_id=1, source_target_pairs={{0,16},{16,0},{1,17},{17,1},{2,18},{18,2},{3,19},{19,3},{4,20},{20... | collective-permute-start | bytes 5505032 | tf_op jit(solution)/shard_map/ppermute | solution.py:365
  13.7 3.0 %collective-permute-start.1 = (f32[32,1792]{1,0:T(8,128)S(1)}, f32[32,1792]{1,0:T(8,128)S(1)}, u32[]{:S(2)}, u32[]{:S(2)}) collective-permute-start(f32[32,1792]{1,0:T(8,128)S(1)} %copy-done.2), channel_id=1, source_target_pairs={{0,192},{32,224},{64,0},{96,32},{128,64},{160,96},{192,128},{224,1... | collective-permute-start | bytes 688136 | tf_op jit(solution)/shard_map/ppermute | solution.py:365
  16.7 7.4 %collective-permute-done.3.refs_7_ = f32[32,1792]{1,0:T(8,128)S(1)} collective-permute-done((f32[32,1792]{1,0:T(8,128)S(1)}, f32[32,1792]{1,0:T(8,128)S(1)}, u32[]{:S(2)}, u32[]{:S(2)}) %collective-permute-start.3) | collective-permute-done | bytes 229408 | tf_op jit(solution)/shard_map/ppermute | solution.py:365
  24.2 4.1 %collective-permute-start.4 = (f32[32,1792]{1,0:T(8,128)S(1)}, f32[32,1792]{1,0:T(8,128)S(1)}, u32[]{:S(2)}, u32[]{:S(2)}) collective-permute-start(f32[32,1792]{1,0:T(8,128)S(1)} %collective-permute-done.3.refs_7_), channel_id=1, source_target_pairs={{0,32},{32,64},{64,96},{96,128},{128,160},{160,192},{192,224},{224... | collective-permute-start | bytes 688136 | tf_op jit(solution)/shard_map/ppermute | solution.py:365
  29.0 2.2 %collective-permute-start = (f32[32,1792]{1,0:T(8,128)S(1)}, f32[32,1792]{1,0:T(8,128)S(1)}, u32[]{:S(2)}, u32[]{:S(2)}) collective-permute-start(f32[32,1792]{1,0:T(8,128)S(1)} %copy-done.2), channel_id=1, source_target_pairs={{0,224},{32,0},{64,32},{96,64},{128,96},{160,128},{192,160},{224,1... | collective-permute-start | bytes 688136 | tf_op jit(solution)/shard_map/ppermute | solution.py:365
  31.2 2.9 %collective-permute-done.4.refs_6_ = f32[32,1792]{1,0:T(8,128)S(1)} collective-permute-done((f32[32,1792]{1,0:T(8,128)S(1)}, f32[32,1792]{1,0:T(8,128)S(1)}, u32[]{:S(2)}, u32[]{:S(2)}) %collective-permute-start.4) | collective-permute-done | bytes 229408 | tf_op jit(solution)/shard_map/ppermute | solution.py:365
  34.8 2.1 %collective-permute-start.6 = (f32[16,1792]{1,0:T(8,128)S(1)}, f32[16,1792]{1,0:T(8,128)S(1)}, u32[]{:S(2)}, u32[]{:S(2)}) collective-permute-start(f32[16,1792]{1,0:T(8,128)S(1)} %slice.21), channel_id=1, source_target_pairs={{0,224},{32,0},{64,32},{96,64},{128,96},{160,128},{192,160},{224,1... | collective-permute-start | bytes 344072 | tf_op jit(solution)/shard_map/ppermute | solution.py:365
  36.9 2.4 %maximum_select_fusion.refs_9_.chip_ref = f32[512,1792]{1,0:T(8,128)S(1)} fusion(f32[256,1792]{1,0:T(8,128)} %collective-permute-done.8, f32[256,1792]{1,0:T(8,128)S(1)} %convert_add_fusion.buffer_ref, pred[]{:T(512)S(6)} %eq.4), kind=kLoop, calls=%fused_computation | loop fusion | flops 2752512 | bytes 7340033 | tf_op jit(solution)/shard_map/jit(_where)/select_n | solution.py:397
  42.2 2.5 %left_product.1 = f32[256,512]{1,0:T(8,128)S(1)} custom-call(f32[32,1792]{1,0:T(8,128)S(1)} %copy-done.2, f32[32,1792]{1,0:T(8,128)S(1)} %collective-permute-done.refs_1_, f32[32,1792]{1,0:T(8,128)S(1)} %collective-permute-done.1.refs_2_, f32[32,1792]{1,0:T(8,128)S(1)} %collective-permute-done.2.refs_3_, f32[16,1792]{1,0:T(8,128)S(1)} %collective-permute-done.5.refs_4_, ...), custom_call_target="tpu_custom_call" | custom-call | flops 3000000000 | bytes 4194304 | tf_op jit(solution)/shard_map/left_product/pallas_call | solution.py:189
  44.7 15.8 %all_to_all.25 = f32[16,16,512]{2,1,0:T(8,128)S(1)} all-to-all(f32[16,16,512]{2,1,0:T(8,128)S(1)} %bitcast.18), channel_id=1, replica_groups=mesh['z'=8,'core'=2,'x'=4,'y'=4] {'x','y'}, dimensions={0} | all-to-all | bytes 1048576 | tf_op jit(solution)/shard_map/all_to_all | solution.py:404
  61.4 3.6 %all-to-all-start.1 = ((f32[16,16,512]{2,1,0:T(8,128)}), f32[16,16,512]{2,1,0:T(8,128)S(1)}, u32[]{:S(2)}, u32[]{:S(2)}) async-start(f32[16,16,512]{2,1,0:T(8,128)} %broadcast_in_dim.13), calls=%async_computation.1 | async-start | bytes 1048576 | tf_op jit(solution)/shard_map/all_to_all | solution.py:370
  65.0 8.8 %all-to-all-done.1 = f32[16,16,512]{2,1,0:T(8,128)S(1)} async-done(((f32[16,16,512]{2,1,0:T(8,128)}), f32[16,16,512]{2,1,0:T(8,128)S(1)}, u32[]{:S(2)}, u32[]{:S(2)}) %all-to-all-start.1) | async-done | bytes 524320 | tf_op jit(solution)/shard_map/all_to_all | solution.py:370
  74.0 4.5 %right_product.1 = f32[256,1792]{1,0:T(8,128)} custom-call(f32[256,512]{1,0:T(8,128)S(1)} %bitcast.19, f32[512,1792]{1,0:T(8,128)} %copy-done), custom_call_target="tpu_custom_call" | custom-call | flops 3000000000 | bytes 4194304 | tf_op jit(solution)/shard_map/right_product/pallas_call | solution.py:189
  78.6 4.5 %collective-permute-start.9 = (f32[8,32,512]{2,1,0:T(8,128)S(1)}, f32[8,32,512]{2,1,0:T(8,128)S(1)}, u32[]{:S(2)}, u32[]{:S(2)}) collective-permute-start(f32[8,32,512]{2,1,0:T(8,128)S(1)} %fusion), channel_id=1, source_target_pairs={{0,16},{16,0},{1,17},{17,1},{2,18},{18,2},{3,19},{19,3},{4,20},{20... | collective-permute-start | bytes 1572872 | tf_op jit(solution)/shard_map/ppermute | solution.py:365
  85.9 20.3 %all_to_all.26 = f32[8,16,512]{2,1,0:T(8,128)S(1)} all-to-all(f32[8,16,512]{2,1,0:T(8,128)S(1)} %broadcast_in_dim.14), channel_id=1, replica_groups=mesh['z'=8,'core'=2,'x'=4,'y'=4] {'z'}, dimensions={0} | all-to-all | bytes 524288 | tf_op jit(solution)/shard_map/all_to_all | solution.py:370
  106.3 11.8 %all_to_all.27 = f32[16,16,512]{2,1,0:T(8,128)S(1)} all-to-all(f32[16,16,512]{2,1,0:T(8,128)S(1)} %broadcast_in_dim.15), channel_id=1, replica_groups=mesh['z'=8,'core'=2,'x'=4,'y'=4] {'x','y'}, dimensions={0} | all-to-all | bytes 1048576 | tf_op jit(solution)/shard_map/all_to_all | solution.py:370
  118.0 3.5 %collective-permute-start.10 = (f32[256,512]{1,0:T(8,128)S(1)}, f32[256,512]{1,0:T(8,128)S(1)}, u32[]{:S(2)}, u32[]{:S(2)}) collective-permute-start(f32[256,512]{1,0:T(8,128)S(1)} %bitcast.25), channel_id=1, source_target_pairs={{0,16},{16,0},{1,17},{17,1},{2,18},{18,2},{3,19},{19,3},{4,20},{20... | collective-permute-start | bytes 1572872 | tf_op jit(solution)/shard_map/ppermute | solution.py:365
  124.9 21.9 %inverse_factor.1.inverse_ref = f32[512,512]{1,0:T(8,128)S(1)} custom-call(f32[512,512]{1,0:T(8,128)S(1)} %maximum_select_fusion.1._.gram, f32[32,1792]{1,0:T(8,128)} %copy_after.1.earlier), custom_call_target="tpu_custom_call" | custom-call | flops 30000001024 | bytes 2097152 | tf_op jit(solution)/shard_map/inverse_factor/pallas_call | solution.py:136
  148.7 19.0 %all-gather.2.cloned.1.call-done.product_ref = f32[512,1792]{1,0:T(8,128)} async-done(((f32[32,1792]{1,0:T(8,128)}), f32[512,1792]{1,0:T(8,128)}) %all-gather.2.cloned.1.call-update) | async-done | bytes 3670032 | tf_op jit(solution)/shard_map/all_gather | solution.py:424
  167.7 7.0 %right_and_squares.1 = (bf16[512,1792]{1,0:T(8,128)(2,1)}, bf16[512,1792]{1,0:T(8,128)(2,1)}, f32[8,512]{1,0:T(8,128)S(1)}) custom-call(f32[512,512]{1,0:T(8,128)S(1)} %inverse_factor.1.inverse_ref, f32[512,1792]{1,0:T(8,128)} %all-gather.2.cloned.1.call-done.product_ref), custom_call_target="tpu_custom_call" | custom-call | flops 3000000000 | bytes 4194304 | tf_op jit(solution)/shard_map/right_and_squares/pallas_call | solution.py:189
  175.3 6.3 %all-to-all-start.4 = ((f32[16,1,512]{2,1,0:T(1,128)}), f32[16,1,512]{2,1,0:T(1,128)S(1)}, u32[]{:S(2)}, u32[]{:S(2)}) async-start(f32[16,1,512]{2,1,0:T(1,128)} %broadcast_in_dim.34), calls=%async_computation.5 | async-start | bytes 65536 | tf_op jit(solution)/shard_map/all_to_all | solution.py:370
  181.7 4.8 %momentum_update.1 = f32[256,1792]{1,0:T(8,128)} custom-call(f32[256,1792]{1,0:T(8,128)} %copy-done.3, f32[256,512]{1,0:T(8,128)S(1)} %fusion.1.ortho_ref, bf16[512,1792]{1,0:T(8,128)(2,1)} %get-tuple-element.8.right_high, bf16[512,1792]{1,0:T(8,128)(2,1)} %get-tuple-element.9.right_low), custom_call_target="tpu_custom_call" | custom-call | flops 3000000000 | bytes 4194304 | tf_op jit(solution)/shard_map/momentum_update/pallas_call | solution.py:189
  188.1 4.9 %weights_update.1 = (f32[256,1792]{1,0:T(8,128)}, f32[32,1792]{1,0:T(8,128)}) custom-call(s32[1]{0:T(128)} %bitcast.start_ref, f32[256,1792]{1,0:T(8,128)} %weights_ref.1, f32[256,512]{1,0:T(8,128)S(1)} %fusion.1.ortho_ref, bf16[512,1792]{1,0:T(8,128)(2,1)} %get-tuple-element.8.right_high, bf16[512,1792]{1,0:T(8,128)(2,1)} %get-tuple-element.9.right_low, ...), custom_call_target="tpu_custom_call" | custom-call | flops 3000000000 | bytes 4194304 | tf_op jit(solution)/shard_map/weights_update/pallas_call | solution.py:189
  (44 shorter events, 17.0 us)
Async XLA Ops:
  7.2 5.3 %copy-start.2 = (f32[32,1792]{1,0:T(8,128)S(1)}, f32[32,1792]{1,0:T(8,128)}, u32[]{:S(2)}) copy-start(f32[32,1792]{1,0:T(8,128)} %refs_0_.1) | copy-start | bytes 688132
  9.1 30.3 %copy-start.3 = (f32[256,1792]{1,0:T(8,128)}, f32[256,1792]{1,0:T(8,128)S(1)}, u32[]{:S(2)}) copy-start(f32[256,1792]{1,0:T(8,128)S(1)} %convert_add_fusion.buffer_ref) | copy-start | bytes 5505028
  9.1 27.8 %collective-permute-start.8 = (f32[256,1792]{1,0:T(8,128)S(1)}, f32[256,1792]{1,0:T(8,128)}, u32[]{:S(2)}, u32[]{:S(2)}) collective-permute-start(f32[256,1792]{1,0:T(8,128)S(1)} %convert_add_fusion.buffer_ref), channel_id=1, source_target_pairs={{0,16},{16,0},{1,17},{17,1},{2,18},{18,2},{3,19},{19,3},{4,20},{20... | collective-permute-start | bytes 5505032 | tf_op jit(solution)/shard_map/ppermute | solution.py:365
  12.4 11.7 %collective-permute-start.3 = (f32[32,1792]{1,0:T(8,128)S(1)}, f32[32,1792]{1,0:T(8,128)S(1)}, u32[]{:S(2)}, u32[]{:S(2)}) collective-permute-start(f32[32,1792]{1,0:T(8,128)S(1)} %copy-done.2), channel_id=1, source_target_pairs={{0,64},{32,96},{64,128},{96,160},{128,192},{160,224},{192,0},{224,... | collective-permute-start | bytes 688136 | tf_op jit(solution)/shard_map/ppermute | solution.py:365
  13.7 14.8 %collective-permute-start.1 = (f32[32,1792]{1,0:T(8,128)S(1)}, f32[32,1792]{1,0:T(8,128)S(1)}, u32[]{:S(2)}, u32[]{:S(2)}) collective-permute-start(f32[32,1792]{1,0:T(8,128)S(1)} %copy-done.2), channel_id=1, source_target_pairs={{0,192},{32,224},{64,0},{96,32},{128,64},{160,96},{192,128},{224,1... | collective-permute-start | bytes 688136 | tf_op jit(solution)/shard_map/ppermute | solution.py:365
  24.2 9.9 %collective-permute-start.4 = (f32[32,1792]{1,0:T(8,128)S(1)}, f32[32,1792]{1,0:T(8,128)S(1)}, u32[]{:S(2)}, u32[]{:S(2)}) collective-permute-start(f32[32,1792]{1,0:T(8,128)S(1)} %collective-permute-done.3.refs_7_), channel_id=1, source_target_pairs={{0,32},{32,64},{64,96},{96,128},{128,160},{160,192},{192,224},{224... | collective-permute-start | bytes 688136 | tf_op jit(solution)/shard_map/ppermute | solution.py:365
  28.5 6.3 %collective-permute-start.2 = (f32[32,1792]{1,0:T(8,128)S(1)}, f32[32,1792]{1,0:T(8,128)S(1)}, u32[]{:S(2)}, u32[]{:S(2)}) collective-permute-start(f32[32,1792]{1,0:T(8,128)S(1)} %collective-permute-done.1.refs_2_), channel_id=1, source_target_pairs={{0,224},{32,0},{64,32},{96,64},{128,96},{160,128},{192,160},{224,1... | collective-permute-start | bytes 688136 | tf_op jit(solution)/shard_map/ppermute | solution.py:365
  29.0 10.7 %collective-permute-start = (f32[32,1792]{1,0:T(8,128)S(1)}, f32[32,1792]{1,0:T(8,128)S(1)}, u32[]{:S(2)}, u32[]{:S(2)}) collective-permute-start(f32[32,1792]{1,0:T(8,128)S(1)} %copy-done.2), channel_id=1, source_target_pairs={{0,224},{32,0},{64,32},{96,64},{128,96},{160,128},{192,160},{224,1... | collective-permute-start | bytes 688136 | tf_op jit(solution)/shard_map/ppermute | solution.py:365
  31.2 8.5 %collective-permute-start.7 = (f32[32,1792]{1,0:T(8,128)S(1)}, f32[32,1792]{1,0:T(8,128)S(1)}, u32[]{:S(2)}, u32[]{:S(2)}) collective-permute-start(f32[32,1792]{1,0:T(8,128)S(1)} %copy-done.2), channel_id=1, source_target_pairs={{0,32},{32,64},{64,96},{96,128},{128,160},{160,192},{192,224},{224... | collective-permute-start | bytes 688136 | tf_op jit(solution)/shard_map/ppermute | solution.py:365
  34.1 6.5 %collective-permute-start.5 = (f32[16,1792]{1,0:T(8,128)S(1)}, f32[16,1792]{1,0:T(8,128)S(1)}, u32[]{:S(2)}, u32[]{:S(2)}) collective-permute-start(f32[16,1792]{1,0:T(8,128)S(1)} %slice.20), channel_id=1, source_target_pairs={{0,32},{32,64},{64,96},{96,128},{128,160},{160,192},{192,224},{224... | collective-permute-start | bytes 344072 | tf_op jit(solution)/shard_map/ppermute | solution.py:365
  34.8 7.3 %collective-permute-start.6 = (f32[16,1792]{1,0:T(8,128)S(1)}, f32[16,1792]{1,0:T(8,128)S(1)}, u32[]{:S(2)}, u32[]{:S(2)}) collective-permute-start(f32[16,1792]{1,0:T(8,128)S(1)} %slice.21), channel_id=1, source_target_pairs={{0,224},{32,0},{64,32},{96,64},{128,96},{160,128},{192,160},{224,1... | collective-permute-start | bytes 344072 | tf_op jit(solution)/shard_map/ppermute | solution.py:365
  39.4 5.3 %copy-start = (f32[512,1792]{1,0:T(8,128)}, f32[512,1792]{1,0:T(8,128)S(1)}, u32[]{:S(2)}) copy-start(f32[512,1792]{1,0:T(8,128)S(1)} %maximum_select_fusion.refs_9_.chip_ref) | copy-start | bytes 11010052
  61.4 12.5 %all-to-all-start.1 = ((f32[16,16,512]{2,1,0:T(8,128)}), f32[16,16,512]{2,1,0:T(8,128)S(1)}, u32[]{:S(2)}, u32[]{:S(2)}) async-start(f32[16,16,512]{2,1,0:T(8,128)} %broadcast_in_dim.13), calls=%async_computation.1 | async-start | bytes 1048576 | tf_op jit(solution)/shard_map/all_to_all | solution.py:370
  65.0 58.2 %reduce-scatter.2.cloned.1.call-start = ((), (), s32[]{:S(2)}) async-start(), calls=%async_computation.6 | async-start | bytes 2064384 | tf_op jit(solution)/shard_map/reduce_scatter | solution.py:409
  78.6 89.2 %all-gather.2.cloned.1.call-start = ((), (), s32[]{:S(2)}) async-start(), calls=%async_computation.7 | async-start | bytes 3899392 | tf_op jit(solution)/shard_map/all_gather | solution.py:424
  78.6 6.0 %collective-permute-start.9 = (f32[8,32,512]{2,1,0:T(8,128)S(1)}, f32[8,32,512]{2,1,0:T(8,128)S(1)}, u32[]{:S(2)}, u32[]{:S(2)}) collective-permute-start(f32[8,32,512]{2,1,0:T(8,128)S(1)} %fusion), channel_id=1, source_target_pairs={{0,16},{16,0},{1,17},{17,1},{2,18},{18,2},{3,19},{19,3},{4,20},{20... | collective-permute-start | bytes 1572872 | tf_op jit(solution)/shard_map/ppermute | solution.py:365
  118.0 5.0 %collective-permute-start.10 = (f32[256,512]{1,0:T(8,128)S(1)}, f32[256,512]{1,0:T(8,128)S(1)}, u32[]{:S(2)}, u32[]{:S(2)}) collective-permute-start(f32[256,512]{1,0:T(8,128)S(1)} %bitcast.25), channel_id=1, source_target_pairs={{0,16},{16,0},{1,17},{17,1},{2,18},{18,2},{3,19},{19,3},{4,20},{20... | collective-permute-start | bytes 1572872 | tf_op jit(solution)/shard_map/ppermute | solution.py:365
  123.2 0.9 copy-start.1
  175.3 12.8 %all-to-all-start.4 = ((f32[16,1,512]{2,1,0:T(1,128)}), f32[16,1,512]{2,1,0:T(1,128)S(1)}, u32[]{:S(2)}, u32[]{:S(2)}) async-start(f32[16,1,512]{2,1,0:T(1,128)} %broadcast_in_dim.34), calls=%async_computation.5 | async-start | bytes 65536 | tf_op jit(solution)/shard_map/all_to_all | solution.py:370
Sparse Core Ops, SparseCore 0:
  78.7 42.1 reduce-scatter.1
  125.0 42.6 all-gather.1

commit v4 on v3

--- a/solution.py
+++ b/solution.py
@@ -92,7 +92,7 @@
             state[after + 8 :, :] = state[after + 8 :, :] - update[after + 8 :, :]
 
 
-def inverse_factor_kernel(gram, earlier, inverse, rest, state, tile):
+def inverse_factor_kernel(gram, earlier, result, inverse, rest, state, tile):
     rows = lax.broadcasted_iota(jnp.int32, (R, R), 0)
     columns = lax.broadcasted_iota(jnp.int32, (R, R), 1)
     rest[...] = gram[...]
@@ -130,6 +130,13 @@
             def _():
                 eliminate(done)
 
+    share = R // (2 * Z)
+    core, chip, place = columns // (R // 2), columns // share % Z, columns % share
+    chosen = jnp.where(rows == (2 * chip + core) * share + place, 1.0, 0.0).astype(jnp.bfloat16)
+    parts = [part.astype(jnp.bfloat16) for part in split_three(inverse[...])]
+    high, middle, low = (jnp.dot(part, chosen, preferred_element_type=F32) for part in parts)
+    result[...] = high + (middle + low)
+
 
 def inverse_factor(gram, earlier):
     whole = pl.BlockSpec(memory_space=pltpu.VMEM)
@@ -140,6 +147,7 @@
         out_specs=whole,
         scratch_shapes=[
             pltpu.VMEM((R, R), F32),
+            pltpu.VMEM((R, R), F32),
             pltpu.VMEM((TILE, 2 * TILE), F32),
             pltpu.VMEM((TILE, TILE), F32),
         ],
@@ -155,11 +163,11 @@
         copy.start()
         copy.wait()
 
-    there = pl.BlockSpec(memory_space=pl.ANY)
+    there = pl.BlockSpec(memory_space=pltpu.HBM)
     return pl.pallas_call(
         kernel,
         out_shape=jax.ShapeDtypeStruct(values.shape, values.dtype),
-        in_specs=[there, there],
+        in_specs=[there, pl.BlockSpec(memory_space=pl.ANY)],
         out_specs=there,
         scratch_shapes=[pltpu.SemaphoreType.DMA],
         compiler_params=pltpu.CompilerParams(vmem_limit_bytes=LIMIT),
@@ -245,7 +253,7 @@
         def _():
             high[...], low[...] = split_two(left_ref[...])
 
-        out[...] = product3((high[...], low[...]), split_two(chip_ref[...]), NN)
+        out[...] = product3((high[...], low[...]), split_two(chip_ref[...]), NN).T
 
     half = pltpu.VMEM((ranks, rows), jnp.bfloat16)
     return call(
@@ -253,71 +261,85 @@
         columns // WIDTH,
         (left, chip),
         [whole(ranks, rows), wide(rows)],
-        jax.ShapeDtypeStruct((ranks, columns), F32),
-        wide(ranks),
+        jax.ShapeDtypeStruct((columns, ranks), F32),
+        pl.BlockSpec((WIDTH, ranks), lambda j: (j, 0)),
         (half, half),
         name="right_product",
     )
 
 
-def right_and_squares(inverse, product):
-    columns = product.shape[1]
-    steps = columns // WIDTH
-
-    def kernel(inverse_ref, product_ref, out_high, out_low, sums, high, low, total):
-        j = pl.program_id(0)
-
-        @pl.when(j == 0)
-        def _():
-            high[...], low[...] = split_two(inverse_ref[...])
-            total[...] = jnp.zeros_like(total)
-
-        right = product3((high[...], low[...]), split_two(product_ref[...]), NN)
-        out_high[...], out_low[...] = split_two(right)
-        squares = right * right
-        total[...] += sum(squares[:, i : i + 128] for i in range(0, WIDTH, 128))
-
-        @pl.when(j == steps - 1)
-        def _():
-            sums[...] = lax.dot_general(
-                jnp.ones((8, 128), F32), total[...], (NT, ((), ())), precision=HIGHEST, preferred_element_type=F32
-            )
-
-    half = pltpu.VMEM((R, R), jnp.bfloat16)
-    pair = jax.ShapeDtypeStruct((R, columns), jnp.bfloat16)
-    return call(
-        kernel,
-        steps,
-        (inverse, product),
-        [whole(R, R), wide(R)],
-        (pair, pair, jax.ShapeDtypeStruct((8, R), F32)),
-        (wide(R), wide(R), whole(8, R)),
-        (half, half, pltpu.VMEM((R, 128), F32)),
-        name="right_and_squares",
-    )
-
-
-def momentum_update(buffer, ortho, right):
+def column_squares(inverse, own, other, core):
+    def kernel(core_ref, inverse_ref, own_ref, other_ref, sums):
+        mine = core_ref[0] == 0
+        first = jnp.where(mine, own_ref[...], other_ref[...])
+        second = jnp.where(mine, other_ref[...], own_ref[...])
+        product = jnp.concatenate([first, second], 1)
+        right = product3(split_two(product), split_two(inverse_ref[...]), NT)
+        sums[...] = jnp.broadcast_to(jnp.sum(right * right, axis=0, keepdims=True), sums.shape)
+
+    vmem = pl.BlockSpec(memory_space=pltpu.VMEM)
+    return pl.pallas_call(
+        kernel,
+        out_shape=jax.ShapeDtypeStruct((Z, 1, R), F32),
+        in_specs=[pl.BlockSpec(memory_space=pltpu.SMEM), vmem, vmem, vmem],
+        out_specs=vmem,
+        compiler_params=pltpu.CompilerParams(vmem_limit_bytes=16 * 2**20),
+        cost_estimate=pl.CostEstimate(flops=10**9, bytes_accessed=2**20, transcendentals=0),
+        name="column_squares",
+    )(core, inverse, own, other)
+
+
+def total_after(sums, earlier):
+    def kernel(sums_ref, _, out):
+        out[...] = jnp.broadcast_to(jnp.sum(sums_ref[...], axis=0, keepdims=True), out.shape)
+
+    vmem = pl.BlockSpec(memory_space=pltpu.VMEM)
+    return pl.pallas_call(
+        kernel,
+        out_shape=jax.ShapeDtypeStruct((XY, 1, R), F32),
+        in_specs=[vmem, pl.BlockSpec(memory_space=pl.ANY)],
+        out_specs=vmem,
+        compiler_params=pltpu.CompilerParams(vmem_limit_bytes=LIMIT),
+        cost_estimate=pl.CostEstimate(flops=1, bytes_accessed=2**16, transcendentals=0),
+        name="total_after",
+    )(sums, earlier)
+
+
+def momentum_update(buffer, ortho, inverse, product):
     rows, columns = buffer.shape
-
-    def kernel(buffer_ref, ortho_ref, right_high, right_low, out, high, low):
+    count = WIDTH // product.shape[2]
+
+    def kernel(buffer_ref, ortho_ref, inverse_ref, product_ref, out, out_high, out_low, *halves):
+        left, inner = halves[:2], halves[2:]
+
         @pl.when(pl.program_id(0) == 0)
         def _():
-            high[...], low[...] = split_two(ortho_ref[...])
-
-        out[...] = buffer_ref[...] - decay_keep * product3(
-            (high[...], low[...]), (right_high[...], right_low[...]), NN
-        )
-
-    half = pltpu.VMEM((rows, R), jnp.bfloat16)
+            left[0][...], left[1][...] = split_two(ortho_ref[...])
+            inner[0][...], inner[1][...] = split_two(inverse_ref[...])
+
+        ranks = product.shape[3]
+        block = jnp.concatenate([product_ref[:, c].reshape(WIDTH, ranks) for c in range(2)], 1)
+        right = product3(split_two(block), (inner[0][...], inner[1][...]), NT)
+        high, low = split_two(right)
+        out_high[...], out_low[...] = high, low
+        out[...] = buffer_ref[...] - decay_keep * product3((left[0][...], left[1][...]), (high, low), NT)
+
+    half, square = pltpu.VMEM((rows, R), jnp.bfloat16), pltpu.VMEM((R, R), jnp.bfloat16)
+    pair = jax.ShapeDtypeStruct((columns, R), jnp.bfloat16)
+    tall = pl.BlockSpec((WIDTH, R), lambda j: (j, 0))
     return call(
         kernel,
         columns // WIDTH,
-        (buffer, ortho, *right),
-        [wide(rows), whole(rows, R), wide(R), wide(R)],
-        jax.ShapeDtypeStruct((rows, columns), F32),
-        wide(rows),
-        (half, half),
+        (buffer, ortho, inverse, product),
+        [
+            wide(rows),
+            whole(rows, R),
+            whole(R, R),
+            pl.BlockSpec((count, *product.shape[1:]), lambda j: (j, 0, 0, 0)),
+        ],
+        (jax.ShapeDtypeStruct((rows, columns), F32), pair, pair),
+        (wide(rows), tall, tall),
+        (half, half, square, square),
         name="momentum_update",
     )
 
@@ -326,33 +348,34 @@
     rows, columns = weights.shape
     count = sums.shape[0]
 
-    def kernel(start_ref, weights_ref, ortho_ref, right_high, right_low, sums_ref, out, own, high, low, own_scale):
-        at = pl.multiple_of(start_ref[0], share)
-
+    def kernel(start_ref, weights_ref, ortho_ref, right_high, right_low, sums_ref, out, own, high, low, chosen, own_scale):
         @pl.when(pl.program_id(0) == 0)
         def _():
-            scale = jnp.sqrt(jnp.sum(sums_ref[...], axis=0, keepdims=True) / N + eps_norm)
+            scale = jnp.sqrt(jnp.sum(sums_ref[...], axis=0) / N + eps_norm)
             high[...], low[...] = split_two(ortho_ref[...] / scale)
             lanes = lax.broadcasted_iota(jnp.int32, (share, R), 1)
-            chosen = lanes == at + lax.broadcasted_iota(jnp.int32, (share, R), 0)
-            picked = jnp.sum(jnp.where(chosen, jnp.broadcast_to(scale, (share, R)), 0.0), axis=1, keepdims=True)
+            mine = lanes == start_ref[0] + lax.broadcasted_iota(jnp.int32, (share, R), 0)
+            chosen[...] = jnp.where(mine, 1.0, 0.0).astype(jnp.bfloat16)
+            picked = jnp.sum(jnp.where(mine, jnp.broadcast_to(scale, (share, R)), 0.0), axis=1, keepdims=True)
             own_scale[...] = jnp.broadcast_to(picked, own_scale.shape)
 
-        out[...] = weights_ref[...] - step_size * product3(
-            (high[...], low[...]), (right_high[...], right_low[...]), NN
+        right = right_high[...], right_low[...]
+        out[...] = weights_ref[...] - step_size * product3((high[...], low[...]), right, NT)
+        rows_high, rows_low = (
+            lax.dot_general(chosen[...], one, (NT, ((), ())), preferred_element_type=F32) for one in right
         )
-        here = pl.ds(at, share)
-        own[...] = (right_high[here, :].astype(F32) + right_low[here, :].astype(F32)) / own_scale[...]
+        own[...] = (rows_high + rows_low) / own_scale[...]
 
     half = pltpu.VMEM((rows, R), jnp.bfloat16)
+    tall = pl.BlockSpec((WIDTH, R), lambda j: (j, 0))
     return call(
         kernel,
         columns // WIDTH,
         (start, weights, ortho, *right, sums),
-        [pl.BlockSpec(memory_space=pltpu.SMEM), wide(rows), whole(rows, R), wide(R), wide(R), whole(count, R)],
+        [pl.BlockSpec(memory_space=pltpu.SMEM), wide(rows), whole(rows, R), tall, tall, whole(count, 1, R)],
         (jax.ShapeDtypeStruct((rows, columns), F32), jax.ShapeDtypeStruct((share, columns), F32)),
         (wide(rows), wide(share)),
-        (half, half, pltpu.VMEM((share, WIDTH), F32)),
+        (half, half, pltpu.VMEM((share, R), jnp.bfloat16), pltpu.VMEM((share, WIDTH), F32)),
         name="weights_update",
     )
 
@@ -375,7 +398,7 @@
     below1, above1 = shift(own, "z", 1), shift(own, "z", -1)
     below2, above2 = shift(own, "z", 2), shift(own, "z", -2)
     below3, above3 = shift(below2, "z", 1), shift(above2, "z", -1)
-    across = (shift(below3[:half], "z", 1), shift(above3[half:], "z", -1))
+    across = (shift(below2[:half], "z", 2), shift(above2[half:], "z", -2))
     return [own, above1, above2, above3, across, below3, below2, below1]
 
 
@@ -409,8 +432,8 @@
     product = lax.psum_scatter(product, "z", scatter_dimension=0, tiled=True)
 
     other = shift(own, "core", 1)
-    left_all = jnp.stack([jnp.where(core == 0, own, other), jnp.where(core == 0, other, own)], 1)
-    left_all = left_all.reshape(R, rows)
+    by_core = [jnp.where(core == 0, own, other), jnp.where(core == 0, other, own)]
+    left_all = jnp.stack(by_core, 1).reshape(R, rows)
     height = R // (2 * XY)
     mine = lax.dynamic_slice_in_dim(left_all, (core * XY + plane) * height, height, 0)
     gram = jnp.sum(spread(dot(mine, left_all, ((1,), (1,)), HIGHEST), "z", Z), 0)
@@ -421,15 +444,20 @@
     )
     product = copy_after(product, gram)
     inverse = inverse_factor(gram, product)
+
+    beside = shift(product, "core", 1)
+    sums = column_squares(inverse, product, beside, jnp.full((1,), core, jnp.int32))
+    sums = lax.all_to_all(sums, "z", 0, 0, tiled=True)
     product = lax.all_gather(product, ("z", "core"), axis=0, tiled=True)
+    product = product.reshape(Z, 2, -1, product.shape[1])
 
     height = rows // 2
-    left_own = jnp.where(core == 0, left_all[:, :height], left_all[:, height:])
+    left_own = jnp.concatenate(by_core, 0).reshape(R, rows)
+    left_own = jnp.where(core == 0, left_own[:, :height], left_own[:, height:])
     ortho = dot(left_own, inverse, ((0,), (1,)), HIGHEST)
-    *right_t, sums = right_and_squares(inverse, product)
-    sums = spread(sums[:1], ("x", "y"), XY).reshape(XY, R)
+    sums = lax.all_to_all(total_after(sums, product), ("x", "y"), 0, 0, tiled=True)
+    new_momentum, *right_t = momentum_update(buffer, ortho, inverse, product)
     start = jnp.full((1,), (2 * z + core) * share, jnp.int32)
-    new_momentum = momentum_update(buffer, ortho, right_t)
     new_weights, new_right = weights_update(weights, ortho, right_t, sums, start, share)
     return (new_weights, new_momentum, new_right)
 

time: 200 us -> 195 us (0.975)
  waiting for transfers between devices: 46.1 us -> 32.8 us
  starting transfers between devices: 35.1 us -> 44.4 us
    all_gather x1, waiting for transfers between devices: 19 us -> 2.97 us  [local(): product = lax.all_gather(product, ('z', 'core'), axis=0, tiled=True)]
    all_to_all x0 -> x2, starting transfers between devices: none -> 12.1 us  [the longest x1 6.4 us: local(): lax.all_to_all(total_after(sums, product), ('x', 'y'), 0, 0, tiled=True)]
    all_to_all x2 -> x1, starting transfers between devices: 9.91 us -> 4.36 us  [spread(): return lax.all_to_all(whole, axes, 0, 0, tiled=True)]
    all_to_all x0 -> x2, waiting for transfers between devices: none -> 4.85 us  [the longest x1 4.84 us: local(): sums = lax.all_to_all(sums, 'z', 0, 0, tiled=True)]
    pallas_call x0 -> x2, Pallas kernels: none -> 2.86 us  [the longest x1 2.22 us: column_squares(): pl.pallas_call(kernel, out_shape=jax.ShapeDtypeStruct((Z, 1, R), F32), in...]
    pallas_call x5 -> x4, Pallas kernels: 23.7 us -> 20.9 us  [call(): pl.pallas_call(kernel, grid=(steps,), out_shape=outs, in_specs=specs, out...]
    ppermute x11 -> x12, starting transfers between devices: 25.1 us -> 27.8 us  [shift(): lax.ppermute(values, axis, [(i, (i + by) % size) for i in range(size)])]
    all_to_all x2 -> x1, waiting for transfers between devices: 10.5 us -> 9.17 us  [spread(): return lax.all_to_all(whole, axes, 0, 0, tiled=True)]
  transfers between devices with their start and end apart: 15 -> 17, of which waited for: 11 -> 11; matrix products, arithmetic and copies ran while one was open for 3% -> 3% of each run, Pallas kernels for 13% -> 17%
where the time goes in v4:
time: 195 us
  Pallas kernels  47.4 us (24%)
  blocking collectives  46.3 us (24%)
  starting transfers between devices  44.4 us (23%)
  waiting for transfers between devices  32.8 us (17%)
  between operations  14.3 us (7%)
  other arithmetic  4.98 us (3%)
  matrix products  2.84 us (1%)
    all_to_all x2, blocking collectives, spread(): return lax.all_to_all(whole, axes, 0, 0, tiled=True)  30.7 us
    ppermute x12, starting transfers between devices, shift(): lax.ppermute(values, axis, [(i, (i + by) % size) for i in range(size)])  27.8 us
    pallas_call x1, Pallas kernels, inverse_factor(): pl.pallas_call(inverse_factor_kernel, out_shape=jax.ShapeDtypeStruct((R,...  23 us
    pallas_call x4, Pallas kernels, call(): pl.pallas_call(kernel, grid=(steps,), out_shape=outs, in_specs=specs, out...  20.9 us
    ppermute x12, waiting for transfers between devices, shift(): lax.ppermute(values, axis, [(i, (i + by) % size) for i in range(size)])  15.8 us
    all_to_all x1, blocking collectives, local(): lax.all_to_all(part.reshape(XY, -1, rows), ('x', 'y'), 0, 0, tiled=True)  15.6 us
    all_to_all x1, waiting for transfers between devices, spread(): return lax.all_to_all(whole, axes, 0, 0, tiled=True)  9.17 us
    all_to_all x1, starting transfers between devices, local(): lax.all_to_all(total_after(sums, product), ('x', 'y'), 0, 0, tiled=True)  6.4 us
  transfers between devices with their start and end apart: 17, of which 11 were waited for; matrix products, arithmetic and copies ran while one was open for 3% of the time, Pallas kernels for 17%

profile of v4, /device:TPU:1, one launch (start us, length us, event | category | flops | bytes accessed | tf_op | source)
XLA Modules:
  0.0 194.9 jit_solution(14092156075682045445)
XLA Ops:
  9.1 3.3 %collective-permute-start.8 = (f32[256,1792]{1,0:T(8,128)S(1)}, f32[256,1792]{1,0:T(8,128)}, u32[]{:S(2)}, u32[]{:S(2)}) collective-permute-start(f32[256,1792]{1,0:T(8,128)S(1)} %convert_add_fusion.buffer_ref), channel_id=1, source_target_pairs={{0,16},{16,0},{1,17},{17,1},{2,18},{18,2},{3,19},{19,3},{4,20},{20... | collective-permute-start | bytes 5505032 | tf_op jit(solution)/shard_map/ppermute | solution.py:388
  13.7 3.0 %collective-permute-start.1 = (f32[32,1792]{1,0:T(8,128)S(1)}, f32[32,1792]{1,0:T(8,128)S(1)}, u32[]{:S(2)}, u32[]{:S(2)}) collective-permute-start(f32[32,1792]{1,0:T(8,128)S(1)} %copy-done.2), channel_id=1, source_target_pairs={{0,192},{32,224},{64,0},{96,32},{128,64},{160,96},{192,128},{224,1... | collective-permute-start | bytes 688136 | tf_op jit(solution)/shard_map/ppermute | solution.py:388
  18.7 5.5 %collective-permute-done.3.refs_7_ = f32[32,1792]{1,0:T(8,128)S(1)} collective-permute-done((f32[32,1792]{1,0:T(8,128)S(1)}, f32[32,1792]{1,0:T(8,128)S(1)}, u32[]{:S(2)}, u32[]{:S(2)}) %collective-permute-start.3) | collective-permute-done | bytes 229408 | tf_op jit(solution)/shard_map/ppermute | solution.py:388
  24.2 3.7 %collective-permute-start.4 = (f32[16,1792]{1,0:T(8,128)S(1)}, f32[16,1792]{1,0:T(8,128)S(1)}, u32[]{:S(2)}, u32[]{:S(2)}) collective-permute-start(f32[16,1792]{1,0:T(8,128)S(1)} %slice.16), channel_id=1, source_target_pairs={{0,64},{32,96},{64,128},{96,160},{128,192},{160,224},{192,0},{224,... | collective-permute-start | bytes 344072 | tf_op jit(solution)/shard_map/ppermute | solution.py:388
  28.6 2.4 %collective-permute-start.5 = (f32[16,1792]{1,0:T(8,128)S(1)}, f32[16,1792]{1,0:T(8,128)S(1)}, u32[]{:S(2)}, u32[]{:S(2)}) collective-permute-start(f32[16,1792]{1,0:T(8,128)S(1)} %slice.17), channel_id=1, source_target_pairs={{0,192},{32,224},{64,0},{96,32},{128,64},{160,96},{192,128},{224,1... | collective-permute-start | bytes 344072 | tf_op jit(solution)/shard_map/ppermute | solution.py:388
  35.6 2.4 %maximum_select_fusion.refs_9_.chip_ref = f32[512,1792]{1,0:T(8,128)S(1)} fusion(f32[256,1792]{1,0:T(8,128)} %collective-permute-done.8, f32[256,1792]{1,0:T(8,128)S(1)} %convert_add_fusion.buffer_ref, pred[]{:T(512)S(6)} %eq.4), kind=kLoop, calls=%fused_computation | loop fusion | flops 2752512 | bytes 7340033 | tf_op jit(solution)/shard_map/jit(_where)/select_n | solution.py:420
  38.3 2.7 %collective-permute-done.6.refs_6_ = f32[32,1792]{1,0:T(8,128)S(1)} collective-permute-done((f32[32,1792]{1,0:T(8,128)S(1)}, f32[32,1792]{1,0:T(8,128)S(1)}, u32[]{:S(2)}, u32[]{:S(2)}) %collective-permute-start.6) | collective-permute-done | bytes 229408 | tf_op jit(solution)/shard_map/ppermute | solution.py:388
  42.6 2.5 %left_product.1 = f32[256,512]{1,0:T(8,128)S(1)} custom-call(f32[32,1792]{1,0:T(8,128)S(1)} %copy-done.2, f32[32,1792]{1,0:T(8,128)S(1)} %collective-permute-done.refs_1_, f32[32,1792]{1,0:T(8,128)S(1)} %collective-permute-done.1.refs_2_, f32[32,1792]{1,0:T(8,128)S(1)} %collective-permute-done.2.refs_3_, f32[16,1792]{1,0:T(8,128)S(1)} %collective-permute-done.4.refs_4_, ...), custom_call_target="tpu_custom_call" | custom-call | flops 3000000000 | bytes 4194304 | tf_op jit(solution)/shard_map/left_product/pallas_call | solution.py:197
  45.2 15.6 %all_to_all.30 = f32[16,16,512]{2,1,0:T(8,128)S(1)} all-to-all(f32[16,16,512]{2,1,0:T(8,128)S(1)} %bitcast.15), channel_id=1, replica_groups=mesh['z'=8,'core'=2,'x'=4,'y'=4] {'x','y'}, dimensions={0} | all-to-all | bytes 1048576 | tf_op jit(solution)/shard_map/all_to_all | solution.py:427
  61.6 4.4 %all-to-all-start.1 = ((f32[16,16,512]{2,1,0:T(8,128)}), f32[16,16,512]{2,1,0:T(8,128)S(1)}, u32[]{:S(2)}, u32[]{:S(2)}) async-start(f32[16,16,512]{2,1,0:T(8,128)} %broadcast_in_dim.11), calls=%async_computation.1 | async-start | bytes 1048576 | tf_op jit(solution)/shard_map/all_to_all | solution.py:393
  66.1 9.2 %all-to-all-done.1 = f32[16,16,512]{2,1,0:T(8,128)S(1)} async-done(((f32[16,16,512]{2,1,0:T(8,128)}), f32[16,16,512]{2,1,0:T(8,128)S(1)}, u32[]{:S(2)}, u32[]{:S(2)}) %all-to-all-start.1) | async-done | bytes 524320 | tf_op jit(solution)/shard_map/all_to_all | solution.py:393
  75.4 4.7 %right_product.1 = f32[1792,256]{1,0:T(8,128)} custom-call(f32[256,512]{1,0:T(8,128)S(1)} %bitcast.16, f32[512,1792]{1,0:T(8,128)} %copy-done), custom_call_target="tpu_custom_call" | custom-call | flops 3000000000 | bytes 4194304 | tf_op jit(solution)/shard_map/right_product/pallas_call | solution.py:197
  80.2 3.6 %collective-permute-start.9 = (f32[8,32,512]{2,1,0:T(8,128)S(1)}, f32[8,32,512]{2,1,0:T(8,128)S(1)}, u32[]{:S(2)}, u32[]{:S(2)}) collective-permute-start(f32[8,32,512]{2,1,0:T(8,128)S(1)} %fusion), channel_id=1, source_target_pairs={{0,16},{16,0},{1,17},{17,1},{2,18},{18,2},{3,19},{19,3},{4,20},{20... | collective-permute-start | bytes 1572872 | tf_op jit(solution)/shard_map/ppermute | solution.py:388
  86.6 19.1 %all_to_all.31 = f32[8,16,512]{2,1,0:T(8,128)S(1)} all-to-all(f32[8,16,512]{2,1,0:T(8,128)S(1)} %broadcast_in_dim.12), channel_id=1, replica_groups=mesh['z'=8,'core'=2,'x'=4,'y'=4] {'z'}, dimensions={0} | all-to-all | bytes 524288 | tf_op jit(solution)/shard_map/all_to_all | solution.py:393
  105.8 11.6 %all_to_all.32 = f32[16,16,512]{2,1,0:T(8,128)S(1)} all-to-all(f32[16,16,512]{2,1,0:T(8,128)S(1)} %broadcast_in_dim.13), channel_id=1, replica_groups=mesh['z'=8,'core'=2,'x'=4,'y'=4] {'x','y'}, dimensions={0} | all-to-all | bytes 1048576 | tf_op jit(solution)/shard_map/all_to_all | solution.py:393
  117.4 3.5 %collective-permute-start.10 = (f32[256,512]{1,0:T(8,128)S(1)}, f32[256,512]{1,0:T(8,128)S(1)}, u32[]{:S(2)}, u32[]{:S(2)}) collective-permute-start(f32[256,512]{1,0:T(8,128)S(1)} %bitcast.25), channel_id=1, source_target_pairs={{0,16},{16,0},{1,17},{17,1},{2,18},{18,2},{3,19},{19,3},{4,20},{20... | collective-permute-start | bytes 1572872 | tf_op jit(solution)/shard_map/ppermute | solution.py:388
  124.3 2.4 %collective-permute-start.11 = (f32[224,256]{1,0:T(8,128)}, f32[224,256]{1,0:T(8,128)S(1)}, u32[]{:S(2)}, u32[]{:S(2)}) collective-permute-start(f32[224,256]{1,0:T(8,128)} %copy_after.1.earlier.own_ref), channel_id=1, source_target_pairs={{0,16},{16,0},{1,17},{17,1},{2,18},{18,2},{3,19},{19,3},{4,20},{20... | collective-permute-start | bytes 688136 | tf_op jit(solution)/shard_map/ppermute | solution.py:388
  126.8 23.0 %inverse_factor.1.inverse_ref = f32[512,512]{1,0:T(8,128)S(1)} custom-call(f32[512,512]{1,0:T(8,128)S(1)} %maximum_select_fusion.1._.gram, f32[224,256]{1,0:T(8,128)} %copy_after.1.earlier.own_ref), custom_call_target="tpu_custom_call" | custom-call | flops 30000001024 | bytes 2097152 | tf_op jit(solution)/shard_map/inverse_factor/pallas_call | solution.py:143
  152.0 5.7 %all-to-all-start.4 = ((f32[8,1,512]{2,1,0:T(1,128)}), f32[8,1,512]{2,1,0:T(1,128)S(1)}, u32[]{:S(2)}, u32[]{:S(2)}) async-start(f32[8,1,512]{2,1,0:T(1,128)} %column_squares.1), calls=%async_computation.5 | async-start | bytes 32768 | tf_op jit(solution)/shard_map/all_to_all | solution.py:450
  159.5 4.8 %all-to-all-done.4.sums_ref = f32[8,1,512]{2,1,0:T(1,128)S(1)} async-done(((f32[8,1,512]{2,1,0:T(1,128)}), f32[8,1,512]{2,1,0:T(1,128)S(1)}, u32[]{:S(2)}, u32[]{:S(2)}) %all-to-all-start.4) | async-done | bytes 16416 | tf_op jit(solution)/shard_map/all_to_all | solution.py:450
  164.4 3.0 %all-gather.2.cloned.1.call-done = f32[3584,256]{1,0:T(8,128)} async-done(((f32[224,256]{1,0:T(8,128)}), f32[3584,256]{1,0:T(8,128)}) %all-gather.2.cloned.1.call-update) | async-done | bytes 3670032 | tf_op jit(solution)/shard_map/all_gather | solution.py:451
  168.0 6.4 %all-to-all-start.5 = ((f32[16,1,512]{2,1,0:T(1,128)}), f32[16,1,512]{2,1,0:T(1,128)S(1)}, u32[]{:S(2)}, u32[]{:S(2)}) async-start(f32[16,1,512]{2,1,0:T(1,128)} %total_after.1), calls=%async_computation.6 | async-start | bytes 65536 | tf_op jit(solution)/shard_map/all_to_all | solution.py:458
  174.4 8.0 %momentum_update.1 = (f32[256,1792]{1,0:T(8,128)}, bf16[1792,512]{1,0:T(8,128)(2,1)}, bf16[1792,512]{1,0:T(8,128)(2,1)}) custom-call(f32[256,1792]{1,0:T(8,128)} %copy-done.3, f32[256,512]{1,0:T(8,128)S(1)} %fusion.1.ortho_ref, f32[512,512]{1,0:T(8,128)S(1)} %inverse_factor.1.inverse_ref, f32[8,2,224,256]{3,2,1,0:T(8,128)} %bitcast.23), custom_call_target="tpu_custom_call" | custom-call | flops 3000000000 | bytes 4194304 | tf_op jit(solution)/shard_map/momentum_update/pallas_call | solution.py:197
  182.4 5.7 %weights_update.1 = (f32[256,1792]{1,0:T(8,128)}, f32[32,1792]{1,0:T(8,128)}) custom-call(s32[1]{0:T(128)} %bitcast.start_ref, f32[256,1792]{1,0:T(8,128)} %weights_ref.1, f32[256,512]{1,0:T(8,128)S(1)} %fusion.1.ortho_ref, bf16[1792,512]{1,0:T(8,128)(2,1)} %get-tuple-element.8.right_high, bf16[1792,512]{1,0:T(8,128)(2,1)} %get-tuple-element.9.right_low, ...), custom_call_target="tpu_custom_call" | custom-call | flops 3000000000 | bytes 4194304 | tf_op jit(solution)/shard_map/weights_update/pallas_call | solution.py:197
  (47 shorter events, 24.4 us)
Async XLA Ops:
  7.2 5.3 %copy-start.2 = (f32[32,1792]{1,0:T(8,128)S(1)}, f32[32,1792]{1,0:T(8,128)}, u32[]{:S(2)}) copy-start(f32[32,1792]{1,0:T(8,128)} %refs_0_.1) | copy-start | bytes 688132
  9.1 28.9 %copy-start.3 = (f32[256,1792]{1,0:T(8,128)}, f32[256,1792]{1,0:T(8,128)S(1)}, u32[]{:S(2)}) copy-start(f32[256,1792]{1,0:T(8,128)S(1)} %convert_add_fusion.buffer_ref) | copy-start | bytes 5505028
  9.1 24.7 %collective-permute-start.8 = (f32[256,1792]{1,0:T(8,128)S(1)}, f32[256,1792]{1,0:T(8,128)}, u32[]{:S(2)}, u32[]{:S(2)}) collective-permute-start(f32[256,1792]{1,0:T(8,128)S(1)} %convert_add_fusion.buffer_ref), channel_id=1, source_target_pairs={{0,16},{16,0},{1,17},{17,1},{2,18},{18,2},{3,19},{19,3},{4,20},{20... | collective-permute-start | bytes 5505032 | tf_op jit(solution)/shard_map/ppermute | solution.py:388
  12.4 11.7 %collective-permute-start.3 = (f32[32,1792]{1,0:T(8,128)S(1)}, f32[32,1792]{1,0:T(8,128)S(1)}, u32[]{:S(2)}, u32[]{:S(2)}) collective-permute-start(f32[32,1792]{1,0:T(8,128)S(1)} %copy-done.2), channel_id=1, source_target_pairs={{0,64},{32,96},{64,128},{96,160},{128,192},{160,224},{192,0},{224,... | collective-permute-start | bytes 688136 | tf_op jit(solution)/shard_map/ppermute | solution.py:388
  13.7 14.9 %collective-permute-start.1 = (f32[32,1792]{1,0:T(8,128)S(1)}, f32[32,1792]{1,0:T(8,128)S(1)}, u32[]{:S(2)}, u32[]{:S(2)}) collective-permute-start(f32[32,1792]{1,0:T(8,128)S(1)} %copy-done.2), channel_id=1, source_target_pairs={{0,192},{32,224},{64,0},{96,32},{128,64},{160,96},{192,128},{224,1... | collective-permute-start | bytes 688136 | tf_op jit(solution)/shard_map/ppermute | solution.py:388
  16.7 16.2 %collective-permute-start = (f32[32,1792]{1,0:T(8,128)S(1)}, f32[32,1792]{1,0:T(8,128)S(1)}, u32[]{:S(2)}, u32[]{:S(2)}) collective-permute-start(f32[32,1792]{1,0:T(8,128)S(1)} %copy-done.2), channel_id=1, source_target_pairs={{0,224},{32,0},{64,32},{96,64},{128,96},{160,128},{192,160},{224,1... | collective-permute-start | bytes 688136 | tf_op jit(solution)/shard_map/ppermute | solution.py:388
  18.7 19.4 %collective-permute-start.7 = (f32[32,1792]{1,0:T(8,128)S(1)}, f32[32,1792]{1,0:T(8,128)S(1)}, u32[]{:S(2)}, u32[]{:S(2)}) collective-permute-start(f32[32,1792]{1,0:T(8,128)S(1)} %copy-done.2), channel_id=1, source_target_pairs={{0,32},{32,64},{64,96},{96,128},{128,160},{160,192},{192,224},{224... | collective-permute-start | bytes 688136 | tf_op jit(solution)/shard_map/ppermute | solution.py:388
  24.2 13.9 %collective-permute-start.4 = (f32[16,1792]{1,0:T(8,128)S(1)}, f32[16,1792]{1,0:T(8,128)S(1)}, u32[]{:S(2)}, u32[]{:S(2)}) collective-permute-start(f32[16,1792]{1,0:T(8,128)S(1)} %slice.16), channel_id=1, source_target_pairs={{0,64},{32,96},{64,128},{96,160},{128,192},{160,224},{192,0},{224,... | collective-permute-start | bytes 344072 | tf_op jit(solution)/shard_map/ppermute | solution.py:388
  28.6 9.7 %collective-permute-start.5 = (f32[16,1792]{1,0:T(8,128)S(1)}, f32[16,1792]{1,0:T(8,128)S(1)}, u32[]{:S(2)}, u32[]{:S(2)}) collective-permute-start(f32[16,1792]{1,0:T(8,128)S(1)} %slice.17), channel_id=1, source_target_pairs={{0,192},{32,224},{64,0},{96,32},{128,64},{160,96},{192,128},{224,1... | collective-permute-start | bytes 344072 | tf_op jit(solution)/shard_map/ppermute | solution.py:388
  33.0 8.0 %collective-permute-start.6 = (f32[32,1792]{1,0:T(8,128)S(1)}, f32[32,1792]{1,0:T(8,128)S(1)}, u32[]{:S(2)}, u32[]{:S(2)}) collective-permute-start(f32[32,1792]{1,0:T(8,128)S(1)} %collective-permute-done.3.refs_7_), channel_id=1, source_target_pairs={{0,32},{32,64},{64,96},{96,128},{128,160},{160,192},{192,224},{224... | collective-permute-start | bytes 688136 | tf_op jit(solution)/shard_map/ppermute | solution.py:388
  33.8 8.9 %collective-permute-start.2 = (f32[32,1792]{1,0:T(8,128)S(1)}, f32[32,1792]{1,0:T(8,128)S(1)}, u32[]{:S(2)}, u32[]{:S(2)}) collective-permute-start(f32[32,1792]{1,0:T(8,128)S(1)} %collective-permute-done.1.refs_2_), channel_id=1, source_target_pairs={{0,224},{32,0},{64,32},{96,64},{128,96},{160,128},{192,160},{224,1... | collective-permute-start | bytes 688136 | tf_op jit(solution)/shard_map/ppermute | solution.py:388
  38.1 7.1 %copy-start = (f32[512,1792]{1,0:T(8,128)}, f32[512,1792]{1,0:T(8,128)S(1)}, u32[]{:S(2)}) copy-start(f32[512,1792]{1,0:T(8,128)S(1)} %maximum_select_fusion.refs_9_.chip_ref) | copy-start | bytes 11010052
  61.6 13.6 %all-to-all-start.1 = ((f32[16,16,512]{2,1,0:T(8,128)}), f32[16,16,512]{2,1,0:T(8,128)S(1)}, u32[]{:S(2)}, u32[]{:S(2)}) async-start(f32[16,16,512]{2,1,0:T(8,128)} %broadcast_in_dim.11), calls=%async_computation.1 | async-start | bytes 1048576 | tf_op jit(solution)/shard_map/all_to_all | solution.py:393
  66.0 56.5 %reduce-scatter.2.cloned.1.call-start = ((), (), s32[]{:S(2)}) async-start(), calls=%async_computation.7 | async-start | bytes 2064384 | tf_op jit(solution)/shard_map/reduce_scatter | solution.py:432
  80.1 87.2 %all-gather.2.cloned.1.call-start = ((), (), s32[]{:S(2)}) async-start(), calls=%async_computation.8 | async-start | bytes 3899392 | tf_op jit(solution)/shard_map/all_gather | solution.py:451
  80.2 5.1 %collective-permute-start.9 = (f32[8,32,512]{2,1,0:T(8,128)S(1)}, f32[8,32,512]{2,1,0:T(8,128)S(1)}, u32[]{:S(2)}, u32[]{:S(2)}) collective-permute-start(f32[8,32,512]{2,1,0:T(8,128)S(1)} %fusion), channel_id=1, source_target_pairs={{0,16},{16,0},{1,17},{17,1},{2,18},{18,2},{3,19},{19,3},{4,20},{20... | collective-permute-start | bytes 1572872 | tf_op jit(solution)/shard_map/ppermute | solution.py:388
  117.4 5.0 %collective-permute-start.10 = (f32[256,512]{1,0:T(8,128)S(1)}, f32[256,512]{1,0:T(8,128)S(1)}, u32[]{:S(2)}, u32[]{:S(2)}) collective-permute-start(f32[256,512]{1,0:T(8,128)S(1)} %bitcast.25), channel_id=1, source_target_pairs={{0,16},{16,0},{1,17},{17,1},{2,18},{18,2},{3,19},{19,3},{4,20},{20... | collective-permute-start | bytes 1572872 | tf_op jit(solution)/shard_map/ppermute | solution.py:388
  122.6 0.9 copy-start.1
  124.3 25.4 %collective-permute-start.11 = (f32[224,256]{1,0:T(8,128)}, f32[224,256]{1,0:T(8,128)S(1)}, u32[]{:S(2)}, u32[]{:S(2)}) collective-permute-start(f32[224,256]{1,0:T(8,128)} %copy_after.1.earlier.own_ref), channel_id=1, source_target_pairs={{0,16},{16,0},{1,17},{17,1},{2,18},{18,2},{3,19},{19,3},{4,20},{20... | collective-permute-start | bytes 688136 | tf_op jit(solution)/shard_map/ppermute | solution.py:388
  152.0 12.4 %all-to-all-start.4 = ((f32[8,1,512]{2,1,0:T(1,128)}), f32[8,1,512]{2,1,0:T(1,128)S(1)}, u32[]{:S(2)}, u32[]{:S(2)}) async-start(f32[8,1,512]{2,1,0:T(1,128)} %column_squares.1), calls=%async_computation.5 | async-start | bytes 32768 | tf_op jit(solution)/shard_map/all_to_all | solution.py:450
  168.0 14.4 %all-to-all-start.5 = ((f32[16,1,512]{2,1,0:T(1,128)}), f32[16,1,512]{2,1,0:T(1,128)S(1)}, u32[]{:S(2)}, u32[]{:S(2)}) async-start(f32[16,1,512]{2,1,0:T(1,128)} %total_after.1), calls=%async_computation.6 | async-start | bytes 65536 | tf_op jit(solution)/shard_map/all_to_all | solution.py:458
Sparse Core Ops, SparseCore 0:
  80.3 39.9 reduce-scatter.1
  124.3 42.9 all-gather.1

commit v5 on v4

--- a/solution.py
+++ b/solution.py
@@ -157,23 +157,10 @@
     )(gram, earlier)
 
 
-def copy_after(values, earlier):
-    def kernel(values_ref, _, out, done):
-        copy = pltpu.make_async_copy(values_ref, out, done)
-        copy.start()
-        copy.wait()
-
-    there = pl.BlockSpec(memory_space=pltpu.HBM)
-    return pl.pallas_call(
-        kernel,
-        out_shape=jax.ShapeDtypeStruct(values.shape, values.dtype),
-        in_specs=[there, pl.BlockSpec(memory_space=pl.ANY)],
-        out_specs=there,
-        scratch_shapes=[pltpu.SemaphoreType.DMA],
-        compiler_params=pltpu.CompilerParams(vmem_limit_bytes=LIMIT),
-        cost_estimate=pl.CostEstimate(flops=1, bytes_accessed=2 * 4 * values.size, transcendentals=0),
-        name="copy_after",
-    )(values, earlier)
+def after(values, earlier):
+    tile = (slice(0, 8), slice(0, 128))
+    first = jnp.where(earlier[tile] == earlier[tile], values[tile], earlier[tile])
+    return lax.dynamic_update_slice(values, first, (0, 0))
 
 
 def split_two(values):
@@ -305,77 +292,76 @@
     )(sums, earlier)
 
 
-def momentum_update(buffer, ortho, inverse, product):
+def columns_first(product_ref):
+    count, _, share, ranks = product_ref.shape
+    return jnp.concatenate([product_ref[:, c].reshape(count * share, ranks) for c in range(2)], 1)
+
+
+def product_blocks(product):
+    chips, cores, share, ranks = product.shape
+    return pl.BlockSpec((WIDTH // share, cores, share, ranks), lambda j: (j, 0, 0, 0))
+
+
+def momentum_update(buffer, left, product):
     rows, columns = buffer.shape
-    count = WIDTH // product.shape[2]
-
-    def kernel(buffer_ref, ortho_ref, inverse_ref, product_ref, out, out_high, out_low, *halves):
-        left, inner = halves[:2], halves[2:]
-
+
+    def kernel(buffer_ref, left_ref, product_ref, out, high, low):
         @pl.when(pl.program_id(0) == 0)
         def _():
-            left[0][...], left[1][...] = split_two(ortho_ref[...])
-            inner[0][...], inner[1][...] = split_two(inverse_ref[...])
-
-        ranks = product.shape[3]
-        block = jnp.concatenate([product_ref[:, c].reshape(WIDTH, ranks) for c in range(2)], 1)
-        right = product3(split_two(block), (inner[0][...], inner[1][...]), NT)
-        high, low = split_two(right)
-        out_high[...], out_low[...] = high, low
-        out[...] = buffer_ref[...] - decay_keep * product3((left[0][...], left[1][...]), (high, low), NT)
-
-    half, square = pltpu.VMEM((rows, R), jnp.bfloat16), pltpu.VMEM((R, R), jnp.bfloat16)
-    pair = jax.ShapeDtypeStruct((columns, R), jnp.bfloat16)
-    tall = pl.BlockSpec((WIDTH, R), lambda j: (j, 0))
+            high[...], low[...] = split_two(left_ref[...])
+
+        step = product3((high[...], low[...]), split_two(columns_first(product_ref)), NT)
+        out[...] = buffer_ref[...] - decay_keep * step
+
+    half = pltpu.VMEM((rows, R), jnp.bfloat16)
     return call(
         kernel,
         columns // WIDTH,
-        (buffer, ortho, inverse, product),
+        (buffer, left, product),
+        [wide(rows), whole(rows, R), product_blocks(product)],
+        jax.ShapeDtypeStruct((rows, columns), F32),
+        wide(rows),
+        (half, half),
+        name="momentum_update",
+    )
+
+
+def weights_update(weights, ortho, inverse, product, sums, start, share):
+    rows, columns = weights.shape
+    height = rows + share
+
+    def kernel(start_ref, weights_ref, ortho_ref, inverse_ref, product_ref, sums_ref, out, own, high, low):
+        @pl.when(pl.program_id(0) == 0)
+        def _():
+            scale = jnp.sqrt(jnp.sum(sums_ref[...], axis=0) / N + eps_norm)
+            at = pl.multiple_of(start_ref[0], share)
+            lanes = lax.broadcasted_iota(jnp.int32, (share, R), 1)
+            mine = lanes == at + lax.broadcasted_iota(jnp.int32, (share, R), 0)
+            picked = jnp.sum(jnp.where(mine, jnp.broadcast_to(scale, (share, R)), 0.0), axis=1, keepdims=True)
+            left = product3(split_two(ortho_ref[...] / scale), split_two(inverse_ref[...]), NN)
+            stack = jnp.concatenate([left, inverse_ref[pl.ds(at, share), :] / picked], 0)
+            high[...], low[...] = split_two(stack)
+
+        both = product3((high[...], low[...]), split_two(columns_first(product_ref)), NT)
+        out[...] = weights_ref[...] - step_size * both[:rows]
+        own[...] = both[rows:]
+
+    half = pltpu.VMEM((height, R), jnp.bfloat16)
+    return call(
+        kernel,
+        columns // WIDTH,
+        (start, weights, ortho, inverse, product, sums),
         [
+            pl.BlockSpec(memory_space=pltpu.SMEM),
             wide(rows),
             whole(rows, R),
             whole(R, R),
-            pl.BlockSpec((count, *product.shape[1:]), lambda j: (j, 0, 0, 0)),
+            product_blocks(product),
+            whole(*sums.shape),
         ],
-        (jax.ShapeDtypeStruct((rows, columns), F32), pair, pair),
-        (wide(rows), tall, tall),
-        (half, half, square, square),
-        name="momentum_update",
-    )
-
-
-def weights_update(weights, ortho, right, sums, start, share):
-    rows, columns = weights.shape
-    count = sums.shape[0]
-
-    def kernel(start_ref, weights_ref, ortho_ref, right_high, right_low, sums_ref, out, own, high, low, chosen, own_scale):
-        @pl.when(pl.program_id(0) == 0)
-        def _():
-            scale = jnp.sqrt(jnp.sum(sums_ref[...], axis=0) / N + eps_norm)
-            high[...], low[...] = split_two(ortho_ref[...] / scale)
-            lanes = lax.broadcasted_iota(jnp.int32, (share, R), 1)
-            mine = lanes == start_ref[0] + lax.broadcasted_iota(jnp.int32, (share, R), 0)
-            chosen[...] = jnp.where(mine, 1.0, 0.0).astype(jnp.bfloat16)
-            picked = jnp.sum(jnp.where(mine, jnp.broadcast_to(scale, (share, R)), 0.0), axis=1, keepdims=True)
-            own_scale[...] = jnp.broadcast_to(picked, own_scale.shape)
-
-        right = right_high[...], right_low[...]
-        out[...] = weights_ref[...] - step_size * product3((high[...], low[...]), right, NT)
-        rows_high, rows_low = (
-            lax.dot_general(chosen[...], one, (NT, ((), ())), preferred_element_type=F32) for one in right
-        )
-        own[...] = (rows_high + rows_low) / own_scale[...]
-
-    half = pltpu.VMEM((rows, R), jnp.bfloat16)
-    tall = pl.BlockSpec((WIDTH, R), lambda j: (j, 0))
-    return call(
-        kernel,
-        columns // WIDTH,
-        (start, weights, ortho, *right, sums),
-        [pl.BlockSpec(memory_space=pltpu.SMEM), wide(rows), whole(rows, R), tall, tall, whole(count, 1, R)],
         (jax.ShapeDtypeStruct((rows, columns), F32), jax.ShapeDtypeStruct((share, columns), F32)),
         (wide(rows), wide(share)),
-        (half, half, pltpu.VMEM((share, R), jnp.bfloat16), pltpu.VMEM((share, WIDTH), F32)),
+        (half, half),
         name="weights_update",
     )
 
@@ -442,7 +428,7 @@
     gram = jnp.where(
         core == 0, jnp.concatenate([gram, gram_other], 0), jnp.concatenate([gram_other, gram], 0)
     )
-    product = copy_after(product, gram)
+    product = after(product, gram)
     inverse = inverse_factor(gram, product)
 
     beside = shift(product, "core", 1)
@@ -456,9 +442,9 @@
     left_own = jnp.where(core == 0, left_own[:, :height], left_own[:, height:])
     ortho = dot(left_own, inverse, ((0,), (1,)), HIGHEST)
     sums = lax.all_to_all(total_after(sums, product), ("x", "y"), 0, 0, tiled=True)
-    new_momentum, *right_t = momentum_update(buffer, ortho, inverse, product)
+    new_momentum = momentum_update(buffer, dot(ortho, inverse, NN, HIGHEST), product)
     start = jnp.full((1,), (2 * z + core) * share, jnp.int32)
-    new_weights, new_right = weights_update(weights, ortho, right_t, sums, start, share)
+    new_weights, new_right = weights_update(weights, ortho, inverse, product, sums, start, share)
     return (new_weights, new_momentum, new_right)
 
 

time: 195 us -> 193 us (0.990)
  Pallas kernels: 47.4 us -> 42.7 us
    pallas_call x4, Pallas kernels: 20.9 us -> 17.8 us  [call(): pl.pallas_call(kernel, grid=(steps,), out_shape=outs, in_specs=specs, out...]
  transfers between devices with their start and end apart: 17 -> 17, of which waited for: 11 -> 12; matrix products, arithmetic and copies ran while one was open for 3% -> 4% of each run, Pallas kernels for 17% -> 15%
where the time goes in v5:
time: 193 us
  blocking collectives  46.3 us (24%)
  starting transfers between devices  44.2 us (23%)
  Pallas kernels  42.7 us (22%)
  waiting for transfers between devices  33.4 us (17%)
  between operations  14.3 us (7%)
  other arithmetic  6.27 us (3%)
  matrix products  3.89 us (2%)
    all_to_all x2, blocking collectives, spread(): return lax.all_to_all(whole, axes, 0, 0, tiled=True)  30.8 us
    ppermute x12, starting transfers between devices, shift(): lax.ppermute(values, axis, [(i, (i + by) % size) for i in range(size)])  27.7 us
    pallas_call x1, Pallas kernels, inverse_factor(): pl.pallas_call(inverse_factor_kernel, out_shape=jax.ShapeDtypeStruct((R,...  23 us
    pallas_call x4, Pallas kernels, call(): pl.pallas_call(kernel, grid=(steps,), out_shape=outs, in_specs=specs, out...  17.8 us
    ppermute x12, waiting for transfers between devices, shift(): lax.ppermute(values, axis, [(i, (i + by) % size) for i in range(size)])  15.8 us
    all_to_all x1, blocking collectives, local(): lax.all_to_all(part.reshape(XY, -1, rows), ('x', 'y'), 0, 0, tiled=True)  15.6 us
    all_to_all x1, waiting for transfers between devices, spread(): return lax.all_to_all(whole, axes, 0, 0, tiled=True)  9.17 us
    all_to_all x1, starting transfers between devices, local(): lax.all_to_all(total_after(sums, product), ('x', 'y'), 0, 0, tiled=True)  6.39 us
  transfers between devices with their start and end apart: 17, of which 12 were waited for; matrix products, arithmetic and copies ran while one was open for 4% of the time, Pallas kernels for 15%

profile of v5, /device:TPU:1, one launch (start us, length us, event | category | flops | bytes accessed | tf_op | source)
XLA Modules:
  0.0 192.8 jit_solution(14203671278179236532)
XLA Ops:
  9.1 3.3 %collective-permute-start.8 = (f32[256,1792]{1,0:T(8,128)S(1)}, f32[256,1792]{1,0:T(8,128)}, u32[]{:S(2)}, u32[]{:S(2)}) collective-permute-start(f32[256,1792]{1,0:T(8,128)S(1)} %convert_add_fusion.buffer_ref), channel_id=1, source_target_pairs={{0,16},{16,0},{1,17},{17,1},{2,18},{18,2},{3,19},{19,3},{4,20},{20... | collective-permute-start | bytes 5505032 | tf_op jit(solution)/shard_map/ppermute | solution.py:374
  13.7 3.0 %collective-permute-start.1 = (f32[32,1792]{1,0:T(8,128)S(1)}, f32[32,1792]{1,0:T(8,128)S(1)}, u32[]{:S(2)}, u32[]{:S(2)}) collective-permute-start(f32[32,1792]{1,0:T(8,128)S(1)} %copy-done.2), channel_id=1, source_target_pairs={{0,192},{32,224},{64,0},{96,32},{128,64},{160,96},{192,128},{224,1... | collective-permute-start | bytes 688136 | tf_op jit(solution)/shard_map/ppermute | solution.py:374
  18.7 5.5 %collective-permute-done.3.refs_7_ = f32[32,1792]{1,0:T(8,128)S(1)} collective-permute-done((f32[32,1792]{1,0:T(8,128)S(1)}, f32[32,1792]{1,0:T(8,128)S(1)}, u32[]{:S(2)}, u32[]{:S(2)}) %collective-permute-start.3) | collective-permute-done | bytes 229408 | tf_op jit(solution)/shard_map/ppermute | solution.py:374
  24.2 3.7 %collective-permute-start.4 = (f32[16,1792]{1,0:T(8,128)S(1)}, f32[16,1792]{1,0:T(8,128)S(1)}, u32[]{:S(2)}, u32[]{:S(2)}) collective-permute-start(f32[16,1792]{1,0:T(8,128)S(1)} %slice.26), channel_id=1, source_target_pairs={{0,64},{32,96},{64,128},{96,160},{128,192},{160,224},{192,0},{224,... | collective-permute-start | bytes 344072 | tf_op jit(solution)/shard_map/ppermute | solution.py:374
  28.6 2.4 %collective-permute-start.5 = (f32[16,1792]{1,0:T(8,128)S(1)}, f32[16,1792]{1,0:T(8,128)S(1)}, u32[]{:S(2)}, u32[]{:S(2)}) collective-permute-start(f32[16,1792]{1,0:T(8,128)S(1)} %slice.27), channel_id=1, source_target_pairs={{0,192},{32,224},{64,0},{96,32},{128,64},{160,96},{192,128},{224,1... | collective-permute-start | bytes 344072 | tf_op jit(solution)/shard_map/ppermute | solution.py:374
  31.0 2.0 %collective-permute-done.refs_1_ = f32[32,1792]{1,0:T(8,128)S(1)} collective-permute-done((f32[32,1792]{1,0:T(8,128)S(1)}, f32[32,1792]{1,0:T(8,128)S(1)}, u32[]{:S(2)}, u32[]{:S(2)}) %collective-permute-start) | collective-permute-done | bytes 229408 | tf_op jit(solution)/shard_map/ppermute | solution.py:374
  35.6 2.4 %maximum_select_fusion.refs_9_.chip_ref = f32[512,1792]{1,0:T(8,128)S(1)} fusion(f32[256,1792]{1,0:T(8,128)} %collective-permute-done.8, f32[256,1792]{1,0:T(8,128)S(1)} %convert_add_fusion.buffer_ref, pred[]{:T(512)S(6)} %eq.6), kind=kLoop, calls=%fused_computation | loop fusion | flops 2752512 | bytes 7340033 | tf_op jit(solution)/shard_map/jit(_where)/select_n | solution.py:406
  38.3 2.7 %collective-permute-done.6.refs_6_ = f32[32,1792]{1,0:T(8,128)S(1)} collective-permute-done((f32[32,1792]{1,0:T(8,128)S(1)}, f32[32,1792]{1,0:T(8,128)S(1)}, u32[]{:S(2)}, u32[]{:S(2)}) %collective-permute-start.6) | collective-permute-done | bytes 229408 | tf_op jit(solution)/shard_map/ppermute | solution.py:374
  42.6 2.5 %left_product.1 = f32[256,512]{1,0:T(8,128)S(1)} custom-call(f32[32,1792]{1,0:T(8,128)S(1)} %copy-done.2, f32[32,1792]{1,0:T(8,128)S(1)} %collective-permute-done.refs_1_, f32[32,1792]{1,0:T(8,128)S(1)} %collective-permute-done.1.refs_2_, f32[32,1792]{1,0:T(8,128)S(1)} %collective-permute-done.2.refs_3_, f32[16,1792]{1,0:T(8,128)S(1)} %collective-permute-done.4.refs_4_, ...), custom_call_target="tpu_custom_call" | custom-call | flops 3000000000 | bytes 4194304 | tf_op jit(solution)/shard_map/left_product/pallas_call | solution.py:184
  45.2 15.6 %all_to_all.30 = f32[16,16,512]{2,1,0:T(8,128)S(1)} all-to-all(f32[16,16,512]{2,1,0:T(8,128)S(1)} %bitcast.17), channel_id=1, replica_groups=mesh['z'=8,'core'=2,'x'=4,'y'=4] {'x','y'}, dimensions={0} | all-to-all | bytes 1048576 | tf_op jit(solution)/shard_map/all_to_all | solution.py:413
  61.6 4.4 %all-to-all-start.1 = ((f32[16,16,512]{2,1,0:T(8,128)}), f32[16,16,512]{2,1,0:T(8,128)S(1)}, u32[]{:S(2)}, u32[]{:S(2)}) async-start(f32[16,16,512]{2,1,0:T(8,128)} %broadcast_in_dim.11), calls=%async_computation.1 | async-start | bytes 1048576 | tf_op jit(solution)/shard_map/all_to_all | solution.py:379
  66.1 9.2 %all-to-all-done.1 = f32[16,16,512]{2,1,0:T(8,128)S(1)} async-done(((f32[16,16,512]{2,1,0:T(8,128)}), f32[16,16,512]{2,1,0:T(8,128)S(1)}, u32[]{:S(2)}, u32[]{:S(2)}) %all-to-all-start.1) | async-done | bytes 524320 | tf_op jit(solution)/shard_map/all_to_all | solution.py:379
  75.4 4.7 %right_product.1 = f32[1792,256]{1,0:T(8,128)} custom-call(f32[256,512]{1,0:T(8,128)S(1)} %bitcast.18, f32[512,1792]{1,0:T(8,128)} %copy-done), custom_call_target="tpu_custom_call" | custom-call | flops 3000000000 | bytes 4194304 | tf_op jit(solution)/shard_map/right_product/pallas_call | solution.py:184
  80.2 3.6 %collective-permute-start.9 = (f32[8,32,512]{2,1,0:T(8,128)S(1)}, f32[8,32,512]{2,1,0:T(8,128)S(1)}, u32[]{:S(2)}, u32[]{:S(2)}) collective-permute-start(f32[8,32,512]{2,1,0:T(8,128)S(1)} %fusion), channel_id=1, source_target_pairs={{0,16},{16,0},{1,17},{17,1},{2,18},{18,2},{3,19},{19,3},{4,20},{20... | collective-permute-start | bytes 1572872 | tf_op jit(solution)/shard_map/ppermute | solution.py:374
  86.6 19.2 %all_to_all.31 = f32[8,16,512]{2,1,0:T(8,128)S(1)} all-to-all(f32[8,16,512]{2,1,0:T(8,128)S(1)} %broadcast_in_dim.12), channel_id=1, replica_groups=mesh['z'=8,'core'=2,'x'=4,'y'=4] {'z'}, dimensions={0} | all-to-all | bytes 524288 | tf_op jit(solution)/shard_map/all_to_all | solution.py:379
  105.8 11.6 %all_to_all.32 = f32[16,16,512]{2,1,0:T(8,128)S(1)} all-to-all(f32[16,16,512]{2,1,0:T(8,128)S(1)} %broadcast_in_dim.13), channel_id=1, replica_groups=mesh['z'=8,'core'=2,'x'=4,'y'=4] {'x','y'}, dimensions={0} | all-to-all | bytes 1048576 | tf_op jit(solution)/shard_map/all_to_all | solution.py:379
  117.4 3.5 %collective-permute-start.10 = (f32[256,512]{1,0:T(8,128)S(1)}, f32[256,512]{1,0:T(8,128)S(1)}, u32[]{:S(2)}, u32[]{:S(2)}) collective-permute-start(f32[256,512]{1,0:T(8,128)S(1)} %bitcast.28), channel_id=1, source_target_pairs={{0,16},{16,0},{1,17},{17,1},{2,18},{18,2},{3,19},{19,3},{4,20},{20... | collective-permute-start | bytes 1572872 | tf_op jit(solution)/shard_map/ppermute | solution.py:374
  124.8 2.3 %collective-permute-start.11 = (f32[224,256]{1,0:T(8,128)S(1)}, f32[224,256]{1,0:T(8,128)S(1)}, u32[]{:S(2)}, u32[]{:S(2)}) collective-permute-start(f32[224,256]{1,0:T(8,128)S(1)} %copy-done.1), channel_id=1, source_target_pairs={{0,16},{16,0},{1,17},{17,1},{2,18},{18,2},{3,19},{19,3},{4,20},{20... | collective-permute-start | bytes 688136 | tf_op jit(solution)/shard_map/ppermute | solution.py:374
  127.1 23.0 %inverse_factor.1.inverse_ref = f32[512,512]{1,0:T(8,128)S(1)} custom-call(f32[512,512]{1,0:T(8,128)S(1)} %maximum_select_fusion.1.gram, f32[224,256]{1,0:T(8,128)S(1)} %copy-done.1), custom_call_target="tpu_custom_call" | custom-call | flops 30000001024 | bytes 2097152 | tf_op jit(solution)/shard_map/inverse_factor/pallas_call | solution.py:143
  153.3 5.7 %all-to-all-start.4 = ((f32[8,1,512]{2,1,0:T(1,128)}), f32[8,1,512]{2,1,0:T(1,128)S(1)}, u32[]{:S(2)}, u32[]{:S(2)}) async-start(f32[8,1,512]{2,1,0:T(1,128)} %column_squares.1), calls=%async_computation.5 | async-start | bytes 32768 | tf_op jit(solution)/shard_map/all_to_all | solution.py:436
  160.0 5.6 %all-to-all-done.4.sums_ref = f32[8,1,512]{2,1,0:T(1,128)S(1)} async-done(((f32[8,1,512]{2,1,0:T(1,128)}), f32[8,1,512]{2,1,0:T(1,128)S(1)}, u32[]{:S(2)}, u32[]{:S(2)}) %all-to-all-start.4) | async-done | bytes 16416 | tf_op jit(solution)/shard_map/all_to_all | solution.py:436
  167.5 6.4 %all-to-all-start.5 = ((f32[16,1,512]{2,1,0:T(1,128)}), f32[16,1,512]{2,1,0:T(1,128)S(1)}, u32[]{:S(2)}, u32[]{:S(2)}) async-start(f32[16,1,512]{2,1,0:T(1,128)} %total_after.1), calls=%async_computation.6 | async-start | bytes 65536 | tf_op jit(solution)/shard_map/all_to_all | solution.py:444
  173.9 4.9 %momentum_update.1 = f32[256,1792]{1,0:T(8,128)} custom-call(f32[256,1792]{1,0:T(8,128)} %copy-done.3, f32[256,512]{1,0:T(8,128)S(1)} %fusion.8.left_ref, f32[8,2,224,256]{3,2,1,0:T(8,128)} %bitcast.25), custom_call_target="tpu_custom_call" | custom-call | flops 3000000000 | bytes 4194304 | tf_op jit(solution)/shard_map/momentum_update/pallas_call | solution.py:184
  180.3 5.6 %weights_update.1 = (f32[256,1792]{1,0:T(8,128)}, f32[32,1792]{1,0:T(8,128)}) custom-call(s32[1]{0:T(128)} %bitcast.start_ref, f32[256,1792]{1,0:T(8,128)} %weights_ref.1, f32[256,512]{1,0:T(8,128)S(1)} %fusion.1.ortho_ref, f32[512,512]{1,0:T(8,128)S(1)} %inverse_factor.1.inverse_ref, f32[8,2,224,256]{3,2,1,0:T(8,128)} %bitcast.26, ...), custom_call_target="tpu_custom_call" | custom-call | flops 3000000000 | bytes 4194304 | tf_op jit(solution)/shard_map/weights_update/pallas_call | solution.py:184
  (48 shorter events, 25.8 us)
Async XLA Ops:
  7.2 5.3 %copy-start.2 = (f32[32,1792]{1,0:T(8,128)S(1)}, f32[32,1792]{1,0:T(8,128)}, u32[]{:S(2)}) copy-start(f32[32,1792]{1,0:T(8,128)} %refs_0_.1) | copy-start | bytes 688132
  9.1 29.0 %copy-start.3 = (f32[256,1792]{1,0:T(8,128)}, f32[256,1792]{1,0:T(8,128)S(1)}, u32[]{:S(2)}) copy-start(f32[256,1792]{1,0:T(8,128)S(1)} %convert_add_fusion.buffer_ref) | copy-start | bytes 5505028
  9.1 24.7 %collective-permute-start.8 = (f32[256,1792]{1,0:T(8,128)S(1)}, f32[256,1792]{1,0:T(8,128)}, u32[]{:S(2)}, u32[]{:S(2)}) collective-permute-start(f32[256,1792]{1,0:T(8,128)S(1)} %convert_add_fusion.buffer_ref), channel_id=1, source_target_pairs={{0,16},{16,0},{1,17},{17,1},{2,18},{18,2},{3,19},{19,3},{4,20},{20... | collective-permute-start | bytes 5505032 | tf_op jit(solution)/shard_map/ppermute | solution.py:374
  12.4 11.7 %collective-permute-start.3 = (f32[32,1792]{1,0:T(8,128)S(1)}, f32[32,1792]{1,0:T(8,128)S(1)}, u32[]{:S(2)}, u32[]{:S(2)}) collective-permute-start(f32[32,1792]{1,0:T(8,128)S(1)} %copy-done.2), channel_id=1, source_target_pairs={{0,64},{32,96},{64,128},{96,160},{128,192},{160,224},{192,0},{224,... | collective-permute-start | bytes 688136 | tf_op jit(solution)/shard_map/ppermute | solution.py:374
  13.7 14.9 %collective-permute-start.1 = (f32[32,1792]{1,0:T(8,128)S(1)}, f32[32,1792]{1,0:T(8,128)S(1)}, u32[]{:S(2)}, u32[]{:S(2)}) collective-permute-start(f32[32,1792]{1,0:T(8,128)S(1)} %copy-done.2), channel_id=1, source_target_pairs={{0,192},{32,224},{64,0},{96,32},{128,64},{160,96},{192,128},{224,1... | collective-permute-start | bytes 688136 | tf_op jit(solution)/shard_map/ppermute | solution.py:374
  16.7 16.2 %collective-permute-start = (f32[32,1792]{1,0:T(8,128)S(1)}, f32[32,1792]{1,0:T(8,128)S(1)}, u32[]{:S(2)}, u32[]{:S(2)}) collective-permute-start(f32[32,1792]{1,0:T(8,128)S(1)} %copy-done.2), channel_id=1, source_target_pairs={{0,224},{32,0},{64,32},{96,64},{128,96},{160,128},{192,160},{224,1... | collective-permute-start | bytes 688136 | tf_op jit(solution)/shard_map/ppermute | solution.py:374
  18.7 19.4 %collective-permute-start.7 = (f32[32,1792]{1,0:T(8,128)S(1)}, f32[32,1792]{1,0:T(8,128)S(1)}, u32[]{:S(2)}, u32[]{:S(2)}) collective-permute-start(f32[32,1792]{1,0:T(8,128)S(1)} %copy-done.2), channel_id=1, source_target_pairs={{0,32},{32,64},{64,96},{96,128},{128,160},{160,192},{192,224},{224... | collective-permute-start | bytes 688136 | tf_op jit(solution)/shard_map/ppermute | solution.py:374
  24.2 13.9 %collective-permute-start.4 = (f32[16,1792]{1,0:T(8,128)S(1)}, f32[16,1792]{1,0:T(8,128)S(1)}, u32[]{:S(2)}, u32[]{:S(2)}) collective-permute-start(f32[16,1792]{1,0:T(8,128)S(1)} %slice.26), channel_id=1, source_target_pairs={{0,64},{32,96},{64,128},{96,160},{128,192},{160,224},{192,0},{224,... | collective-permute-start | bytes 344072 | tf_op jit(solution)/shard_map/ppermute | solution.py:374
  28.6 9.7 %collective-permute-start.5 = (f32[16,1792]{1,0:T(8,128)S(1)}, f32[16,1792]{1,0:T(8,128)S(1)}, u32[]{:S(2)}, u32[]{:S(2)}) collective-permute-start(f32[16,1792]{1,0:T(8,128)S(1)} %slice.27), channel_id=1, source_target_pairs={{0,192},{32,224},{64,0},{96,32},{128,64},{160,96},{192,128},{224,1... | collective-permute-start | bytes 344072 | tf_op jit(solution)/shard_map/ppermute | solution.py:374
  33.0 8.0 %collective-permute-start.6 = (f32[32,1792]{1,0:T(8,128)S(1)}, f32[32,1792]{1,0:T(8,128)S(1)}, u32[]{:S(2)}, u32[]{:S(2)}) collective-permute-start(f32[32,1792]{1,0:T(8,128)S(1)} %collective-permute-done.3.refs_7_), channel_id=1, source_target_pairs={{0,32},{32,64},{64,96},{96,128},{128,160},{160,192},{192,224},{224... | collective-permute-start | bytes 688136 | tf_op jit(solution)/shard_map/ppermute | solution.py:374
  33.8 8.9 %collective-permute-start.2 = (f32[32,1792]{1,0:T(8,128)S(1)}, f32[32,1792]{1,0:T(8,128)S(1)}, u32[]{:S(2)}, u32[]{:S(2)}) collective-permute-start(f32[32,1792]{1,0:T(8,128)S(1)} %collective-permute-done.1.refs_2_), channel_id=1, source_target_pairs={{0,224},{32,0},{64,32},{96,64},{128,96},{160,128},{192,160},{224,1... | collective-permute-start | bytes 688136 | tf_op jit(solution)/shard_map/ppermute | solution.py:374
  38.1 7.1 %copy-start = (f32[512,1792]{1,0:T(8,128)}, f32[512,1792]{1,0:T(8,128)S(1)}, u32[]{:S(2)}) copy-start(f32[512,1792]{1,0:T(8,128)S(1)} %maximum_select_fusion.refs_9_.chip_ref) | copy-start | bytes 11010052
  61.6 13.6 %all-to-all-start.1 = ((f32[16,16,512]{2,1,0:T(8,128)}), f32[16,16,512]{2,1,0:T(8,128)S(1)}, u32[]{:S(2)}, u32[]{:S(2)}) async-start(f32[16,16,512]{2,1,0:T(8,128)} %broadcast_in_dim.11), calls=%async_computation.1 | async-start | bytes 1048576 | tf_op jit(solution)/shard_map/all_to_all | solution.py:379
  66.0 56.6 %reduce-scatter.2.cloned.1.call-start = ((), (), s32[]{:S(2)}) async-start(), calls=%async_computation.7 | async-start | bytes 2064384 | tf_op jit(solution)/shard_map/reduce_scatter | solution.py:418
  80.1 86.7 %all-gather.2.cloned.1.call-start = ((), (), s32[]{:S(2)}) async-start(), calls=%async_computation.8 | async-start | bytes 3899392 | tf_op jit(solution)/shard_map/all_gather | solution.py:437
  80.2 5.1 %collective-permute-start.9 = (f32[8,32,512]{2,1,0:T(8,128)S(1)}, f32[8,32,512]{2,1,0:T(8,128)S(1)}, u32[]{:S(2)}, u32[]{:S(2)}) collective-permute-start(f32[8,32,512]{2,1,0:T(8,128)S(1)} %fusion), channel_id=1, source_target_pairs={{0,16},{16,0},{1,17},{17,1},{2,18},{18,2},{3,19},{19,3},{4,20},{20... | collective-permute-start | bytes 1572872 | tf_op jit(solution)/shard_map/ppermute | solution.py:374
  117.4 5.0 %collective-permute-start.10 = (f32[256,512]{1,0:T(8,128)S(1)}, f32[256,512]{1,0:T(8,128)S(1)}, u32[]{:S(2)}, u32[]{:S(2)}) collective-permute-start(f32[256,512]{1,0:T(8,128)S(1)} %bitcast.28), channel_id=1, source_target_pairs={{0,16},{16,0},{1,17},{17,1},{2,18},{18,2},{3,19},{19,3},{4,20},{20... | collective-permute-start | bytes 1572872 | tf_op jit(solution)/shard_map/ppermute | solution.py:374
  123.9 0.9 copy-start.1
  124.8 27.2 %collective-permute-start.11 = (f32[224,256]{1,0:T(8,128)S(1)}, f32[224,256]{1,0:T(8,128)S(1)}, u32[]{:S(2)}, u32[]{:S(2)}) collective-permute-start(f32[224,256]{1,0:T(8,128)S(1)} %copy-done.1), channel_id=1, source_target_pairs={{0,16},{16,0},{1,17},{17,1},{2,18},{18,2},{3,19},{19,3},{4,20},{20... | collective-permute-start | bytes 688136 | tf_op jit(solution)/shard_map/ppermute | solution.py:374
  153.3 12.4 %all-to-all-start.4 = ((f32[8,1,512]{2,1,0:T(1,128)}), f32[8,1,512]{2,1,0:T(1,128)S(1)}, u32[]{:S(2)}, u32[]{:S(2)}) async-start(f32[8,1,512]{2,1,0:T(1,128)} %column_squares.1), calls=%async_computation.5 | async-start | bytes 32768 | tf_op jit(solution)/shard_map/all_to_all | solution.py:436
  167.5 12.9 %all-to-all-start.5 = ((f32[16,1,512]{2,1,0:T(1,128)}), f32[16,1,512]{2,1,0:T(1,128)S(1)}, u32[]{:S(2)}, u32[]{:S(2)}) async-start(f32[16,1,512]{2,1,0:T(1,128)} %total_after.1), calls=%async_computation.6 | async-start | bytes 65536 | tf_op jit(solution)/shard_map/all_to_all | solution.py:444
Sparse Core Ops, SparseCore 0:
  80.3 40.2 reduce-scatter.1
  124.0 42.7 all-gather.1

commit v6 on v5

--- a/solution.py
+++ b/solution.py
@@ -276,22 +276,6 @@
     )(core, inverse, own, other)
 
 
-def total_after(sums, earlier):
-    def kernel(sums_ref, _, out):
-        out[...] = jnp.broadcast_to(jnp.sum(sums_ref[...], axis=0, keepdims=True), out.shape)
-
-    vmem = pl.BlockSpec(memory_space=pltpu.VMEM)
-    return pl.pallas_call(
-        kernel,
-        out_shape=jax.ShapeDtypeStruct((XY, 1, R), F32),
-        in_specs=[vmem, pl.BlockSpec(memory_space=pl.ANY)],
-        out_specs=vmem,
-        compiler_params=pltpu.CompilerParams(vmem_limit_bytes=LIMIT),
-        cost_estimate=pl.CostEstimate(flops=1, bytes_accessed=2**16, transcendentals=0),
-        name="total_after",
-    )(sums, earlier)
-
-
 def columns_first(product_ref):
     count, _, share, ranks = product_ref.shape
     return jnp.concatenate([product_ref[:, c].reshape(count * share, ranks) for c in range(2)], 1)
@@ -302,35 +286,14 @@
     return pl.BlockSpec((WIDTH // share, cores, share, ranks), lambda j: (j, 0, 0, 0))
 
 
-def momentum_update(buffer, left, product):
-    rows, columns = buffer.shape
-
-    def kernel(buffer_ref, left_ref, product_ref, out, high, low):
-        @pl.when(pl.program_id(0) == 0)
-        def _():
-            high[...], low[...] = split_two(left_ref[...])
-
-        step = product3((high[...], low[...]), split_two(columns_first(product_ref)), NT)
-        out[...] = buffer_ref[...] - decay_keep * step
-
-    half = pltpu.VMEM((rows, R), jnp.bfloat16)
-    return call(
-        kernel,
-        columns // WIDTH,
-        (buffer, left, product),
-        [wide(rows), whole(rows, R), product_blocks(product)],
-        jax.ShapeDtypeStruct((rows, columns), F32),
-        wide(rows),
-        (half, half),
-        name="momentum_update",
-    )
-
-
-def weights_update(weights, ortho, inverse, product, sums, start, share):
+def update(weights, buffer, ortho, inverse, product, sums, start, share):
     rows, columns = weights.shape
-    height = rows + share
-
-    def kernel(start_ref, weights_ref, ortho_ref, inverse_ref, product_ref, sums_ref, out, own, high, low):
+    height = 2 * rows + share
+
+    def kernel(
+        start_ref, weights_ref, buffer_ref, ortho_ref, inverse_ref, product_ref, sums_ref,
+        new_weights, new_momentum, own, high, low,
+    ):
         @pl.when(pl.program_id(0) == 0)
         def _():
             scale = jnp.sqrt(jnp.sum(sums_ref[...], axis=0) / N + eps_norm)
@@ -338,31 +301,35 @@
             lanes = lax.broadcasted_iota(jnp.int32, (share, R), 1)
             mine = lanes == at + lax.broadcasted_iota(jnp.int32, (share, R), 0)
             picked = jnp.sum(jnp.where(mine, jnp.broadcast_to(scale, (share, R)), 0.0), axis=1, keepdims=True)
-            left = product3(split_two(ortho_ref[...] / scale), split_two(inverse_ref[...]), NN)
+            both = jnp.concatenate([ortho_ref[...], ortho_ref[...] / scale], 0)
+            left = product3(split_two(both), split_two(inverse_ref[...]), NN)
             stack = jnp.concatenate([left, inverse_ref[pl.ds(at, share), :] / picked], 0)
             high[...], low[...] = split_two(stack)
 
-        both = product3((high[...], low[...]), split_two(columns_first(product_ref)), NT)
-        out[...] = weights_ref[...] - step_size * both[:rows]
-        own[...] = both[rows:]
-
-    half = pltpu.VMEM((height, R), jnp.bfloat16)
+        steps = product3((high[...], low[...]), split_two(columns_first(product_ref)), NT)
+        new_momentum[...] = buffer_ref[...] - decay_keep * steps[:rows]
+        new_weights[...] = weights_ref[...] - step_size * steps[rows : 2 * rows]
+        own[...] = steps[2 * rows :]
+
+    full = jax.ShapeDtypeStruct((rows, columns), F32)
+    stacked = pltpu.VMEM((height, R), jnp.bfloat16)
     return call(
         kernel,
         columns // WIDTH,
-        (start, weights, ortho, inverse, product, sums),
+        (start, weights, buffer, ortho, inverse, product, sums),
         [
             pl.BlockSpec(memory_space=pltpu.SMEM),
+            wide(rows),
             wide(rows),
             whole(rows, R),
             whole(R, R),
             product_blocks(product),
             whole(*sums.shape),
         ],
-        (jax.ShapeDtypeStruct((rows, columns), F32), jax.ShapeDtypeStruct((share, columns), F32)),
-        (wide(rows), wide(share)),
-        (half, half),
-        name="weights_update",
+        (full, full, jax.ShapeDtypeStruct((share, columns), F32)),
+        (wide(rows), wide(rows), wide(share)),
+        (stacked, stacked),
+        name="update",
     )
 
 
@@ -441,10 +408,9 @@
     left_own = jnp.concatenate(by_core, 0).reshape(R, rows)
     left_own = jnp.where(core == 0, left_own[:, :height], left_own[:, height:])
     ortho = dot(left_own, inverse, ((0,), (1,)), HIGHEST)
-    sums = lax.all_to_all(total_after(sums, product), ("x", "y"), 0, 0, tiled=True)
-    new_momentum = momentum_update(buffer, dot(ortho, inverse, NN, HIGHEST), product)
+    sums = spread(jnp.sum(sums, 0), ("x", "y"), XY)
     start = jnp.full((1,), (2 * z + core) * share, jnp.int32)
-    new_weights, new_right = weights_update(weights, ortho, inverse, product, sums, start, share)
+    new_weights, new_momentum, new_right = update(weights, buffer, ortho, inverse, product, sums, start, share)
     return (new_weights, new_momentum, new_right)
 
 

time: 193 us -> 192 us (level)
  Pallas kernels: 42.7 us -> 39.7 us
    all_to_all x1 -> x0, starting transfers between devices: 6.39 us -> none  [local(): lax.all_to_all(total_after(sums, product), ('x', 'y'), 0, 0, tiled=True)]
    all_to_all x1 -> x2, starting transfers between devices: 4.36 us -> 9.17 us  [spread(): return lax.all_to_all(whole, axes, 0, 0, tiled=True)]
    all_to_all x1 -> x2, waiting for transfers between devices: 9.17 us -> 12.6 us  [spread(): return lax.all_to_all(whole, axes, 0, 0, tiled=True)]
    pallas_call x4 -> x3, Pallas kernels: 17.8 us -> 15.4 us  [call(): pl.pallas_call(kernel, grid=(steps,), out_shape=outs, in_specs=specs, out...]
    dot_general x3 -> x2, matrix products: 3.89 us -> 4.04 us  [dot(): lax.dot_general(first, second, ((dims[0], dims[1]), ((), ())), precision=...]
  transfers between devices with their start and end apart: 17 -> 17, of which waited for: 12 -> 11; matrix products, arithmetic and copies ran while one was open for 4% -> 5% of each run, Pallas kernels for 15% -> 13%
where the time goes in v6:
time: 192 us; the launch traced here: 191 us
  blocking collectives  46.3 us (24%)
  starting transfers between devices  42.8 us (22%)
  Pallas kernels  39.7 us (21%)
  waiting for transfers between devices  34 us (18%)
  between operations  14.3 us (7%)
  other arithmetic  7.28 us (4%)
  matrix products  4.04 us (2%)
  local copies, waits for them, and re-layouts  2.54 us (1%)
    all_to_all x2, blocking collectives, spread(): return lax.all_to_all(whole, axes, 0, 0, tiled=True)  30.7 us
    ppermute x12, starting transfers between devices, shift(): lax.ppermute(values, axis, [(i, (i + by) % size) for i in range(size)])  27.8 us
    pallas_call x1, Pallas kernels, inverse_factor(): pl.pallas_call(inverse_factor_kernel, out_shape=jax.ShapeDtypeStruct((R,...  23 us
    ppermute x12, waiting for transfers between devices, shift(): lax.ppermute(values, axis, [(i, (i + by) % size) for i in range(size)])  15.7 us
    all_to_all x1, blocking collectives, local(): lax.all_to_all(part.reshape(XY, -1, rows), ('x', 'y'), 0, 0, tiled=True)  15.6 us
    pallas_call x3, Pallas kernels, call(): pl.pallas_call(kernel, grid=(steps,), out_shape=outs, in_specs=specs, out...  15.4 us
    all_to_all x2, waiting for transfers between devices, spread(): return lax.all_to_all(whole, axes, 0, 0, tiled=True)  12.6 us
    all_to_all x2, starting transfers between devices, spread(): return lax.all_to_all(whole, axes, 0, 0, tiled=True)  9.17 us
  transfers between devices with their start and end apart: 17, of which 11 were waited for; matrix products, arithmetic and copies ran while one was open for 5% of the time, Pallas kernels for 13%

profile of v6, /device:TPU:1, one launch (start us, length us, event | category | flops | bytes accessed | tf_op | source)
XLA Modules:
  0.0 190.9 jit_solution(10740011744055001238)
XLA Ops:
  9.1 3.3 %collective-permute-start.8 = (f32[256,1792]{1,0:T(8,128)S(1)}, f32[256,1792]{1,0:T(8,128)}, u32[]{:S(2)}, u32[]{:S(2)}) collective-permute-start(f32[256,1792]{1,0:T(8,128)S(1)} %convert_add_fusion.buffer_ref), channel_id=1, source_target_pairs={{0,16},{16,0},{1,17},{17,1},{2,18},{18,2},{3,19},{19,3},{4,20},{20... | collective-permute-start | bytes 5505032 | tf_op jit(solution)/shard_map/ppermute | solution.py:341
  13.7 3.0 %collective-permute-start.1 = (f32[32,1792]{1,0:T(8,128)S(1)}, f32[32,1792]{1,0:T(8,128)S(1)}, u32[]{:S(2)}, u32[]{:S(2)}) collective-permute-start(f32[32,1792]{1,0:T(8,128)S(1)} %copy-done.3), channel_id=1, source_target_pairs={{0,192},{32,224},{64,0},{96,32},{128,64},{160,96},{192,128},{224,1... | collective-permute-start | bytes 688136 | tf_op jit(solution)/shard_map/ppermute | solution.py:341
  18.7 5.5 %collective-permute-done.3.refs_7_ = f32[32,1792]{1,0:T(8,128)S(1)} collective-permute-done((f32[32,1792]{1,0:T(8,128)S(1)}, f32[32,1792]{1,0:T(8,128)S(1)}, u32[]{:S(2)}, u32[]{:S(2)}) %collective-permute-start.3) | collective-permute-done | bytes 229408 | tf_op jit(solution)/shard_map/ppermute | solution.py:341
  24.2 3.7 %collective-permute-start.4 = (f32[16,1792]{1,0:T(8,128)S(1)}, f32[16,1792]{1,0:T(8,128)S(1)}, u32[]{:S(2)}, u32[]{:S(2)}) collective-permute-start(f32[16,1792]{1,0:T(8,128)S(1)} %slice.26), channel_id=1, source_target_pairs={{0,64},{32,96},{64,128},{96,160},{128,192},{160,224},{192,0},{224,... | collective-permute-start | bytes 344072 | tf_op jit(solution)/shard_map/ppermute | solution.py:341
  28.6 2.4 %collective-permute-start.5 = (f32[16,1792]{1,0:T(8,128)S(1)}, f32[16,1792]{1,0:T(8,128)S(1)}, u32[]{:S(2)}, u32[]{:S(2)}) collective-permute-start(f32[16,1792]{1,0:T(8,128)S(1)} %slice.27), channel_id=1, source_target_pairs={{0,192},{32,224},{64,0},{96,32},{128,64},{160,96},{192,128},{224,1... | collective-permute-start | bytes 344072 | tf_op jit(solution)/shard_map/ppermute | solution.py:341
  35.6 2.4 %maximum_select_fusion.refs_9_.chip_ref = f32[512,1792]{1,0:T(8,128)S(1)} fusion(f32[256,1792]{1,0:T(8,128)} %collective-permute-done.8, f32[256,1792]{1,0:T(8,128)S(1)} %convert_add_fusion.buffer_ref, pred[]{:T(512)S(6)} %eq.6), kind=kLoop, calls=%fused_computation | loop fusion | flops 2752512 | bytes 7340033 | tf_op jit(solution)/shard_map/jit(_where)/select_n | solution.py:373
  38.3 2.7 %collective-permute-done.6.refs_6_ = f32[32,1792]{1,0:T(8,128)S(1)} collective-permute-done((f32[32,1792]{1,0:T(8,128)S(1)}, f32[32,1792]{1,0:T(8,128)S(1)}, u32[]{:S(2)}, u32[]{:S(2)}) %collective-permute-start.6) | collective-permute-done | bytes 229408 | tf_op jit(solution)/shard_map/ppermute | solution.py:341
  42.6 2.5 %left_product.1 = f32[256,512]{1,0:T(8,128)S(1)} custom-call(f32[32,1792]{1,0:T(8,128)S(1)} %copy-done.3, f32[32,1792]{1,0:T(8,128)S(1)} %collective-permute-done.refs_1_, f32[32,1792]{1,0:T(8,128)S(1)} %collective-permute-done.1.refs_2_, f32[32,1792]{1,0:T(8,128)S(1)} %collective-permute-done.2.refs_3_, f32[16,1792]{1,0:T(8,128)S(1)} %collective-permute-done.4.refs_4_, ...), custom_call_target="tpu_custom_call" | custom-call | flops 3000000000 | bytes 4194304 | tf_op jit(solution)/shard_map/left_product/pallas_call | solution.py:184
  45.2 15.6 %all_to_all.30 = f32[16,16,512]{2,1,0:T(8,128)S(1)} all-to-all(f32[16,16,512]{2,1,0:T(8,128)S(1)} %bitcast.15), channel_id=1, replica_groups=mesh['z'=8,'core'=2,'x'=4,'y'=4] {'x','y'}, dimensions={0} | all-to-all | bytes 1048576 | tf_op jit(solution)/shard_map/all_to_all | solution.py:380
  61.6 4.4 %all-to-all-start.1 = ((f32[16,16,512]{2,1,0:T(8,128)}), f32[16,16,512]{2,1,0:T(8,128)S(1)}, u32[]{:S(2)}, u32[]{:S(2)}) async-start(f32[16,16,512]{2,1,0:T(8,128)} %broadcast_in_dim.13), calls=%async_computation.1 | async-start | bytes 1048576 | tf_op jit(solution)/shard_map/all_to_all | solution.py:346
  66.1 9.2 %all-to-all-done.1 = f32[16,16,512]{2,1,0:T(8,128)S(1)} async-done(((f32[16,16,512]{2,1,0:T(8,128)}), f32[16,16,512]{2,1,0:T(8,128)S(1)}, u32[]{:S(2)}, u32[]{:S(2)}) %all-to-all-start.1) | async-done | bytes 524320 | tf_op jit(solution)/shard_map/all_to_all | solution.py:346
  75.4 4.7 %right_product.1 = f32[1792,256]{1,0:T(8,128)} custom-call(f32[256,512]{1,0:T(8,128)S(1)} %bitcast.16, f32[512,1792]{1,0:T(8,128)} %copy-done), custom_call_target="tpu_custom_call" | custom-call | flops 3000000000 | bytes 4194304 | tf_op jit(solution)/shard_map/right_product/pallas_call | solution.py:184
  80.2 3.6 %collective-permute-start.9 = (f32[8,32,512]{2,1,0:T(8,128)S(1)}, f32[8,32,512]{2,1,0:T(8,128)S(1)}, u32[]{:S(2)}, u32[]{:S(2)}) collective-permute-start(f32[8,32,512]{2,1,0:T(8,128)S(1)} %fusion), channel_id=1, source_target_pairs={{0,16},{16,0},{1,17},{17,1},{2,18},{18,2},{3,19},{19,3},{4,20},{20... | collective-permute-start | bytes 1572872 | tf_op jit(solution)/shard_map/ppermute | solution.py:341
  86.6 19.1 %all_to_all.31 = f32[8,16,512]{2,1,0:T(8,128)S(1)} all-to-all(f32[8,16,512]{2,1,0:T(8,128)S(1)} %broadcast_in_dim.14), channel_id=1, replica_groups=mesh['z'=8,'core'=2,'x'=4,'y'=4] {'z'}, dimensions={0} | all-to-all | bytes 524288 | tf_op jit(solution)/shard_map/all_to_all | solution.py:346
  105.8 11.6 %all_to_all.32 = f32[16,16,512]{2,1,0:T(8,128)S(1)} all-to-all(f32[16,16,512]{2,1,0:T(8,128)S(1)} %broadcast_in_dim.15), channel_id=1, replica_groups=mesh['z'=8,'core'=2,'x'=4,'y'=4] {'x','y'}, dimensions={0} | all-to-all | bytes 1048576 | tf_op jit(solution)/shard_map/all_to_all | solution.py:346
  117.4 3.5 %collective-permute-start.10 = (f32[256,512]{1,0:T(8,128)S(1)}, f32[256,512]{1,0:T(8,128)S(1)}, u32[]{:S(2)}, u32[]{:S(2)}) collective-permute-start(f32[256,512]{1,0:T(8,128)S(1)} %bitcast.23), channel_id=1, source_target_pairs={{0,16},{16,0},{1,17},{17,1},{2,18},{18,2},{3,19},{19,3},{4,20},{20... | collective-permute-start | bytes 1572872 | tf_op jit(solution)/shard_map/ppermute | solution.py:341
  123.9 2.4 %collective-permute-start.11 = (f32[224,256]{1,0:T(8,128)}, f32[224,256]{1,0:T(8,128)S(1)}, u32[]{:S(2)}, u32[]{:S(2)}) collective-permute-start(f32[224,256]{1,0:T(8,128)} %fusion.6.earlier.own_ref), channel_id=1, source_target_pairs={{0,16},{16,0},{1,17},{17,1},{2,18},{18,2},{3,19},{19,3},{4,20},{20... | collective-permute-start | bytes 688136 | tf_op jit(solution)/shard_map/ppermute | solution.py:341
  127.2 23.0 %inverse_factor.1.inverse_ref = f32[512,512]{1,0:T(8,128)S(1)} custom-call(f32[512,512]{1,0:T(8,128)S(1)} %maximum_select_fusion.1.gram, f32[224,256]{1,0:T(8,128)S(1)} %copy-done.1), custom_call_target="tpu_custom_call" | custom-call | flops 30000001024 | bytes 2097152 | tf_op jit(solution)/shard_map/inverse_factor/pallas_call | solution.py:143
  151.5 5.7 %all-to-all-start.4 = ((f32[8,1,512]{2,1,0:T(1,128)}), f32[8,1,512]{2,1,0:T(1,128)S(1)}, u32[]{:S(2)}, u32[]{:S(2)}) async-start(f32[8,1,512]{2,1,0:T(1,128)} %column_squares.1), calls=%async_computation.5 | async-start | bytes 32768 | tf_op jit(solution)/shard_map/all_to_all | solution.py:403
  158.3 5.7 %all-to-all-done.4 = f32[8,1,512]{2,1,0:T(1,128)S(1)} async-done(((f32[8,1,512]{2,1,0:T(1,128)}), f32[8,1,512]{2,1,0:T(1,128)S(1)}, u32[]{:S(2)}, u32[]{:S(2)}) %all-to-all-start.4) | async-done | bytes 16416 | tf_op jit(solution)/shard_map/all_to_all | solution.py:403
  164.6 4.8 %all-to-all-start.5 = ((f32[16,1,512]{2,1,0:T(1,128)}), f32[16,1,512]{2,1,0:T(1,128)S(1)}, u32[]{:S(2)}, u32[]{:S(2)}) async-start(f32[16,1,512]{2,1,0:T(1,128)} %broadcast_in_dim.17), calls=%async_computation.6 | async-start | bytes 65536 | tf_op jit(solution)/shard_map/all_to_all | solution.py:346
  169.4 3.1 %fusion.1.ortho_ref = f32[256,512]{1,0:T(8,128)S(1)} fusion(f32[512,512]{1,0:T(8,128)S(1)} %inverse_factor.1.inverse_ref, f32[512,512]{1,0:T(8,128)} %bitcast.22, pred[]{:T(512)S(6)} %eq.6), kind=kOutput, calls=%fused_computation.9 | convolution fusion | flops 805437440 | bytes 2621441 | tf_op jit(solution)/shard_map/dot_general | solution.py:359
  172.5 3.4 %all-to-all-done.5.sums_ref = f32[16,1,512]{2,1,0:T(1,128)S(1)} async-done(((f32[16,1,512]{2,1,0:T(1,128)}), f32[16,1,512]{2,1,0:T(1,128)S(1)}, u32[]{:S(2)}, u32[]{:S(2)}) %all-to-all-start.5) | async-done | bytes 32800 | tf_op jit(solution)/shard_map/all_to_all | solution.py:346
  175.9 8.1 %update.1 = (f32[256,1792]{1,0:T(8,128)}, f32[256,1792]{1,0:T(8,128)}, f32[32,1792]{1,0:T(8,128)}) custom-call(s32[1]{0:T(128)} %bitcast.start_ref, f32[256,1792]{1,0:T(8,128)} %weights_ref.1, f32[256,1792]{1,0:T(8,128)} %copy-done.4, f32[256,512]{1,0:T(8,128)S(1)} %fusion.1.ortho_ref, f32[512,512]{1,0:T(8,128)S(1)} %inverse_factor.1.inverse_ref, ...), custom_call_target="tpu_custom_call" | custom-call | flops 3000000000 | bytes 4194304 | tf_op jit(solution)/shard_map/update/pallas_call | solution.py:184
  (49 shorter events, 23.2 us)
Async XLA Ops:
  7.2 5.3 %copy-start.3 = (f32[32,1792]{1,0:T(8,128)S(1)}, f32[32,1792]{1,0:T(8,128)}, u32[]{:S(2)}) copy-start(f32[32,1792]{1,0:T(8,128)} %refs_0_.1) | copy-start | bytes 688132
  9.1 29.0 %copy-start.4 = (f32[256,1792]{1,0:T(8,128)}, f32[256,1792]{1,0:T(8,128)S(1)}, u32[]{:S(2)}) copy-start(f32[256,1792]{1,0:T(8,128)S(1)} %convert_add_fusion.buffer_ref) | copy-start | bytes 5505028
  9.1 24.7 %collective-permute-start.8 = (f32[256,1792]{1,0:T(8,128)S(1)}, f32[256,1792]{1,0:T(8,128)}, u32[]{:S(2)}, u32[]{:S(2)}) collective-permute-start(f32[256,1792]{1,0:T(8,128)S(1)} %convert_add_fusion.buffer_ref), channel_id=1, source_target_pairs={{0,16},{16,0},{1,17},{17,1},{2,18},{18,2},{3,19},{19,3},{4,20},{20... | collective-permute-start | bytes 5505032 | tf_op jit(solution)/shard_map/ppermute | solution.py:341
  12.4 11.7 %collective-permute-start.3 = (f32[32,1792]{1,0:T(8,128)S(1)}, f32[32,1792]{1,0:T(8,128)S(1)}, u32[]{:S(2)}, u32[]{:S(2)}) collective-permute-start(f32[32,1792]{1,0:T(8,128)S(1)} %copy-done.3), channel_id=1, source_target_pairs={{0,64},{32,96},{64,128},{96,160},{128,192},{160,224},{192,0},{224,... | collective-permute-start | bytes 688136 | tf_op jit(solution)/shard_map/ppermute | solution.py:341
  13.7 14.9 %collective-permute-start.1 = (f32[32,1792]{1,0:T(8,128)S(1)}, f32[32,1792]{1,0:T(8,128)S(1)}, u32[]{:S(2)}, u32[]{:S(2)}) collective-permute-start(f32[32,1792]{1,0:T(8,128)S(1)} %copy-done.3), channel_id=1, source_target_pairs={{0,192},{32,224},{64,0},{96,32},{128,64},{160,96},{192,128},{224,1... | collective-permute-start | bytes 688136 | tf_op jit(solution)/shard_map/ppermute | solution.py:341
  16.7 16.2 %collective-permute-start = (f32[32,1792]{1,0:T(8,128)S(1)}, f32[32,1792]{1,0:T(8,128)S(1)}, u32[]{:S(2)}, u32[]{:S(2)}) collective-permute-start(f32[32,1792]{1,0:T(8,128)S(1)} %copy-done.3), channel_id=1, source_target_pairs={{0,224},{32,0},{64,32},{96,64},{128,96},{160,128},{192,160},{224,1... | collective-permute-start | bytes 688136 | tf_op jit(solution)/shard_map/ppermute | solution.py:341
  18.7 19.4 %collective-permute-start.7 = (f32[32,1792]{1,0:T(8,128)S(1)}, f32[32,1792]{1,0:T(8,128)S(1)}, u32[]{:S(2)}, u32[]{:S(2)}) collective-permute-start(f32[32,1792]{1,0:T(8,128)S(1)} %copy-done.3), channel_id=1, source_target_pairs={{0,32},{32,64},{64,96},{96,128},{128,160},{160,192},{192,224},{224... | collective-permute-start | bytes 688136 | tf_op jit(solution)/shard_map/ppermute | solution.py:341
  24.2 13.9 %collective-permute-start.4 = (f32[16,1792]{1,0:T(8,128)S(1)}, f32[16,1792]{1,0:T(8,128)S(1)}, u32[]{:S(2)}, u32[]{:S(2)}) collective-permute-start(f32[16,1792]{1,0:T(8,128)S(1)} %slice.26), channel_id=1, source_target_pairs={{0,64},{32,96},{64,128},{96,160},{128,192},{160,224},{192,0},{224,... | collective-permute-start | bytes 344072 | tf_op jit(solution)/shard_map/ppermute | solution.py:341
  28.6 9.7 %collective-permute-start.5 = (f32[16,1792]{1,0:T(8,128)S(1)}, f32[16,1792]{1,0:T(8,128)S(1)}, u32[]{:S(2)}, u32[]{:S(2)}) collective-permute-start(f32[16,1792]{1,0:T(8,128)S(1)} %slice.27), channel_id=1, source_target_pairs={{0,192},{32,224},{64,0},{96,32},{128,64},{160,96},{192,128},{224,1... | collective-permute-start | bytes 344072 | tf_op jit(solution)/shard_map/ppermute | solution.py:341
  33.0 8.0 %collective-permute-start.6 = (f32[32,1792]{1,0:T(8,128)S(1)}, f32[32,1792]{1,0:T(8,128)S(1)}, u32[]{:S(2)}, u32[]{:S(2)}) collective-permute-start(f32[32,1792]{1,0:T(8,128)S(1)} %collective-permute-done.3.refs_7_), channel_id=1, source_target_pairs={{0,32},{32,64},{64,96},{96,128},{128,160},{160,192},{192,224},{224... | collective-permute-start | bytes 688136 | tf_op jit(solution)/shard_map/ppermute | solution.py:341
  33.8 8.9 %collective-permute-start.2 = (f32[32,1792]{1,0:T(8,128)S(1)}, f32[32,1792]{1,0:T(8,128)S(1)}, u32[]{:S(2)}, u32[]{:S(2)}) collective-permute-start(f32[32,1792]{1,0:T(8,128)S(1)} %collective-permute-done.1.refs_2_), channel_id=1, source_target_pairs={{0,224},{32,0},{64,32},{96,64},{128,96},{160,128},{192,160},{224,1... | collective-permute-start | bytes 688136 | tf_op jit(solution)/shard_map/ppermute | solution.py:341
  38.1 7.1 %copy-start = (f32[512,1792]{1,0:T(8,128)}, f32[512,1792]{1,0:T(8,128)S(1)}, u32[]{:S(2)}) copy-start(f32[512,1792]{1,0:T(8,128)S(1)} %maximum_select_fusion.refs_9_.chip_ref) | copy-start | bytes 11010052
  61.6 13.6 %all-to-all-start.1 = ((f32[16,16,512]{2,1,0:T(8,128)}), f32[16,16,512]{2,1,0:T(8,128)S(1)}, u32[]{:S(2)}, u32[]{:S(2)}) async-start(f32[16,16,512]{2,1,0:T(8,128)} %broadcast_in_dim.13), calls=%async_computation.1 | async-start | bytes 1048576 | tf_op jit(solution)/shard_map/all_to_all | solution.py:346
  66.0 56.5 %reduce-scatter.2.cloned.1.call-start = ((), (), s32[]{:S(2)}) async-start(), calls=%async_computation.7 | async-start | bytes 2064384 | tf_op jit(solution)/shard_map/reduce_scatter | solution.py:385
  80.1 95.8 %all-gather.2.cloned.1.call-start = ((), (), s32[]{:S(2)}) async-start(), calls=%async_computation.8 | async-start | bytes 3899392 | tf_op jit(solution)/shard_map/all_gather | solution.py:404
  80.2 5.1 %collective-permute-start.9 = (f32[8,32,512]{2,1,0:T(8,128)S(1)}, f32[8,32,512]{2,1,0:T(8,128)S(1)}, u32[]{:S(2)}, u32[]{:S(2)}) collective-permute-start(f32[8,32,512]{2,1,0:T(8,128)S(1)} %fusion), channel_id=1, source_target_pairs={{0,16},{16,0},{1,17},{17,1},{2,18},{18,2},{3,19},{19,3},{4,20},{20... | collective-permute-start | bytes 1572872 | tf_op jit(solution)/shard_map/ppermute | solution.py:341
  117.4 5.0 %collective-permute-start.10 = (f32[256,512]{1,0:T(8,128)S(1)}, f32[256,512]{1,0:T(8,128)S(1)}, u32[]{:S(2)}, u32[]{:S(2)}) collective-permute-start(f32[256,512]{1,0:T(8,128)S(1)} %bitcast.23), channel_id=1, source_target_pairs={{0,16},{16,0},{1,17},{17,1},{2,18},{18,2},{3,19},{19,3},{4,20},{20... | collective-permute-start | bytes 1572872 | tf_op jit(solution)/shard_map/ppermute | solution.py:341
  123.9 26.4 %collective-permute-start.11 = (f32[224,256]{1,0:T(8,128)}, f32[224,256]{1,0:T(8,128)S(1)}, u32[]{:S(2)}, u32[]{:S(2)}) collective-permute-start(f32[224,256]{1,0:T(8,128)} %fusion.6.earlier.own_ref), channel_id=1, source_target_pairs={{0,16},{16,0},{1,17},{17,1},{2,18},{18,2},{3,19},{19,3},{4,20},{20... | collective-permute-start | bytes 688136 | tf_op jit(solution)/shard_map/ppermute | solution.py:341
  126.3 0.9 copy-start.1
  127.2 23.0 %copy-start.2 = (f32[224,256]{1,0:T(8,128)S(1)}, f32[224,256]{1,0:T(8,128)}, u32[]{:S(2)}) copy-start(f32[224,256]{1,0:T(8,128)} %fusion.6.earlier.own_ref) | copy-start | bytes 688132
  151.5 12.4 %all-to-all-start.4 = ((f32[8,1,512]{2,1,0:T(1,128)}), f32[8,1,512]{2,1,0:T(1,128)S(1)}, u32[]{:S(2)}, u32[]{:S(2)}) async-start(f32[8,1,512]{2,1,0:T(1,128)} %column_squares.1), calls=%async_computation.5 | async-start | bytes 32768 | tf_op jit(solution)/shard_map/all_to_all | solution.py:403
  164.6 11.3 %all-to-all-start.5 = ((f32[16,1,512]{2,1,0:T(1,128)}), f32[16,1,512]{2,1,0:T(1,128)S(1)}, u32[]{:S(2)}, u32[]{:S(2)}) async-start(f32[16,1,512]{2,1,0:T(1,128)} %broadcast_in_dim.17), calls=%async_computation.6 | async-start | bytes 65536 | tf_op jit(solution)/shard_map/all_to_all | solution.py:346
Sparse Core Ops, SparseCore 0:
  80.3 39.9 reduce-scatter.1
  124.0 43.0 all-gather.1

commit v7 on v6

--- a/solution.py
+++ b/solution.py
@@ -396,7 +396,7 @@
         core == 0, jnp.concatenate([gram, gram_other], 0), jnp.concatenate([gram_other, gram], 0)
     )
     product = after(product, gram)
-    inverse = inverse_factor(gram, product)
+    inverse = inverse_factor(gram, product[:8, :128])
 
     beside = shift(product, "core", 1)
     sums = column_squares(inverse, product, beside, jnp.full((1,), core, jnp.int32))

time: 192 us -> 191 us (level)
  no operation moved by 1% of the time
where the time goes in v7:
time: 191 us; the launch traced here: 190 us
  blocking collectives  46.3 us (24%)
  starting transfers between devices  42.7 us (22%)
  Pallas kernels  39.6 us (21%)
  waiting for transfers between devices  34 us (18%)
  between operations  14.3 us (7%)
  other arithmetic  7.28 us (4%)
  matrix products  4.04 us (2%)
    all_to_all x2, blocking collectives, spread(): return lax.all_to_all(whole, axes, 0, 0, tiled=True)  30.8 us
    ppermute x12, starting transfers between devices, shift(): lax.ppermute(values, axis, [(i, (i + by) % size) for i in range(size)])  27.8 us
    pallas_call x1, Pallas kernels, inverse_factor(): pl.pallas_call(inverse_factor_kernel, out_shape=jax.ShapeDtypeStruct((R,...  23 us
    ppermute x12, waiting for transfers between devices, shift(): lax.ppermute(values, axis, [(i, (i + by) % size) for i in range(size)])  15.7 us
    all_to_all x1, blocking collectives, local(): lax.all_to_all(part.reshape(XY, -1, rows), ('x', 'y'), 0, 0, tiled=True)  15.6 us
    pallas_call x3, Pallas kernels, call(): pl.pallas_call(kernel, grid=(steps,), out_shape=outs, in_specs=specs, out...  15.4 us
    all_to_all x2, waiting for transfers between devices, spread(): return lax.all_to_all(whole, axes, 0, 0, tiled=True)  12.6 us
    all_to_all x2, starting transfers between devices, spread(): return lax.all_to_all(whole, axes, 0, 0, tiled=True)  9.07 us
  transfers between devices with their start and end apart: 17, of which 11 were waited for; matrix products, arithmetic and copies ran while one was open for 5% of the time, Pallas kernels for 13%

profile of v7, /device:TPU:1, one launch (start us, length us, event | category | flops | bytes accessed | tf_op | source)
XLA Modules:
  0.0 189.9 jit_solution(6919250176150342245)
XLA Ops:
  9.1 3.3 %collective-permute-start.8 = (f32[256,1792]{1,0:T(8,128)S(1)}, f32[256,1792]{1,0:T(8,128)}, u32[]{:S(2)}, u32[]{:S(2)}) collective-permute-start(f32[256,1792]{1,0:T(8,128)S(1)} %convert_add_fusion.buffer_ref), channel_id=1, source_target_pairs={{0,16},{16,0},{1,17},{17,1},{2,18},{18,2},{3,19},{19,3},{4,20},{20... | collective-permute-start | bytes 5505032 | tf_op jit(solution)/shard_map/ppermute | solution.py:341
  13.7 3.0 %collective-permute-start.1 = (f32[32,1792]{1,0:T(8,128)S(1)}, f32[32,1792]{1,0:T(8,128)S(1)}, u32[]{:S(2)}, u32[]{:S(2)}) collective-permute-start(f32[32,1792]{1,0:T(8,128)S(1)} %copy-done.2), channel_id=1, source_target_pairs={{0,192},{32,224},{64,0},{96,32},{128,64},{160,96},{192,128},{224,1... | collective-permute-start | bytes 688136 | tf_op jit(solution)/shard_map/ppermute | solution.py:341
  18.7 5.5 %collective-permute-done.3.refs_7_ = f32[32,1792]{1,0:T(8,128)S(1)} collective-permute-done((f32[32,1792]{1,0:T(8,128)S(1)}, f32[32,1792]{1,0:T(8,128)S(1)}, u32[]{:S(2)}, u32[]{:S(2)}) %collective-permute-start.3) | collective-permute-done | bytes 229408 | tf_op jit(solution)/shard_map/ppermute | solution.py:341
  24.2 3.7 %collective-permute-start.4 = (f32[16,1792]{1,0:T(8,128)S(1)}, f32[16,1792]{1,0:T(8,128)S(1)}, u32[]{:S(2)}, u32[]{:S(2)}) collective-permute-start(f32[16,1792]{1,0:T(8,128)S(1)} %slice.27), channel_id=1, source_target_pairs={{0,64},{32,96},{64,128},{96,160},{128,192},{160,224},{192,0},{224,... | collective-permute-start | bytes 344072 | tf_op jit(solution)/shard_map/ppermute | solution.py:341
  28.6 2.4 %collective-permute-start.5 = (f32[16,1792]{1,0:T(8,128)S(1)}, f32[16,1792]{1,0:T(8,128)S(1)}, u32[]{:S(2)}, u32[]{:S(2)}) collective-permute-start(f32[16,1792]{1,0:T(8,128)S(1)} %slice.28), channel_id=1, source_target_pairs={{0,192},{32,224},{64,0},{96,32},{128,64},{160,96},{192,128},{224,1... | collective-permute-start | bytes 344072 | tf_op jit(solution)/shard_map/ppermute | solution.py:341
  35.6 2.4 %maximum_select_fusion.refs_9_.chip_ref = f32[512,1792]{1,0:T(8,128)S(1)} fusion(f32[256,1792]{1,0:T(8,128)} %collective-permute-done.8, f32[256,1792]{1,0:T(8,128)S(1)} %convert_add_fusion.buffer_ref, pred[]{:T(512)S(6)} %eq.6), kind=kLoop, calls=%fused_computation | loop fusion | flops 2752512 | bytes 7340033 | tf_op jit(solution)/shard_map/jit(_where)/select_n | solution.py:373
  38.3 2.7 %collective-permute-done.6.refs_6_ = f32[32,1792]{1,0:T(8,128)S(1)} collective-permute-done((f32[32,1792]{1,0:T(8,128)S(1)}, f32[32,1792]{1,0:T(8,128)S(1)}, u32[]{:S(2)}, u32[]{:S(2)}) %collective-permute-start.6) | collective-permute-done | bytes 229408 | tf_op jit(solution)/shard_map/ppermute | solution.py:341
  42.6 2.5 %left_product.1 = f32[256,512]{1,0:T(8,128)S(1)} custom-call(f32[32,1792]{1,0:T(8,128)S(1)} %copy-done.2, f32[32,1792]{1,0:T(8,128)S(1)} %collective-permute-done.refs_1_, f32[32,1792]{1,0:T(8,128)S(1)} %collective-permute-done.1.refs_2_, f32[32,1792]{1,0:T(8,128)S(1)} %collective-permute-done.2.refs_3_, f32[16,1792]{1,0:T(8,128)S(1)} %collective-permute-done.4.refs_4_, ...), custom_call_target="tpu_custom_call" | custom-call | flops 3000000000 | bytes 4194304 | tf_op jit(solution)/shard_map/left_product/pallas_call | solution.py:184
  45.2 15.6 %all_to_all.30 = f32[16,16,512]{2,1,0:T(8,128)S(1)} all-to-all(f32[16,16,512]{2,1,0:T(8,128)S(1)} %bitcast.15), channel_id=1, replica_groups=mesh['z'=8,'core'=2,'x'=4,'y'=4] {'x','y'}, dimensions={0} | all-to-all | bytes 1048576 | tf_op jit(solution)/shard_map/all_to_all | solution.py:380
  61.6 4.4 %all-to-all-start.1 = ((f32[16,16,512]{2,1,0:T(8,128)}), f32[16,16,512]{2,1,0:T(8,128)S(1)}, u32[]{:S(2)}, u32[]{:S(2)}) async-start(f32[16,16,512]{2,1,0:T(8,128)} %broadcast_in_dim.13), calls=%async_computation.1 | async-start | bytes 1048576 | tf_op jit(solution)/shard_map/all_to_all | solution.py:346
  66.1 9.2 %all-to-all-done.1 = f32[16,16,512]{2,1,0:T(8,128)S(1)} async-done(((f32[16,16,512]{2,1,0:T(8,128)}), f32[16,16,512]{2,1,0:T(8,128)S(1)}, u32[]{:S(2)}, u32[]{:S(2)}) %all-to-all-start.1) | async-done | bytes 524320 | tf_op jit(solution)/shard_map/all_to_all | solution.py:346
  75.4 4.7 %right_product.1 = f32[1792,256]{1,0:T(8,128)} custom-call(f32[256,512]{1,0:T(8,128)S(1)} %bitcast.16, f32[512,1792]{1,0:T(8,128)} %copy-done), custom_call_target="tpu_custom_call" | custom-call | flops 3000000000 | bytes 4194304 | tf_op jit(solution)/shard_map/right_product/pallas_call | solution.py:184
  80.2 3.6 %collective-permute-start.9 = (f32[8,32,512]{2,1,0:T(8,128)S(1)}, f32[8,32,512]{2,1,0:T(8,128)S(1)}, u32[]{:S(2)}, u32[]{:S(2)}) collective-permute-start(f32[8,32,512]{2,1,0:T(8,128)S(1)} %fusion), channel_id=1, source_target_pairs={{0,16},{16,0},{1,17},{17,1},{2,18},{18,2},{3,19},{19,3},{4,20},{20... | collective-permute-start | bytes 1572872 | tf_op jit(solution)/shard_map/ppermute | solution.py:341
  86.6 19.1 %all_to_all.31 = f32[8,16,512]{2,1,0:T(8,128)S(1)} all-to-all(f32[8,16,512]{2,1,0:T(8,128)S(1)} %broadcast_in_dim.14), channel_id=1, replica_groups=mesh['z'=8,'core'=2,'x'=4,'y'=4] {'z'}, dimensions={0} | all-to-all | bytes 524288 | tf_op jit(solution)/shard_map/all_to_all | solution.py:346
  105.8 11.6 %all_to_all.32 = f32[16,16,512]{2,1,0:T(8,128)S(1)} all-to-all(f32[16,16,512]{2,1,0:T(8,128)S(1)} %broadcast_in_dim.15), channel_id=1, replica_groups=mesh['z'=8,'core'=2,'x'=4,'y'=4] {'x','y'}, dimensions={0} | all-to-all | bytes 1048576 | tf_op jit(solution)/shard_map/all_to_all | solution.py:346
  117.4 3.4 %collective-permute-start.10 = (f32[256,512]{1,0:T(8,128)S(1)}, f32[256,512]{1,0:T(8,128)S(1)}, u32[]{:S(2)}, u32[]{:S(2)}) collective-permute-start(f32[256,512]{1,0:T(8,128)S(1)} %bitcast.23), channel_id=1, source_target_pairs={{0,16},{16,0},{1,17},{17,1},{2,18},{18,2},{3,19},{19,3},{4,20},{20... | collective-permute-start | bytes 1572872 | tf_op jit(solution)/shard_map/ppermute | solution.py:341
  123.8 2.4 %collective-permute-start.11 = (f32[224,256]{1,0:T(8,128)}, f32[224,256]{1,0:T(8,128)S(1)}, u32[]{:S(2)}, u32[]{:S(2)}) collective-permute-start(f32[224,256]{1,0:T(8,128)} %get-tuple-element.3.own_ref), channel_id=1, source_target_pairs={{0,16},{16,0},{1,17},{17,1},{2,18},{18,2},{3,19},{19,3},{4,20},{20... | collective-permute-start | bytes 688136 | tf_op jit(solution)/shard_map/ppermute | solution.py:341
  126.3 23.0 %inverse_factor.1.inverse_ref = f32[512,512]{1,0:T(8,128)S(1)} custom-call(f32[512,512]{1,0:T(8,128)S(1)} %maximum_select_fusion.1.gram, f32[8,128]{1,0:T(8,128)S(1)} %get-tuple-element.4.earlier), custom_call_target="tpu_custom_call" | custom-call | flops 30000001024 | bytes 2097152 | tf_op jit(solution)/shard_map/inverse_factor/pallas_call | solution.py:143
  150.5 5.8 %all-to-all-start.4 = ((f32[8,1,512]{2,1,0:T(1,128)}), f32[8,1,512]{2,1,0:T(1,128)S(1)}, u32[]{:S(2)}, u32[]{:S(2)}) async-start(f32[8,1,512]{2,1,0:T(1,128)} %column_squares.1), calls=%async_computation.5 | async-start | bytes 32768 | tf_op jit(solution)/shard_map/all_to_all | solution.py:403
  157.4 5.7 %all-to-all-done.4 = f32[8,1,512]{2,1,0:T(1,128)S(1)} async-done(((f32[8,1,512]{2,1,0:T(1,128)}), f32[8,1,512]{2,1,0:T(1,128)S(1)}, u32[]{:S(2)}, u32[]{:S(2)}) %all-to-all-start.4) | async-done | bytes 16416 | tf_op jit(solution)/shard_map/all_to_all | solution.py:403
  163.7 4.7 %all-to-all-start.5 = ((f32[16,1,512]{2,1,0:T(1,128)}), f32[16,1,512]{2,1,0:T(1,128)S(1)}, u32[]{:S(2)}, u32[]{:S(2)}) async-start(f32[16,1,512]{2,1,0:T(1,128)} %broadcast_in_dim.17), calls=%async_computation.6 | async-start | bytes 65536 | tf_op jit(solution)/shard_map/all_to_all | solution.py:346
  168.4 3.1 %fusion.1.ortho_ref = f32[256,512]{1,0:T(8,128)S(1)} fusion(f32[512,512]{1,0:T(8,128)S(1)} %inverse_factor.1.inverse_ref, f32[512,512]{1,0:T(8,128)} %bitcast.22, pred[]{:T(512)S(6)} %eq.6), kind=kOutput, calls=%fused_computation.9 | convolution fusion | flops 805437440 | bytes 2621441 | tf_op jit(solution)/shard_map/dot_general | solution.py:359
  171.5 3.4 %all-to-all-done.5.sums_ref = f32[16,1,512]{2,1,0:T(1,128)S(1)} async-done(((f32[16,1,512]{2,1,0:T(1,128)}), f32[16,1,512]{2,1,0:T(1,128)S(1)}, u32[]{:S(2)}, u32[]{:S(2)}) %all-to-all-start.5) | async-done | bytes 32800 | tf_op jit(solution)/shard_map/all_to_all | solution.py:346
  174.9 8.1 %update.1 = (f32[256,1792]{1,0:T(8,128)}, f32[256,1792]{1,0:T(8,128)}, f32[32,1792]{1,0:T(8,128)}) custom-call(s32[1]{0:T(128)} %bitcast.start_ref, f32[256,1792]{1,0:T(8,128)} %weights_ref.1, f32[256,1792]{1,0:T(8,128)} %copy-done.3, f32[256,512]{1,0:T(8,128)S(1)} %fusion.1.ortho_ref, f32[512,512]{1,0:T(8,128)S(1)} %inverse_factor.1.inverse_ref, ...), custom_call_target="tpu_custom_call" | custom-call | flops 3000000000 | bytes 4194304 | tf_op jit(solution)/shard_map/update/pallas_call | solution.py:184
  (47 shorter events, 22.3 us)
Async XLA Ops:
  7.2 5.3 %copy-start.2 = (f32[32,1792]{1,0:T(8,128)S(1)}, f32[32,1792]{1,0:T(8,128)}, u32[]{:S(2)}) copy-start(f32[32,1792]{1,0:T(8,128)} %refs_0_.1) | copy-start | bytes 688132
  9.1 29.0 %copy-start.3 = (f32[256,1792]{1,0:T(8,128)}, f32[256,1792]{1,0:T(8,128)S(1)}, u32[]{:S(2)}) copy-start(f32[256,1792]{1,0:T(8,128)S(1)} %convert_add_fusion.buffer_ref) | copy-start | bytes 5505028
  9.1 24.7 %collective-permute-start.8 = (f32[256,1792]{1,0:T(8,128)S(1)}, f32[256,1792]{1,0:T(8,128)}, u32[]{:S(2)}, u32[]{:S(2)}) collective-permute-start(f32[256,1792]{1,0:T(8,128)S(1)} %convert_add_fusion.buffer_ref), channel_id=1, source_target_pairs={{0,16},{16,0},{1,17},{17,1},{2,18},{18,2},{3,19},{19,3},{4,20},{20... | collective-permute-start | bytes 5505032 | tf_op jit(solution)/shard_map/ppermute | solution.py:341
  12.4 11.7 %collective-permute-start.3 = (f32[32,1792]{1,0:T(8,128)S(1)}, f32[32,1792]{1,0:T(8,128)S(1)}, u32[]{:S(2)}, u32[]{:S(2)}) collective-permute-start(f32[32,1792]{1,0:T(8,128)S(1)} %copy-done.2), channel_id=1, source_target_pairs={{0,64},{32,96},{64,128},{96,160},{128,192},{160,224},{192,0},{224,... | collective-permute-start | bytes 688136 | tf_op jit(solution)/shard_map/ppermute | solution.py:341
  13.7 14.9 %collective-permute-start.1 = (f32[32,1792]{1,0:T(8,128)S(1)}, f32[32,1792]{1,0:T(8,128)S(1)}, u32[]{:S(2)}, u32[]{:S(2)}) collective-permute-start(f32[32,1792]{1,0:T(8,128)S(1)} %copy-done.2), channel_id=1, source_target_pairs={{0,192},{32,224},{64,0},{96,32},{128,64},{160,96},{192,128},{224,1... | collective-permute-start | bytes 688136 | tf_op jit(solution)/shard_map/ppermute | solution.py:341
  16.7 16.2 %collective-permute-start = (f32[32,1792]{1,0:T(8,128)S(1)}, f32[32,1792]{1,0:T(8,128)S(1)}, u32[]{:S(2)}, u32[]{:S(2)}) collective-permute-start(f32[32,1792]{1,0:T(8,128)S(1)} %copy-done.2), channel_id=1, source_target_pairs={{0,224},{32,0},{64,32},{96,64},{128,96},{160,128},{192,160},{224,1... | collective-permute-start | bytes 688136 | tf_op jit(solution)/shard_map/ppermute | solution.py:341
  18.7 19.4 %collective-permute-start.7 = (f32[32,1792]{1,0:T(8,128)S(1)}, f32[32,1792]{1,0:T(8,128)S(1)}, u32[]{:S(2)}, u32[]{:S(2)}) collective-permute-start(f32[32,1792]{1,0:T(8,128)S(1)} %copy-done.2), channel_id=1, source_target_pairs={{0,32},{32,64},{64,96},{96,128},{128,160},{160,192},{192,224},{224... | collective-permute-start | bytes 688136 | tf_op jit(solution)/shard_map/ppermute | solution.py:341
  24.2 13.9 %collective-permute-start.4 = (f32[16,1792]{1,0:T(8,128)S(1)}, f32[16,1792]{1,0:T(8,128)S(1)}, u32[]{:S(2)}, u32[]{:S(2)}) collective-permute-start(f32[16,1792]{1,0:T(8,128)S(1)} %slice.27), channel_id=1, source_target_pairs={{0,64},{32,96},{64,128},{96,160},{128,192},{160,224},{192,0},{224,... | collective-permute-start | bytes 344072 | tf_op jit(solution)/shard_map/ppermute | solution.py:341
  28.6 9.7 %collective-permute-start.5 = (f32[16,1792]{1,0:T(8,128)S(1)}, f32[16,1792]{1,0:T(8,128)S(1)}, u32[]{:S(2)}, u32[]{:S(2)}) collective-permute-start(f32[16,1792]{1,0:T(8,128)S(1)} %slice.28), channel_id=1, source_target_pairs={{0,192},{32,224},{64,0},{96,32},{128,64},{160,96},{192,128},{224,1... | collective-permute-start | bytes 344072 | tf_op jit(solution)/shard_map/ppermute | solution.py:341
  33.0 8.0 %collective-permute-start.6 = (f32[32,1792]{1,0:T(8,128)S(1)}, f32[32,1792]{1,0:T(8,128)S(1)}, u32[]{:S(2)}, u32[]{:S(2)}) collective-permute-start(f32[32,1792]{1,0:T(8,128)S(1)} %collective-permute-done.3.refs_7_), channel_id=1, source_target_pairs={{0,32},{32,64},{64,96},{96,128},{128,160},{160,192},{192,224},{224... | collective-permute-start | bytes 688136 | tf_op jit(solution)/shard_map/ppermute | solution.py:341
  33.8 8.9 %collective-permute-start.2 = (f32[32,1792]{1,0:T(8,128)S(1)}, f32[32,1792]{1,0:T(8,128)S(1)}, u32[]{:S(2)}, u32[]{:S(2)}) collective-permute-start(f32[32,1792]{1,0:T(8,128)S(1)} %collective-permute-done.1.refs_2_), channel_id=1, source_target_pairs={{0,224},{32,0},{64,32},{96,64},{128,96},{160,128},{192,160},{224,1... | collective-permute-start | bytes 688136 | tf_op jit(solution)/shard_map/ppermute | solution.py:341
  38.1 7.1 %copy-start = (f32[512,1792]{1,0:T(8,128)}, f32[512,1792]{1,0:T(8,128)S(1)}, u32[]{:S(2)}) copy-start(f32[512,1792]{1,0:T(8,128)S(1)} %maximum_select_fusion.refs_9_.chip_ref) | copy-start | bytes 11010052
  61.6 13.6 %all-to-all-start.1 = ((f32[16,16,512]{2,1,0:T(8,128)}), f32[16,16,512]{2,1,0:T(8,128)S(1)}, u32[]{:S(2)}, u32[]{:S(2)}) async-start(f32[16,16,512]{2,1,0:T(8,128)} %broadcast_in_dim.13), calls=%async_computation.1 | async-start | bytes 1048576 | tf_op jit(solution)/shard_map/all_to_all | solution.py:346
  66.0 56.5 %reduce-scatter.2.cloned.1.call-start = ((), (), s32[]{:S(2)}) async-start(), calls=%async_computation.7 | async-start | bytes 2064384 | tf_op jit(solution)/shard_map/reduce_scatter | solution.py:385
  80.1 94.8 %all-gather.2.cloned.1.call-start = ((), (), s32[]{:S(2)}) async-start(), calls=%async_computation.8 | async-start | bytes 3899392 | tf_op jit(solution)/shard_map/all_gather | solution.py:404
  80.2 5.1 %collective-permute-start.9 = (f32[8,32,512]{2,1,0:T(8,128)S(1)}, f32[8,32,512]{2,1,0:T(8,128)S(1)}, u32[]{:S(2)}, u32[]{:S(2)}) collective-permute-start(f32[8,32,512]{2,1,0:T(8,128)S(1)} %fusion), channel_id=1, source_target_pairs={{0,16},{16,0},{1,17},{17,1},{2,18},{18,2},{3,19},{19,3},{4,20},{20... | collective-permute-start | bytes 1572872 | tf_op jit(solution)/shard_map/ppermute | solution.py:341
  117.4 5.0 %collective-permute-start.10 = (f32[256,512]{1,0:T(8,128)S(1)}, f32[256,512]{1,0:T(8,128)S(1)}, u32[]{:S(2)}, u32[]{:S(2)}) collective-permute-start(f32[256,512]{1,0:T(8,128)S(1)} %bitcast.23), channel_id=1, source_target_pairs={{0,16},{16,0},{1,17},{17,1},{2,18},{18,2},{3,19},{19,3},{4,20},{20... | collective-permute-start | bytes 1572872 | tf_op jit(solution)/shard_map/ppermute | solution.py:341
  123.8 25.4 %collective-permute-start.11 = (f32[224,256]{1,0:T(8,128)}, f32[224,256]{1,0:T(8,128)S(1)}, u32[]{:S(2)}, u32[]{:S(2)}) collective-permute-start(f32[224,256]{1,0:T(8,128)} %get-tuple-element.3.own_ref), channel_id=1, source_target_pairs={{0,16},{16,0},{1,17},{17,1},{2,18},{18,2},{3,19},{19,3},{4,20},{20... | collective-permute-start | bytes 688136 | tf_op jit(solution)/shard_map/ppermute | solution.py:341
  126.3 23.0 %copy-start.1 = (f32[224,256]{1,0:T(8,128)S(1)}, f32[224,256]{1,0:T(8,128)}, u32[]{:S(2)}) copy-start(f32[224,256]{1,0:T(8,128)} %get-tuple-element.3.own_ref) | copy-start | bytes 688132
  150.5 12.5 %all-to-all-start.4 = ((f32[8,1,512]{2,1,0:T(1,128)}), f32[8,1,512]{2,1,0:T(1,128)S(1)}, u32[]{:S(2)}, u32[]{:S(2)}) async-start(f32[8,1,512]{2,1,0:T(1,128)} %column_squares.1), calls=%async_computation.5 | async-start | bytes 32768 | tf_op jit(solution)/shard_map/all_to_all | solution.py:403
  163.7 11.2 %all-to-all-start.5 = ((f32[16,1,512]{2,1,0:T(1,128)}), f32[16,1,512]{2,1,0:T(1,128)S(1)}, u32[]{:S(2)}, u32[]{:S(2)}) async-start(f32[16,1,512]{2,1,0:T(1,128)} %broadcast_in_dim.17), calls=%async_computation.6 | async-start | bytes 65536 | tf_op jit(solution)/shard_map/all_to_all | solution.py:346
Sparse Core Ops, SparseCore 0:
  80.3 39.9 reduce-scatter.1
  124.0 42.8 all-gather.1
